TPU v7x, 32 devices: a whole 2x2x4 slice. The times are simulated.
32 devices in a mesh: pipe: 2 (over x), expert: 4 (over y, core), edp: 4 (over z).
Axes of the slice: x: 2, y: 2, z: 4, core: 2. Of those that a mesh axis runs over, the one named last changes fastest.
Arguments:
- head_grads: bfloat16 [2, 1024, 1792], P('pipe', ('expert', 'edp')), may hold values from -6 to 6
- tail_grad: bfloat16 [1024, 1792], P(('expert', 'edp')), may hold values from -6 to 6
- saved_input: bfloat16 [2, 2, 1024, 1792], P('pipe', None, ('expert', 'edp')), may hold values from -48 to 48
- norm_gain: float32 [2, 1792], P('pipe'), may hold values from 0.25 to 1.75
- route_expert: int32 [2, 2, 1024, 1], P('pipe', None, ('expert', 'edp')), may hold values from 0 to 3, as said below
- route_slot: int32 [2, 2, 1024, 1], P('pipe', None, ('expert', 'edp')), may hold values from 0 to 15, as said below
- gates: float32 [2, 2, 1024, 1], P('pipe', None, ('expert', 'edp')), may hold values from 0.05 to 0.6
- saved_pre: bfloat16 [2, 2, 4, 256, 1408], P('pipe', None, 'expert', 'edp'), may hold values from -6 to 6
- w_gate_up: bfloat16 [2, 4, 1792, 1408], P('pipe', 'expert'), may hold values from -0.125 to 0.125
- w_down: bfloat16 [2, 4, 704, 1792], P('pipe', 'expert'), may hold values from -0.21875 to 0.21875
Outputs:
- input_grads: bfloat16 [2, 2, 1024, 1792], P('pipe', None, ('expert', 'edp'))
- w_down_grad: float32 [2, 4, 704, 1792], P('pipe', 'expert', 'edp')
Inputs may be any that keep to these rules, and one draw needn't show every extreme that they name: `route_expert`: for each section, round and block of 64 consecutive tokens, each token names 1 different experts and each expert is named exactly 16 times; the experts fall into 1 disjoint sets of 4, and a token's k-th choice lies in the k-th set. `route_slot`: within one such block, the choices that name one expert carry the slots 0 to 15, each once.
All inputs are finite; a program needn't handle non-finite values.
Results may differ from a plain program's by a relative error of at most 0.0052.
Values may be sent and summed in bfloat16 or wider, within the bound.
No kernel may reach another device: no remote copies, remote signals or barrier semaphores. Data moves between devices by JAX's collectives and lax.ppermute only.
A program may use at most 64 MiB of HBM per device.

v0:
```python
import jax
import jax.numpy as jnp
from jax import lax
from jax.sharding import PartitionSpec as P

ROUNDS = 2


norm_eps = 1e-06


def from_behind(value, axis, steps):
    count = lax.axis_size(axis)
    first, last = (max(0, -steps), min(count, count - steps))
    return lax.ppermute(value, axis, [(source, source + steps) for source in range(first, last)])


def section_pass(
    grad_local,
    round_index,
    route_expert,
    route_slot,
    gates,
    saved_input,
    norm_gain,
    saved_pre,
    w_gate_up,
    w_down,
):
    senders = lax.axis_size("expert")
    tokens, model_width = grad_local.shape
    top_count = route_expert.shape[3]
    capacity = saved_pre.shape[3] // senders
    hidden_width = w_down.shape[2]
    picked = route_expert[0, round_index]
    placed = route_slot[0, round_index]
    weights_now = gates[0, round_index]
    targets = (picked * capacity + placed).reshape(-1)
    sources = (
        jnp.zeros((senders * capacity,), jnp.int32)
        .at[targets]
        .set(jnp.arange(tokens * top_count, dtype=jnp.int32))
    )
    scaled = (
        grad_local[sources // top_count].astype(jnp.float32)
        * weights_now.reshape(-1)[sources][:, None]
    )
    outgoing = scaled.astype(jnp.bfloat16).reshape(senders, capacity, model_width)
    arrived = lax.all_to_all(outgoing, "expert", split_axis=0, concat_axis=0, tiled=True)
    routed = arrived.reshape(senders * capacity, model_width)
    hidden_grad = lax.dot_general(
        routed, w_down[0, 0], (((1,), (1,)), ((), ())), preferred_element_type=jnp.float32
    )
    stored = saved_pre[0, round_index, 0].astype(jnp.float32)
    gate_pre = stored[:, :hidden_width]
    up_value = stored[:, hidden_width:]
    sigmoid_gate = jax.nn.sigmoid(gate_pre)
    silu_gate = gate_pre * sigmoid_gate
    act_grad = jnp.concatenate(
        [
            hidden_grad * up_value * sigmoid_gate * (1.0 + gate_pre * (1.0 - sigmoid_gate)),
            hidden_grad * silu_gate,
        ],
        axis=1,
    ).astype(jnp.bfloat16)
    expert_grad = lax.dot_general(
        act_grad, w_gate_up[0, 0], (((1,), (1,)), ((), ())), preferred_element_type=jnp.float32
    ).astype(jnp.bfloat16)
    hidden = (silu_gate * up_value).astype(jnp.bfloat16)
    returned = lax.all_to_all(
        expert_grad.reshape(senders, capacity, model_width),
        "expert",
        split_axis=0,
        concat_axis=0,
        tiled=True,
    )
    branch = (
        returned.reshape(senders * capacity, model_width)[targets]
        .reshape(tokens, top_count, model_width)
        .astype(jnp.float32)
        .sum(axis=1)
    )
    normed_in = saved_input[0, round_index].astype(jnp.float32)
    inverse = lax.rsqrt(jnp.mean(normed_in * normed_in, axis=1, keepdims=True) + norm_eps)
    scaled_in = normed_in * inverse
    norm_grad = branch * norm_gain[0][None, :]
    result = grad_local.astype(jnp.float32) + inverse * (
        norm_grad - scaled_in * jnp.mean(norm_grad * scaled_in, axis=1, keepdims=True)
    )
    return (result.astype(jnp.bfloat16), hidden, routed)


def outer_term(hidden_rows, routed_rows):
    return lax.dot_general(
        hidden_rows, routed_rows, (((0,), (0,)), ((), ())), preferred_element_type=jnp.float32
    )


def local(
    head_grads,
    tail_grad,
    saved_input,
    norm_gain,
    route_expert,
    route_slot,
    gates,
    saved_pre,
    w_gate_up,
    w_down,
):
    section_index = lax.axis_index("pipe")
    last_section = lax.axis_size("pipe") - 1
    replicas = lax.axis_size("edp")
    first_out, first_hidden, first_rows = section_pass(
        head_grads[0],
        0,
        route_expert,
        route_slot,
        gates,
        saved_input,
        norm_gain,
        saved_pre,
        w_gate_up,
        w_down,
    )
    passed = from_behind(first_out, "pipe", -1)
    second_in = jnp.where(section_index == last_section, tail_grad, passed)
    second_out, second_hidden, second_rows = section_pass(
        second_in,
        1,
        route_expert,
        route_slot,
        gates,
        saved_input,
        norm_gain,
        saved_pre,
        w_gate_up,
        w_down,
    )
    both_hidden = jnp.concatenate([first_hidden, second_hidden], axis=0)
    both_rows = jnp.concatenate([first_rows, second_rows], axis=0)
    summed = lax.psum_scatter(
        outer_term(both_hidden, both_rows), "edp", scatter_dimension=0, tiled=True
    )
    grad_shard = (summed / (replicas * ROUNDS))[None, None]
    input_out = jnp.stack([first_out, second_out])[None]
    return (input_out, grad_shard)


def solution(mesh):
    return jax.shard_map(
        local,
        mesh=mesh,
        in_specs=(
            P("pipe", ("expert", "edp"), None),
            P(("expert", "edp"), None),
            P("pipe", None, ("expert", "edp"), None),
            P("pipe", None),
            P("pipe", None, ("expert", "edp"), None),
            P("pipe", None, ("expert", "edp"), None),
            P("pipe", None, ("expert", "edp"), None),
            P("pipe", None, "expert", "edp", None),
            P("pipe", "expert", None, None),
            P("pipe", "expert", None, None),
        ),
        out_specs=(P("pipe", None, ("expert", "edp"), None), P("pipe", "expert", "edp", None)),
        check_vma=False,
    )
```

profile of v0, /device:TPU:0, one launch (start us, length us, event | category | flops | bytes accessed | tf_op | source)
XLA Modules:
  0.0 169.5 jit_solution(14853387439357729716)
XLA Ops:
  7.2 0.0 copy-start
  7.2 0.0 copy-start.6
  7.2 0.0 copy-start.2
  7.2 0.9 fusion.58
  8.1 0.0 copy-start.9
  8.1 0.8 scatter_custom_fusion
  8.9 0.7 slice_bitcast_fusion
  9.5 0.8 gather_fusion.1
  10.3 0.1 mul.209
  10.4 1.9 %gather_fusion = bf16[64,1792]{1,0:T(8,128)(2,1)S(1)} fusion(bf16[64,1792]{1,0:T(8,128)(2,1)} %bitcast.99, s32[1024]{0:T(1024)S(1)} %pad_clamp_fusion.3), kind=kCustom, calls=%fused_computation | custom fusion | bytes 459008 | tf_op jit(solution)/shard_map/gather | solution.py:45
  12.3 0.8 fusion.44
  13.1 4.2 %all-to-all-start = ((bf16[4,16,1792]{2,1,0:T(8,128)(2,1)}), bf16[4,16,1792]{2,1,0:T(8,128)(2,1)S(1)}, u32[]{:S(2)}, u32[]{:S(2)}) async-start(bf16[4,16,1792]{2,1,0:T(8,128)(2,1)} %fusion.44), calls=%async_computation | async-start | bytes 458752 | tf_op jit(solution)/shard_map/all_to_all | solution.py:49
  17.3 1.9 %bitcast_convert_fusion = (f32[64,1408]{1,0:T(8,128)}, f32[64,1408]{1,0:T(8,128)}) fusion(bf16[1,2,1,64,1408]{4,3,2,1,0:T(8,128)(2,1)} %param.17), kind=kLoop, calls=%fused_computation.81 | loop fusion | flops 180224 | bytes 1081344 | tf_op jit(solution)/shard_map/convert_element_type | solution.py:54
  19.3 1.3 scatter_custom_fusion.1
  20.5 0.0 copy-done.6
  20.5 0.0 copy-done.2
  20.6 0.7 fusion.30
  21.3 1.8 %all-to-all-done = bf16[4,16,1792]{2,1,0:T(8,128)(2,1)S(1)} async-done(((bf16[4,16,1792]{2,1,0:T(8,128)(2,1)}), bf16[4,16,1792]{2,1,0:T(8,128)(2,1)S(1)}, u32[]{:S(2)}, u32[]{:S(2)}) %all-to-all-start) | async-done | bytes 229408 | tf_op jit(solution)/shard_map/all_to_all | solution.py:49
  23.0 0.0 copy-start.3
  23.0 0.0 copy-done.9
  23.0 0.0 copy-done
  23.0 2.0 %multiply_convert_fusion.5 = (bf16[64,704]{1,0:T(8,128)(2,1)S(1)}, bf16[64,704]{1,0:T(8,128)(2,1)S(1)}, bf16[64,704]{1,0:T(8,128)(2,1)S(1)}) fusion(f32[64,1408]{1,0:T(8,128)} %get-tuple-element.11, bf16[64,1792]{1,0:T(8,128)(2,1)S(1)} %bitcast.104, bf16[1,1,704,1792]{3,2,1,0:T(8,128)(2,1)S(1)} %copy-done), kind=kOutput, calls=%fused_computation.72 | convolution fusion | flops 162156544 | bytes 3383296 | tf_op jit(solution)/shard_map/dot_general | solution.py:51
  25.0 0.0 copy-done.3
  25.0 4.7 %fusion.8 = bf16[64,1792]{1,0:T(8,128)(2,1)} fusion(bf16[1,1,1792,1408]{3,2,1,0:T(8,128)(2,1)} %param.18, bf16[64,704]{1,0:T(8,128)(2,1)S(1)} %get-tuple-element.7, bf16[64,704]{1,0:T(8,128)(2,1)S(1)} %get-tuple-element.6), kind=kOutput, calls=%fused_computation.16 | convolution fusion | flops 323436544 | bytes 5455872 | tf_op jit(solution)/shard_map/dot_general | solution.py:66
  29.7 0.0 copy-start.1
  29.7 3.5 %all-to-all-start.1 = ((bf16[4,16,1792]{2,1,0:T(8,128)(2,1)}), bf16[4,16,1792]{2,1,0:T(8,128)(2,1)S(1)}, u32[]{:S(2)}, u32[]{:S(2)}) async-start(bf16[4,16,1792]{2,1,0:T(8,128)(2,1)} %bitcast.108), calls=%async_computation.1 | async-start | bytes 458752 | tf_op jit(solution)/shard_map/all_to_all | solution.py:70
  33.2 0.0 reduce-scatter.2.cloned.1.call-start
  33.3 1.2 add_rsqrt_fusion.1
  34.5 4.4 %all-to-all-done.1 = bf16[4,16,1792]{2,1,0:T(8,128)(2,1)S(1)} async-done(((bf16[4,16,1792]{2,1,0:T(8,128)(2,1)}), bf16[4,16,1792]{2,1,0:T(8,128)(2,1)S(1)}, u32[]{:S(2)}, u32[]{:S(2)}) %all-to-all-start.1) | async-done | bytes 229408 | tf_op jit(solution)/shard_map/all_to_all | solution.py:70
  38.9 1.4 gather_fusion.2
  40.3 1.7 %fusion.38 = (f32[64]{0:T(128)}, f32[64]{0:T(128)S(1)}) fusion(bf16[1,2,64,1792]{3,2,1,0:T(8,128)(2,1)S(1)} %copy-done.2, f32[64]{0:T(128)} %add_rsqrt_fusion.1, f32[1792]{0:T(1024)S(1)} %reduce, bf16[64,1792]{1,0:T(8,128)(2,1)} %gather_fusion.2), kind=kLoop, calls=%fused_computation.49 | loop fusion | flops 1032064 | bytes 696064 | tf_op jit(solution)/shard_map/reduce_sum | solution.py:84
  42.0 0.0 copy-done.1
  42.0 0.0 copy-start.8
  42.0 1.1 fusion.28
  43.2 1.3 collective-permute-start
  44.5 0.0 copy-done.8
  44.5 0.6 compare_select_fusion
  45.1 1.3 gather_fusion.4
  46.4 0.7 mul.236
  47.0 5.3 %collective-permute-done = bf16[64,1792]{1,0:T(8,128)(2,1)} collective-permute-done((bf16[64,1792]{1,0:T(8,128)(2,1)S(1)}, bf16[64,1792]{1,0:T(8,128)(2,1)}, u32[]{:S(2)}, u32[]{:S(2)}) %collective-permute-start) | collective-permute-done | bytes 229408 | tf_op jit(solution)/shard_map/ppermute | solution.py:15
  52.3 1.0 broadcast_select_fusion
  53.3 1.4 gather_fusion.3
  54.7 0.0 copy-start.4
  54.7 1.1 fusion.43
  55.8 8.1 %all_to_all.20 = bf16[4,16,1792]{2,1,0:T(8,128)(2,1)S(1)} all-to-all(bf16[4,16,1792]{2,1,0:T(8,128)(2,1)S(1)} %fusion.43), channel_id=1, replica_groups=mesh['pipe'=2,'expert'=4,'edp'=4] {'expert'}, dimensions={0} | all-to-all | bytes 458752 | tf_op jit(solution)/shard_map/all_to_all | solution.py:49
  63.9 2.6 %multiply_convert_fusion.3 = (bf16[64,704]{1,0:T(8,128)(2,1)}, bf16[64,704]{1,0:T(8,128)(2,1)}, bf16[64,704]{1,0:T(8,128)(2,1)S(1)}) fusion(f32[64,1408]{1,0:T(8,128)} %get-tuple-element.10, bf16[64,1792]{1,0:T(8,128)(2,1)S(1)} %bitcast.106, bf16[1,1,704,1792]{3,2,1,0:T(8,128)(2,1)S(1)} %copy-done), kind=kOutput, calls=%fused_computation.68 | convolution fusion | flops 162156544 | bytes 3383296 | tf_op jit(solution)/shard_map/dot_general | solution.py:51
  66.5 0.0 copy-done.4
  66.5 3.1 %fusion.39 = f32[704,1792]{1,0:T(8,128)} fusion(bf16[64,1792]{1,0:T(8,128)(2,1)S(1)} %bitcast.107, bf16[64,1792]{1,0:T(8,128)(2,1)S(1)} %bitcast.105, bf16[64,704]{1,0:T(8,128)(2,1)S(1)} %get-tuple-element.9, bf16[64,704]{1,0:T(8,128)(2,1)S(1)} %get-tuple-element.8), kind=kOutput, calls=%fused_computation.51 | convolution fusion | flops 324239360 | bytes 5685248 | tf_op jit(solution)/shard_map/dot_general | solution.py:94
  69.6 0.0 copy-start.7
  69.6 0.0 reduce-scatter.2.cloned.1.call-update
  69.6 0.6 pad_clamp_fusion
  70.2 0.0 copy-done.7
  70.2 1.8 %fusion.36 = bf16[1,64,1792]{2,1,0:T(8,128)(2,1)} fusion(bf16[64,1792]{1,0:T(8,128)(2,1)} %gather_fusion.2, bf16[1,64,1792]{2,1,0:T(8,128)(2,1)S(1)} %copy-done.1, f32[64]{0:T(128)} %copy-done.8, f32[1792]{0:T(1024)S(1)} %reduce, f32[64]{0:T(128)S(1)} %copy-done.7, bf16[1,2,64,1792]{3,2,1,0:T(8,128)(2,1)S(1)} %copy-done.2), kind=kLoop, calls=%fused_computation.47 | loop fusion | flops 1146880 | bytes 925184 | tf_op jit(solution)/shard_map/convert_element_type | solution.py:90
  72.1 0.0 copy-done.5
  72.1 4.7 %fusion.11 = bf16[64,1792]{1,0:T(8,128)(2,1)} fusion(bf16[1,1,1792,1408]{3,2,1,0:T(8,128)(2,1)} %param.18, bf16[64,704]{1,0:T(8,128)(2,1)} %get-tuple-element.5, bf16[64,704]{1,0:T(8,128)(2,1)S(1)} %copy-done.5), kind=kOutput, calls=%fused_computation.17 | convolution fusion | flops 323436544 | bytes 5455872 | tf_op jit(solution)/shard_map/dot_general | solution.py:66
  76.8 3.4 %all-to-all-start.3 = ((bf16[4,16,1792]{2,1,0:T(8,128)(2,1)}), bf16[4,16,1792]{2,1,0:T(8,128)(2,1)S(1)}, u32[]{:S(2)}, u32[]{:S(2)}) async-start(bf16[4,16,1792]{2,1,0:T(8,128)(2,1)} %bitcast.109), calls=%async_computation.3 | async-start | bytes 458752 | tf_op jit(solution)/shard_map/all_to_all | solution.py:70
  80.2 0.6 add_rsqrt_fusion
  80.8 5.0 %all-to-all-done.3 = bf16[4,16,1792]{2,1,0:T(8,128)(2,1)S(1)} async-done(((bf16[4,16,1792]{2,1,0:T(8,128)(2,1)}), bf16[4,16,1792]{2,1,0:T(8,128)(2,1)S(1)}, u32[]{:S(2)}, u32[]{:S(2)}) %all-to-all-start.3) | async-done | bytes 229408 | tf_op jit(solution)/shard_map/all_to_all | solution.py:70
  85.8 1.4 gather_fusion.5
  87.2 1.2 fusion.21
  88.4 1.1 fusion.45
  89.6 1.8 %maximum_bitcast_fusion = bf16[1,2,64,1792]{3,2,1,0:T(8,128)(2,1)} fusion(bf16[1,64,1792]{2,1,0:T(8,128)(2,1)S(1)} %fusion.45, bf16[1,64,1792]{2,1,0:T(8,128)(2,1)} %fusion.36), kind=kLoop, calls=%fused_computation.50 | loop fusion | flops 229376 | bytes 917504 | tf_op jit(solution)/shard_map/broadcast_in_dim | solution.py:146
  91.3 68.9 %reduce-scatter.2.cloned.1.call-done = f32[176,1792]{1,0:T(8,128)} async-done(((f32[704,1792]{1,0:T(8,128)}), f32[176,1792]{1,0:T(8,128)}) %reduce-scatter.2.cloned.1.call-update) | async-done | bytes 1261584 | tf_op jit(solution)/shard_map/reduce_scatter | solution.py:142
  160.2 2.4 %multiply_bitcast_fusion = f32[1,1,176,1792]{3,2,1,0:T(8,128)} fusion(f32[176,1792]{1,0:T(8,128)} %reduce-scatter.2.cloned.1.call-done), kind=kLoop, calls=%fused_computation.18 | loop fusion | flops 315392 | bytes 2523136 | tf_op jit(solution)/shard_map/broadcast_in_dim | solution.py:145
  (10 shorter events, 0.1 us)
Async XLA Ops:
  7.2 15.9 %copy-start = (bf16[1,1,704,1792]{3,2,1,0:T(8,128)(2,1)S(1)}, bf16[1,1,704,1792]{3,2,1,0:T(8,128)(2,1)}, u32[]{:S(2)}) copy-start(bf16[1,1,704,1792]{3,2,1,0:T(8,128)(2,1)} %param.19) | copy-start | bytes 7569412
  7.2 13.3 %copy-start.6 = (f32[1,1792]{1,0:T(1,128)S(1)}, f32[1,1792]{1,0:T(1,128)}, u32[]{:S(2)}) copy-start(f32[1,1792]{1,0:T(1,128)} %param.13) | copy-start | bytes 21508
  7.2 13.4 %copy-start.2 = (bf16[1,2,64,1792]{3,2,1,0:T(8,128)(2,1)S(1)}, bf16[1,2,64,1792]{3,2,1,0:T(8,128)(2,1)}, u32[]{:S(2)}) copy-start(bf16[1,2,64,1792]{3,2,1,0:T(8,128)(2,1)} %param.12) | copy-start | bytes 1376260
  8.1 15.0 %copy-start.9 = (s32[64]{0:T(128)}, s32[64]{0:T(128)S(1)}, u32[]{:S(2)}) copy-start(s32[64]{0:T(128)S(1)} %get-tuple-element.12) | copy-start | bytes 772
  13.1 9.9 %all-to-all-start = ((bf16[4,16,1792]{2,1,0:T(8,128)(2,1)}), bf16[4,16,1792]{2,1,0:T(8,128)(2,1)S(1)}, u32[]{:S(2)}, u32[]{:S(2)}) async-start(bf16[4,16,1792]{2,1,0:T(8,128)(2,1)} %fusion.44), calls=%async_computation | async-start | bytes 458752 | tf_op jit(solution)/shard_map/all_to_all | solution.py:49
  23.0 2.0 %copy-start.3 = (bf16[4,16,1792]{2,1,0:T(8,128)(2,1)}, bf16[4,16,1792]{2,1,0:T(8,128)(2,1)S(1)}, u32[]{:S(2)}) copy-start(bf16[4,16,1792]{2,1,0:T(8,128)(2,1)S(1)} %all-to-all-done) | copy-start | bytes 688132
  29.7 12.3 %copy-start.1 = (bf16[1,64,1792]{2,1,0:T(8,128)(2,1)S(1)}, bf16[1,64,1792]{2,1,0:T(8,128)(2,1)}, u32[]{:S(2)}) copy-start(bf16[1,64,1792]{2,1,0:T(8,128)(2,1)} %param.10) | copy-start | bytes 688132
  29.7 9.2 %all-to-all-start.1 = ((bf16[4,16,1792]{2,1,0:T(8,128)(2,1)}), bf16[4,16,1792]{2,1,0:T(8,128)(2,1)S(1)}, u32[]{:S(2)}, u32[]{:S(2)}) async-start(bf16[4,16,1792]{2,1,0:T(8,128)(2,1)} %bitcast.108), calls=%async_computation.1 | async-start | bytes 458752 | tf_op jit(solution)/shard_map/all_to_all | solution.py:70
  33.2 127.0 %reduce-scatter.2.cloned.1.call-start = ((), (), s32[]{:S(2)}) async-start(), calls=%async_computation.5 | async-start | bytes 6307840 | tf_op jit(solution)/shard_map/reduce_scatter | solution.py:142
  42.0 2.4 %copy-start.8 = (f32[64]{0:T(128)}, f32[64]{0:T(128)S(1)}, u32[]{:S(2)}) copy-start(f32[64]{0:T(128)S(1)} %broadcast_multiply_fusion.1) | copy-start | bytes 772
  43.2 9.1 %collective-permute-start = (bf16[64,1792]{1,0:T(8,128)(2,1)S(1)}, bf16[64,1792]{1,0:T(8,128)(2,1)}, u32[]{:S(2)}, u32[]{:S(2)}) collective-permute-start(bf16[64,1792]{1,0:T(8,128)(2,1)S(1)} %fusion.28), channel_id=1, source_target_pairs={{16,0},{17,1},{18,2},{19,3},{20,4},{21,5},{22,6},{23,7},{24,8},{25... | collective-permute-start | bytes 688136 | tf_op jit(solution)/shard_map/ppermute | solution.py:15
  54.7 11.7 %copy-start.4 = (bf16[4,16,1792]{2,1,0:T(8,128)(2,1)S(1)}, bf16[4,16,1792]{2,1,0:T(8,128)(2,1)}, u32[]{:S(2)}) copy-start(bf16[4,16,1792]{2,1,0:T(8,128)(2,1)} %copy-done.3) | copy-start | bytes 688132
  69.6 0.7 copy-start.7
  69.6 2.5 %copy-start.5 = (bf16[64,704]{1,0:T(8,128)(2,1)S(1)}, bf16[64,704]{1,0:T(8,128)(2,1)}, u32[]{:S(2)}) copy-start(bf16[64,704]{1,0:T(8,128)(2,1)} %get-tuple-element.4) | copy-start | bytes 270340
  76.8 9.0 %all-to-all-start.3 = ((bf16[4,16,1792]{2,1,0:T(8,128)(2,1)}), bf16[4,16,1792]{2,1,0:T(8,128)(2,1)S(1)}, u32[]{:S(2)}, u32[]{:S(2)}) async-start(bf16[4,16,1792]{2,1,0:T(8,128)(2,1)} %bitcast.109), calls=%async_computation.3 | async-start | bytes 458752 | tf_op jit(solution)/shard_map/all_to_all | solution.py:70
Sparse Core Ops, SparseCore 0:
  69.7 90.4 reduce-scatter.1
where the time goes:
time: 170 us
  waiting for transfers between devices  85.4 us (50%)
  other arithmetic  20.6 us (12%)
  matrix products  17 us (10%)
  between operations  14.2 us (8%)
  starting transfers between devices  12.5 us (7%)
  local copies, waits for them, and re-layouts  11.8 us (7%)
  blocking collectives  8.06 us (5%)
    reduce_scatter x1, waiting for transfers between devices, local(): lax.psum_scatter(outer_term(both_hidden, both_rows), 'edp', scatter_dimen...  68.9 us
    all_to_all x2, waiting for transfers between devices, section_pass(): lax.all_to_all(expert_grad.reshape(senders, capacity, model_width), 'expe...  9.44 us
    dot_general x2, matrix products, section_pass(): lax.dot_general(act_grad, w_gate_up[0, 0], (((1,), (1,)), ((), ())), pref...  9.36 us
    all_to_all x1, blocking collectives, section_pass(): lax.all_to_all(outgoing, 'expert', split_axis=0, concat_axis=0, tiled=True)  8.06 us
    all_to_all x2, starting transfers between devices, section_pass(): lax.all_to_all(expert_grad.reshape(senders, capacity, model_width), 'expe...  6.9 us
    ppermute x1, waiting for transfers between devices, from_behind(): lax.ppermute(value, axis, [(source, source + steps) for source in range(f...  5.28 us
    dot_general x2, matrix products, section_pass(): lax.dot_general(routed, w_down[0, 0], (((1,), (1,)), ((), ())), preferred...  4.56 us
    all_to_all x1, starting transfers between devices, section_pass(): lax.all_to_all(outgoing, 'expert', split_axis=0, concat_axis=0, tiled=True)  4.24 us
  transfers between devices with their start and end apart: 5, of which 5 were waited for; matrix products, arithmetic and copies ran while one was open for 12% of the time, Pallas kernels for 0%

commit v1 on v0

v1 whole, which is shorter than its diff:
```python
import jax
import jax.numpy as jnp
from jax import lax
from jax.experimental import pallas as pl
from jax.experimental.pallas import tpu as pltpu
from jax.sharding import PartitionSpec as P

ROUNDS = 2
NORM_EPS = 1e-06
VMEM_LIMIT = 24 * 2**20

bf16 = jnp.bfloat16
f32 = jnp.float32


def on_chip(body, outs, args, flops=0, moved=0):
    spec = pl.BlockSpec(memory_space=pltpu.VMEM)
    return pl.pallas_call(
        body,
        out_shape=outs,
        in_specs=[spec] * len(args),
        out_specs=jax.tree.map(lambda _: spec, outs),
        compiler_params=pltpu.CompilerParams(vmem_limit_bytes=VMEM_LIMIT),
        cost_estimate=pl.CostEstimate(flops=flops, bytes_accessed=moved, transcendentals=0),
    )(*args)


def dot(left, right, left_dim, right_dim):
    return lax.dot_general(
        left, right, (((left_dim,), (right_dim,)), ((), ())), preferred_element_type=f32
    )


def split_rows(value, refs, rows):
    for index, ref in enumerate(refs):
        ref[...] = value[index * rows : (index + 1) * rows].astype(ref.dtype)


def join_rows(refs):
    if len(refs) == 1:
        return refs[0][...]
    return jnp.concatenate([ref[...] for ref in refs], axis=0)


def one_hot(target, rows):
    lanes = lax.broadcasted_iota(jnp.int32, (target.shape[0], rows), 1)
    return jnp.where(target == lanes, 1.0, 0.0).astype(bf16)


def target_of(expert, slot, capacity):
    mine = lax.axis_index("expert")
    return (expert ^ mine) * capacity + slot


def dispatch_rows(grad, gate, target, rows):
    scaled = (grad.astype(f32) * gate).astype(bf16)
    return dot(one_hot(target, rows), scaled, 0, 0)


def stored_rows(stored_ref, round_index, senders, capacity):
    mine = lax.axis_index("expert")
    if capacity % 16 == 0:
        return jnp.concatenate(
            [
                stored_ref[
                    0,
                    round_index,
                    0,
                    pl.ds(pl.multiple_of((mine ^ step) * capacity, 16), capacity),
                    :,
                ]
                for step in range(senders)
            ],
            axis=0,
        ).astype(f32)
    rows = senders * capacity
    row = lax.broadcasted_iota(jnp.int32, (rows, rows), 0)
    column = lax.broadcasted_iota(jnp.int32, (rows, rows), 1)
    moved = ((row // capacity) ^ mine) * capacity + row % capacity
    order = jnp.where(moved == column, 1.0, 0.0).astype(bf16)
    return dot(order, stored_ref[0, round_index, 0], 1, 0)


def first_dispatch(grad, route_expert, route_slot, gates, capacity, senders, pieces):
    tokens, width = grad.shape
    rows = senders * capacity

    def body(grad_ref, expert_ref, slot_ref, gate_ref, table_ref, *out_refs):
        target = target_of(expert_ref[0, 0], slot_ref[0, 0], capacity)
        sent = dispatch_rows(grad_ref[...], gate_ref[0, 0], target, rows)
        split_rows(sent, out_refs, rows // pieces)
        later = target_of(expert_ref[0, 1], slot_ref[0, 1], capacity).astype(f32)
        lane = lax.broadcasted_iota(jnp.int32, table_ref.shape, 1)
        table_ref[...] = jnp.where(lane == 0, later, gate_ref[0, 1])

    table, *sent = on_chip(
        body,
        [jax.ShapeDtypeStruct((tokens, 2), f32)]
        + [jax.ShapeDtypeStruct((rows // pieces, width), bf16)] * pieces,
        (grad, route_expert, route_slot, gates),
        moved=3 * tokens * width * 2,
    )
    return table, sent


def hidden_blocks(saved_pre, senders, capacity, hidden_width, replicas):
    rows = senders * capacity
    aligned = (hidden_width // replicas) % 16 == 0
    block = hidden_width // replicas

    def body(stored_ref, *refs):
        *out_refs, held = refs
        for round_index in range(ROUNDS):
            stored = stored_rows(stored_ref, round_index, senders, capacity)
            gate_pre, up_value = stored[:, :hidden_width], stored[:, hidden_width:]
            hidden = (gate_pre * up_value) / (1.0 + jnp.exp(-gate_pre))
            held[:, round_index * rows : (round_index + 1) * rows] = hidden.T.astype(bf16)
        if not aligned:
            out_refs[0][...] = held[...]
            return
        mine = lax.axis_index("edp")
        for step, ref in enumerate(out_refs):
            start = pl.multiple_of((mine ^ step) * block, 16)
            ref[...] = held[pl.ds(start, block), :]

    shapes = (
        [jax.ShapeDtypeStruct((block, ROUNDS * rows), bf16)] * replicas
        if aligned
        else [jax.ShapeDtypeStruct((hidden_width, ROUNDS * rows), bf16)]
    )
    spec = pl.BlockSpec(memory_space=pltpu.VMEM)
    out = pl.pallas_call(
        body,
        out_shape=shapes,
        in_specs=[spec],
        out_specs=[spec] * len(shapes),
        scratch_shapes=[pltpu.VMEM((hidden_width, ROUNDS * rows), bf16)],
        compiler_params=pltpu.CompilerParams(vmem_limit_bytes=VMEM_LIMIT),
        cost_estimate=pl.CostEstimate(flops=0, bytes_accessed=2**20, transcendentals=0),
    )(saved_pre)
    if aligned:
        return out
    mine = lax.axis_index("edp")
    return [
        lax.dynamic_slice_in_dim(out[0], (mine ^ step) * block, block, 0)
        for step in range(replicas)
    ]


def expert_rows(pieces_in, saved_pre, w_gate_up, w_down, round_index, senders, capacity):
    rows = senders * capacity
    hidden_width, width = w_down.shape
    pieces = len(pieces_in)

    def body(stored_ref, up_ref, down_ref, *refs):
        in_refs, out_refs = refs[:pieces], refs[pieces:]
        routed = join_rows(in_refs)
        hidden_grad = dot(routed, down_ref[...], 1, 1)
        stored = stored_rows(stored_ref, round_index, senders, capacity)
        gate_pre, up_value = stored[:, :hidden_width], stored[:, hidden_width:]
        gate = 1.0 / (1.0 + jnp.exp(-gate_pre))
        act_grad = jnp.concatenate(
            [
                hidden_grad * up_value * gate * (1.0 + gate_pre * (1.0 - gate)),
                hidden_grad * gate_pre * gate,
            ],
            axis=1,
        ).astype(bf16)
        split_rows(dot(act_grad, up_ref[...], 1, 1), out_refs, rows // pieces)

    return on_chip(
        body,
        [jax.ShapeDtypeStruct((rows // pieces, width), bf16)] * pieces,
        (saved_pre, w_gate_up, w_down, *pieces_in),
        flops=6 * rows * hidden_width * width,
        moved=6 * hidden_width * width,
    )


def norm_backward(grad_out, branch, saved, gain):
    normed_in = saved.astype(f32)
    inverse = lax.rsqrt(jnp.mean(normed_in * normed_in, axis=1, keepdims=True) + NORM_EPS)
    scaled_in = normed_in * inverse
    norm_grad = branch * gain
    result = grad_out.astype(f32) + inverse * (
        norm_grad - scaled_in * jnp.mean(norm_grad * scaled_in, axis=1, keepdims=True)
    )
    return result.astype(bf16)


def first_combine(
    returned, grad, tail, saved_input, gain, route_expert, route_slot, table, capacity, senders
):
    tokens, width = grad.shape
    rows = senders * capacity
    pieces = len(returned)

    def body(grad_ref, tail_ref, saved_ref, gain_ref, expert_ref, slot_ref, table_ref, *refs):
        in_refs, (result_ref, *out_refs) = refs[:pieces], refs[pieces:]
        target = target_of(expert_ref[0, 0], slot_ref[0, 0], capacity)
        branch = dot(one_hot(target, rows), join_rows(in_refs), 1, 0)
        result = norm_backward(grad_ref[...], branch, saved_ref[0, 0], gain_ref[...])
        result_ref[...] = result
        first = lax.axis_index("pipe") == 0
        passed = jnp.where(first, tail_ref[...].astype(f32), result.astype(f32))
        later = table_ref[:, 0:1].astype(jnp.int32)
        split_rows(
            dispatch_rows(passed, table_ref[:, 1:2], later, rows), out_refs, rows // pieces
        )

    result, *sent = on_chip(
        body,
        [jax.ShapeDtypeStruct((tokens, width), bf16)]
        + [jax.ShapeDtypeStruct((rows // pieces, width), bf16)] * pieces,
        (grad, tail, saved_input, gain, route_expert, route_slot, table, *returned),
        moved=8 * tokens * width * 2,
    )
    return result, sent


def second_combine(
    returned, first_out, passed, tail, saved_input, gain, route_expert, route_slot, capacity, senders
):
    tokens, width = first_out.shape
    rows = senders * capacity
    pieces = len(returned)

    def body(first_ref, passed_ref, tail_ref, saved_ref, gain_ref, expert_ref, slot_ref, *refs):
        in_refs, (out_ref,) = refs[:pieces], refs[pieces:]
        out_ref[0, 0] = first_ref[...]
        target = target_of(expert_ref[0, 1], slot_ref[0, 1], capacity)
        branch = dot(one_hot(target, rows), join_rows(in_refs), 1, 0)
        last = lax.axis_index("pipe") == lax.axis_size("pipe") - 1
        grad = jnp.where(last, tail_ref[...].astype(f32), passed_ref[...].astype(f32))
        out_ref[0, 1] = norm_backward(grad, branch, saved_ref[0, 1], gain_ref[...])

    return on_chip(
        body,
        [jax.ShapeDtypeStruct((1, ROUNDS, tokens, width), bf16)],
        (first_out, passed, tail, saved_input, gain, route_expert, route_slot, *returned),
        moved=8 * tokens * width * 2,
    )[0]


def weight_grad(hidden, first_rows, second_rows, scale):
    replicas = len(hidden)
    block = hidden[0].shape[0]
    rows, width = first_rows[0].shape

    def body(*refs):
        hidden_refs = refs[:replicas]
        first_refs = refs[replicas : 2 * replicas]
        second_refs = refs[2 * replicas : 3 * replicas]
        out_ref = refs[-1]
        left = jnp.concatenate([ref[...] for ref in hidden_refs], axis=1)
        right = jnp.concatenate(
            [ref[...] for pair in zip(first_refs, second_refs) for ref in pair], axis=0
        )
        out_ref[0, 0] = dot(left, right, 1, 0) / scale

    return on_chip(
        body,
        [jax.ShapeDtypeStruct((1, 1, block, width), f32)],
        (*hidden, *first_rows, *second_rows),
        flops=4 * replicas * rows * block * width,
        moved=4 * block * width + 4 * replicas * rows * width,
    )[0]


def steps_over(axis, values):
    count = lax.axis_size(axis)
    return [values[0]] + [
        lax.ppermute(values[step], axis, [(source, source ^ step) for source in range(count)])
        for step in range(1, count)
    ]


def behind(values):
    sections, count = lax.axis_size("pipe"), lax.axis_size("expert")
    return [
        lax.ppermute(
            value,
            ("pipe", "expert"),
            [
                (section * count + source, (section - 1) % sections * count + (source ^ step))
                for section in range(sections)
                for source in range(count)
            ],
        )
        for step, value in enumerate(values)
    ]


def local(
    head_grads,
    tail_grad,
    saved_input,
    norm_gain,
    route_expert,
    route_slot,
    gates,
    saved_pre,
    w_gate_up,
    w_down,
):
    senders = lax.axis_size("expert")
    replicas = lax.axis_size("edp")
    sections = lax.axis_size("pipe")
    rows = saved_pre.shape[3]
    capacity = rows // senders
    width = w_down.shape[3]
    hidden_width = w_down.shape[2]
    pieces = senders if capacity % 16 == 0 else 1
    grad = head_grads[0]
    up, down = w_gate_up[0, 0], w_down[0, 0]

    def apart(parts):
        if pieces == senders:
            return parts
        return [parts[0][k * capacity : (k + 1) * capacity] for k in range(senders)]

    def together(parts):
        return parts if pieces == senders else [jnp.concatenate(parts, axis=0)]

    def whole(parts):
        return parts[0] if len(parts) == 1 else jnp.concatenate(parts, axis=0)

    def over_experts(parts):
        return together(steps_over("expert", apart(parts)))

    hidden = hidden_blocks(saved_pre, senders, capacity, hidden_width, replicas)
    hidden = steps_over("edp", hidden)

    table, sent = first_dispatch(
        grad, route_expert, route_slot, gates, capacity, senders, pieces
    )
    table = lax.ppermute(
        table, "pipe", [(source, (source + 1) % sections) for source in range(sections)]
    )
    arrived = over_experts(sent)
    first_rows = steps_over("edp", [whole(arrived)] * replicas)
    returned = over_experts(
        expert_rows(arrived, saved_pre, up, down, 0, senders, capacity)
    )
    first_out, sent = first_combine(
        returned,
        grad,
        tail_grad,
        saved_input,
        norm_gain,
        route_expert,
        route_slot,
        table,
        capacity,
        senders,
    )
    arrived = together(behind(apart(sent)))
    passed = lax.ppermute(
        first_out, "pipe", [(source, (source - 1) % sections) for source in range(sections)]
    )
    second_rows = steps_over("edp", [whole(arrived)] * replicas)
    returned = over_experts(
        expert_rows(arrived, saved_pre, up, down, 1, senders, capacity)
    )
    input_out = second_combine(
        returned,
        first_out,
        passed,
        tail_grad,
        saved_input,
        norm_gain,
        route_expert,
        route_slot,
        capacity,
        senders,
    )
    grad_shard = weight_grad(hidden, first_rows, second_rows, float(replicas * ROUNDS))
    return (input_out, grad_shard)


def solution(mesh):
    return jax.shard_map(
        local,
        mesh=mesh,
        in_specs=(
            P("pipe", ("expert", "edp"), None),
            P(("expert", "edp"), None),
            P("pipe", None, ("expert", "edp"), None),
            P("pipe", None),
            P("pipe", None, ("expert", "edp"), None),
            P("pipe", None, ("expert", "edp"), None),
            P("pipe", None, ("expert", "edp"), None),
            P("pipe", None, "expert", "edp", None),
            P("pipe", "expert", None, None),
            P("pipe", "expert", None, None),
        ),
        out_specs=(P("pipe", None, ("expert", "edp"), None), P("pipe", "expert", "edp", None)),
        check_vma=False,
    )
```

time: 170 us -> 88.1 us (0.52)
  waiting for transfers between devices: 85.4 us -> 41.3 us
  other arithmetic: 20.6 us -> 0 us
  matrix products: 17 us -> 0 us
  starting transfers between devices: 12.5 us -> 27.1 us
  between operations: 14.2 us -> 0.81 us
  Pallas kernels: 0 us -> 9.2 us
  blocking collectives: 8.06 us -> 0 us
  local copies, waits for them, and re-layouts: 11.8 us -> 9.44 us
    reduce_scatter x1 -> x0, waiting for transfers between devices: 68.9 us -> none  [local(): lax.psum_scatter(outer_term(both_hidden, both_rows), 'edp', scatter_dimen...]
    ppermute x1 -> x24, waiting for transfers between devices: 5.28 us -> 41.3 us  [the longest x18 28.9 us: steps_over(): lax.ppermute(values[step], axis, [(source, source ^ step) for source in r...]
    ppermute x1 -> x24, starting transfers between devices: 1.29 us -> 27.1 us  [the longest x18 22.2 us: steps_over(): lax.ppermute(values[step], axis, [(source, source ^ step) for source in r...]
    dot_general x5 -> x0, matrix products: 17 us -> none  [the longest x2 9.36 us: section_pass(): lax.dot_general(act_grad, w_gate_up[0, 0], (((1,), (1,)), ((), ())), pref...]
    all_to_all x3 -> x0, waiting for transfers between devices: 11.2 us -> none  [the longest x2 9.44 us: section_pass(): lax.all_to_all(expert_grad.reshape(senders, capacity, model_width), 'expe...]
    all_to_all x3 -> x0, starting transfers between devices: 11.1 us -> none  [the longest x2 6.9 us: section_pass(): lax.all_to_all(expert_grad.reshape(senders, capacity, model_width), 'expe...]
    unnamed x20 -> x33, local copies, waits for them, and re-layouts: 0.04 us -> 9.43 us
    pallas_call x0 -> x7, Pallas kernels: none -> 9.2 us  [the longest x6 8.76 us: on_chip(): pl.pallas_call(body, out_shape=outs, in_specs=[spec] * len(args), out_spe...]
  transfers between devices with their start and end apart: 5 -> 24, of which waited for: 5 -> 11; matrix products, arithmetic and copies ran while one was open for 12% -> 3% of each run, Pallas kernels for 0% -> 8%
where the time goes in v1:
time: 88.1 us; the launch traced here: 87.8 us
  waiting for transfers between devices  41.3 us (47%)
  starting transfers between devices  27.1 us (31%)
  local copies, waits for them, and re-layouts  9.44 us (11%)
  Pallas kernels  9.2 us (10%)
    ppermute x18, waiting for transfers between devices, steps_over(): lax.ppermute(values[step], axis, [(source, source ^ step) for source in r...  28.9 us
    ppermute x18, starting transfers between devices, steps_over(): lax.ppermute(values[step], axis, [(source, source ^ step) for source in r...  22.2 us
    ppermute x4, waiting for transfers between devices, behind(): lax.ppermute(value, ('pipe', 'expert'), [(section * count + source, (sect...  12.4 us
    unnamed x33, local copies, waits for them, and re-layouts  9.43 us
    pallas_call x6, Pallas kernels, on_chip(): pl.pallas_call(body, out_shape=outs, in_specs=[spec] * len(args), out_spe...  8.76 us
    ppermute x4, starting transfers between devices, behind(): lax.ppermute(value, ('pipe', 'expert'), [(section * count + source, (sect...  2.19 us
  transfers between devices with their start and end apart: 24, of which 11 were waited for; matrix products, arithmetic and copies ran while one was open for 3% of the time, Pallas kernels for 8%

profile of v1, /device:TPU:0, one launch (start us, length us, event | category | flops | bytes accessed | tf_op | source)
XLA Modules:
  0.0 87.8 jit_solution(11489433970901936517)
XLA Ops:
  0.6 0.0 copy-start.4
  0.6 1.0 %copy-done.4 = bf16[1,2,1,64,1408]{4,3,2,1,0:T(8,128)(2,1)S(1)} copy-done((bf16[1,2,1,64,1408]{4,3,2,1,0:T(8,128)(2,1)S(1)}, bf16[1,2,1,64,1408]{4,3,2,1,0:T(8,128)(2,1)}, u32[]{:S(2)}) %copy-start.4) | copy-done | bytes 360472
  1.6 0.4 shard_map.118
  2.1 3.1 %collective-permute-start.15 = (bf16[176,128]{1,0:T(8,128)(2,1)S(1)}, bf16[176,128]{1,0:T(8,128)(2,1)S(1)}, u32[]{:S(2)}, u32[]{:S(2)}) collective-permute-start(bf16[176,128]{1,0:T(8,128)(2,1)S(1)} %get-tuple-element.43), channel_id=1, source_target_pairs={{0,1},{1,0},{2,3},{3,2},{4,5},{5,4},{6,7},{7,6},{8,9},{9,8},{10,11... | collective-permute-start | bytes 135176 | tf_op jit(solution)/shard_map/ppermute | solution.py:273
  5.2 0.8 copy.15.expert_ref
  5.9 0.8 copy.16.slot_ref
  6.7 0.8 copy.14.gate_ref
  7.5 0.0 copy-start.8
  7.5 0.9 %copy-done.8 = bf16[1,64,1792]{2,1,0:T(8,128)(2,1)S(1)} copy-done((bf16[1,64,1792]{2,1,0:T(8,128)(2,1)S(1)}, bf16[1,64,1792]{2,1,0:T(8,128)(2,1)}, u32[]{:S(2)}) %copy-start.8) | copy-done | bytes 229400
  8.4 0.3 shard_map.113
  8.8 1.6 %collective-permute-start = (f32[64,2]{1,0:T(8,128)S(1)}, f32[64,2]{1,0:T(8,128)S(1)}, u32[]{:S(2)}, u32[]{:S(2)}) collective-permute-start(f32[64,2]{1,0:T(8,128)S(1)} %get-tuple-element.24), channel_id=1, source_target_pairs={{0,16},{16,0},{1,17},{17,1},{2,18},{18,2},{3,19},{19,3},{4,20},{20... | collective-permute-start | bytes 1544 | tf_op jit(solution)/shard_map/ppermute | solution.py:337
  10.3 0.0 collective-permute-start.1
  10.3 1.5 %collective-permute-start.2 = (bf16[16,1792]{1,0:T(8,128)(2,1)S(1)}, bf16[16,1792]{1,0:T(8,128)(2,1)S(1)}, u32[]{:S(2)}, u32[]{:S(2)}) collective-permute-start(bf16[16,1792]{1,0:T(8,128)(2,1)S(1)} %get-tuple-element.27), channel_id=1, source_target_pairs={{0,8},{4,12},{8,0},{12,4},{1,9},{5,13},{9,1},{13,5},{2,10},{6,14},... | collective-permute-start | bytes 172040 | tf_op jit(solution)/shard_map/ppermute | solution.py:273
  11.9 0.3 collective-permute-start.3
  12.2 0.0 collective-permute-done.1.refs_1_
  12.2 2.5 %collective-permute-done.2.refs_2_ = bf16[16,1792]{1,0:T(8,128)(2,1)S(1)} collective-permute-done((bf16[16,1792]{1,0:T(8,128)(2,1)S(1)}, bf16[16,1792]{1,0:T(8,128)(2,1)S(1)}, u32[]{:S(2)}, u32[]{:S(2)}) %collective-permute-start.2) | collective-permute-done | bytes 57376 | tf_op jit(solution)/shard_map/ppermute | solution.py:273
  14.7 1.1 %collective-permute-done.3.refs_3_ = bf16[16,1792]{1,0:T(8,128)(2,1)S(1)} collective-permute-done((bf16[16,1792]{1,0:T(8,128)(2,1)S(1)}, bf16[16,1792]{1,0:T(8,128)(2,1)S(1)}, u32[]{:S(2)}, u32[]{:S(2)}) %collective-permute-start.3) | collective-permute-done | bytes 57376 | tf_op jit(solution)/shard_map/ppermute | solution.py:273
  15.8 2.4 %copy-done = bf16[1,1,1792,1408]{3,2,1,0:T(8,128)(2,1)S(1)} copy-done((bf16[1,1,1792,1408]{3,2,1,0:T(8,128)(2,1)S(1)}, bf16[1,1,1792,1408]{3,2,1,0:T(8,128)(2,1)}, u32[]{:S(2)}) %copy-start) | copy-done | bytes 5046296
  18.2 1.7 %copy-done.2 = bf16[1,1,704,1792]{3,2,1,0:T(8,128)(2,1)S(1)} copy-done((bf16[1,1,704,1792]{3,2,1,0:T(8,128)(2,1)S(1)}, bf16[1,1,704,1792]{3,2,1,0:T(8,128)(2,1)}, u32[]{:S(2)}) %copy-start.2) | copy-done | bytes 2523160
  19.9 1.0 %copy-done.5 = bf16[1,2,1,64,1408]{4,3,2,1,0:T(8,128)(2,1)S(1)} copy-done((bf16[1,2,1,64,1408]{4,3,2,1,0:T(8,128)(2,1)S(1)}, bf16[1,2,1,64,1408]{4,3,2,1,0:T(8,128)(2,1)}, u32[]{:S(2)}) %copy-start.5) | copy-done | bytes 360472
  20.9 2.5 %shard_map.114 = (bf16[16,1792]{1,0:T(8,128)(2,1)S(1)}, bf16[16,1792]{1,0:T(8,128)(2,1)S(1)}, bf16[16,1792]{1,0:T(8,128)(2,1)S(1)}, bf16[16,1792]{1,0:T(8,128)(2,1)S(1)}) custom-call(bf16[1,2,1,64,1408]{4,3,2,1,0:T(8,128)(2,1)S(1)} %copy-done.5, bf16[1792,1408]{1,0:T(8,128)(2,1)S(1)} %bitcast.3, bf16[704,1792]{1,0:T(8,128)(2,1)S(1)} %bitcast.5, ...), custom_call_target="tpu_custom_call" | custom-call | flops 484442112 | bytes 7569408 | tf_op jit(solution)/shard_map/pallas_call | solution.py:18
  23.4 0.2 collective-permute-start.4
  23.6 1.3 %collective-permute-start.5 = (bf16[16,1792]{1,0:T(8,128)(2,1)S(1)}, bf16[16,1792]{1,0:T(8,128)(2,1)S(1)}, u32[]{:S(2)}, u32[]{:S(2)}) collective-permute-start(bf16[16,1792]{1,0:T(8,128)(2,1)S(1)} %get-tuple-element.31), channel_id=1, source_target_pairs={{0,8},{4,12},{8,0},{12,4},{1,9},{5,13},{9,1},{13,5},{2,10},{6,14},... | collective-permute-start | bytes 172040 | tf_op jit(solution)/shard_map/ppermute | solution.py:273
  25.0 0.4 collective-permute-start.6
  25.4 0.0 collective-permute-done.table_ref
  25.4 2.7 %collective-permute-start.16 = (bf16[176,128]{1,0:T(8,128)(2,1)S(1)}, bf16[176,128]{1,0:T(8,128)(2,1)S(1)}, u32[]{:S(2)}, u32[]{:S(2)}) collective-permute-start(bf16[176,128]{1,0:T(8,128)(2,1)S(1)} %get-tuple-element.44), channel_id=1, source_target_pairs={{0,2},{1,3},{2,0},{3,1},{4,6},{5,7},{6,4},{7,5},{8,10},{9,11},{10,... | collective-permute-start | bytes 135176 | tf_op jit(solution)/shard_map/ppermute | solution.py:273
  28.0 0.0 collective-permute-done.4.refs_1_
  28.0 0.2 collective-permute-start.17
  28.2 0.0 collective-permute-done.5.refs_2_
  28.3 0.7 collective-permute-done.6.refs_3_
  29.0 0.7 shard_map.115
  29.7 0.6 collective-permute-start.8
  30.3 2.9 %collective-permute-start.20 = (bf16[64,1792]{1,0:T(8,128)(2,1)S(1)}, bf16[64,1792]{1,0:T(8,128)(2,1)S(1)}, u32[]{:S(2)}, u32[]{:S(2)}) collective-permute-start(bf16[64,1792]{1,0:T(8,128)(2,1)S(1)} %constant_dynamic-update-slice_fusion.refs_4_), channel_id=1, source_target_pairs={{0,3},{1,2},{2,1},{3,0},{4,7},{5,6},{6,5},{7,4},{8,11},{9,10},{10,... | collective-permute-start | bytes 688136 | tf_op jit(solution)/shard_map/ppermute | solution.py:273
  33.2 0.7 collective-permute-done.8.refs_0_
  33.9 0.0 collective-permute-start.9
  34.0 3.6 %collective-permute-done.9.refs_1_ = bf16[16,1792]{1,0:T(8,128)(2,1)S(1)} collective-permute-done((bf16[16,1792]{1,0:T(8,128)(2,1)S(1)}, bf16[16,1792]{1,0:T(8,128)(2,1)S(1)}, u32[]{:S(2)}, u32[]{:S(2)}) %collective-permute-start.9) | collective-permute-done | bytes 57376 | tf_op jit(solution)/shard_map/ppermute | solution.py:281
  37.6 1.6 %collective-permute-start.10 = (bf16[16,1792]{1,0:T(8,128)(2,1)S(1)}, bf16[16,1792]{1,0:T(8,128)(2,1)S(1)}, u32[]{:S(2)}, u32[]{:S(2)}) collective-permute-start(bf16[16,1792]{1,0:T(8,128)(2,1)S(1)} %get-tuple-element.36), channel_id=1, source_target_pairs={{0,24},{4,28},{8,16},{12,20},{16,8},{20,12},{24,0},{28,4},{1,25},{... | collective-permute-start | bytes 172040 | tf_op jit(solution)/shard_map/ppermute | solution.py:281
  39.2 3.5 %collective-permute-done.10.refs_2_ = bf16[16,1792]{1,0:T(8,128)(2,1)S(1)} collective-permute-done((bf16[16,1792]{1,0:T(8,128)(2,1)S(1)}, bf16[16,1792]{1,0:T(8,128)(2,1)S(1)}, u32[]{:S(2)}, u32[]{:S(2)}) %collective-permute-start.10) | collective-permute-done | bytes 57376 | tf_op jit(solution)/shard_map/ppermute | solution.py:281
  42.7 0.0 collective-permute-start.11
  42.7 4.5 %collective-permute-done.11.refs_3_ = bf16[16,1792]{1,0:T(8,128)(2,1)S(1)} collective-permute-done((bf16[16,1792]{1,0:T(8,128)(2,1)S(1)}, bf16[16,1792]{1,0:T(8,128)(2,1)S(1)}, u32[]{:S(2)}, u32[]{:S(2)}) %collective-permute-start.11) | collective-permute-done | bytes 57376 | tf_op jit(solution)/shard_map/ppermute | solution.py:281
  47.2 1.1 %collective-permute-start.7 = (bf16[64,1792]{1,0:T(8,128)(2,1)S(1)}, bf16[64,1792]{1,0:T(8,128)(2,1)S(1)}, u32[]{:S(2)}, u32[]{:S(2)}) collective-permute-start(bf16[64,1792]{1,0:T(8,128)(2,1)S(1)} %get-tuple-element.33.first_ref), channel_id=1, source_target_pairs={{0,16},{16,0},{1,17},{17,1},{2,18},{18,2},{3,19},{19,3},{4,20},{20... | collective-permute-start | bytes 688136 | tf_op jit(solution)/shard_map/ppermute | solution.py:358
  48.3 2.5 %shard_map.116 = (bf16[16,1792]{1,0:T(8,128)(2,1)S(1)}, bf16[16,1792]{1,0:T(8,128)(2,1)S(1)}, bf16[16,1792]{1,0:T(8,128)(2,1)S(1)}, bf16[16,1792]{1,0:T(8,128)(2,1)S(1)}) custom-call(bf16[1,2,1,64,1408]{4,3,2,1,0:T(8,128)(2,1)S(1)} %copy-done.6, bf16[1792,1408]{1,0:T(8,128)(2,1)S(1)} %bitcast.4, bf16[704,1792]{1,0:T(8,128)(2,1)S(1)} %bitcast.6, ...), custom_call_target="tpu_custom_call" | custom-call | flops 484442112 | bytes 7569408 | tf_op jit(solution)/shard_map/pallas_call | solution.py:18
  50.8 0.0 collective-permute-done.15.refs_1_
  50.8 0.1 collective-permute-start.12
  50.9 0.0 collective-permute-done.16.refs_2_
  50.9 1.1 %collective-permute-start.13 = (bf16[16,1792]{1,0:T(8,128)(2,1)S(1)}, bf16[16,1792]{1,0:T(8,128)(2,1)S(1)}, u32[]{:S(2)}, u32[]{:S(2)}) collective-permute-start(bf16[16,1792]{1,0:T(8,128)(2,1)S(1)} %get-tuple-element.40), channel_id=1, source_target_pairs={{0,8},{4,12},{8,0},{12,4},{1,9},{5,13},{9,1},{13,5},{2,10},{6,14},... | collective-permute-start | bytes 172040 | tf_op jit(solution)/shard_map/ppermute | solution.py:273
  52.0 0.0 collective-permute-done.17.refs_3_
  52.0 0.8 collective-permute-start.14
  52.8 0.0 collective-permute-done.12.refs_1_
  52.8 2.6 %collective-permute-start.19 = (bf16[64,1792]{1,0:T(8,128)(2,1)S(1)}, bf16[64,1792]{1,0:T(8,128)(2,1)S(1)}, u32[]{:S(2)}, u32[]{:S(2)}) collective-permute-start(bf16[64,1792]{1,0:T(8,128)(2,1)S(1)} %constant_dynamic-update-slice_fusion.refs_4_), channel_id=1, source_target_pairs={{0,2},{1,3},{2,0},{3,1},{4,6},{5,7},{6,4},{7,5},{8,10},{9,11},{10,... | collective-permute-start | bytes 688136 | tf_op jit(solution)/shard_map/ppermute | solution.py:273
  55.4 0.2 collective-permute-done.13.refs_2_
  55.6 0.6 collective-permute-start.18
  56.2 0.0 collective-permute-done.14.refs_3_
  56.2 3.4 %collective-permute-start.23 = (bf16[64,1792]{1,0:T(8,128)(2,1)S(1)}, bf16[64,1792]{1,0:T(8,128)(2,1)S(1)}, u32[]{:S(2)}, u32[]{:S(2)}) collective-permute-start(bf16[64,1792]{1,0:T(8,128)(2,1)S(1)} %constant_dynamic-update-slice_fusion.4.refs_8_), channel_id=1, source_target_pairs={{0,3},{1,2},{2,1},{3,0},{4,7},{5,6},{6,5},{7,4},{8,11},{9,10},{10,... | collective-permute-start | bytes 688136 | tf_op jit(solution)/shard_map/ppermute | solution.py:273
  59.6 0.0 collective-permute-done.20.refs_7_
  59.6 0.0 collective-permute-start.22
  59.6 0.0 collective-permute-done.7.passed_ref
  59.6 1.0 %collective-permute-start.21 = (bf16[64,1792]{1,0:T(8,128)(2,1)S(1)}, bf16[64,1792]{1,0:T(8,128)(2,1)S(1)}, u32[]{:S(2)}, u32[]{:S(2)}) collective-permute-start(bf16[64,1792]{1,0:T(8,128)(2,1)S(1)} %constant_dynamic-update-slice_fusion.4.refs_8_), channel_id=1, source_target_pairs={{0,1},{1,0},{2,3},{3,2},{4,5},{5,4},{6,7},{7,6},{8,9},{9,8},{10,11... | collective-permute-start | bytes 688136 | tf_op jit(solution)/shard_map/ppermute | solution.py:273
  60.6 1.2 %shard_map.117 = bf16[1,2,64,1792]{3,2,1,0:T(8,128)(2,1)} custom-call(bf16[64,1792]{1,0:T(8,128)(2,1)S(1)} %get-tuple-element.33.first_ref, bf16[64,1792]{1,0:T(8,128)(2,1)S(1)} %collective-permute-done.7.passed_ref, bf16[64,1792]{1,0:T(8,128)(2,1)S(1)} %copy-done.10, bf16[1,2,64,1792]{3,2,1,0:T(8,128)(2,1)S(1)} %copy-done.7, f32[1,1792]{1,0:T(1,128)S(1)} %copy-done.11, ...), custom_call_target="tpu_custom_call" | custom-call | bytes 1835008 | tf_op jit(solution)/shard_map/pallas_call | solution.py:18
  61.8 5.4 %collective-permute-done.19.refs_6_ = bf16[64,1792]{1,0:T(8,128)(2,1)S(1)} collective-permute-done((bf16[64,1792]{1,0:T(8,128)(2,1)S(1)}, bf16[64,1792]{1,0:T(8,128)(2,1)S(1)}, u32[]{:S(2)}, u32[]{:S(2)}) %collective-permute-start.19) | collective-permute-done | bytes 229408 | tf_op jit(solution)/shard_map/ppermute | solution.py:273
  67.2 6.4 %collective-permute-done.18.refs_5_ = bf16[64,1792]{1,0:T(8,128)(2,1)S(1)} collective-permute-done((bf16[64,1792]{1,0:T(8,128)(2,1)S(1)}, bf16[64,1792]{1,0:T(8,128)(2,1)S(1)}, u32[]{:S(2)}, u32[]{:S(2)}) %collective-permute-start.18) | collective-permute-done | bytes 229408 | tf_op jit(solution)/shard_map/ppermute | solution.py:273
  73.6 0.0 collective-permute-done.23.refs_11_
  73.7 12.6 %collective-permute-done.22.refs_10_ = bf16[64,1792]{1,0:T(8,128)(2,1)S(1)} collective-permute-done((bf16[64,1792]{1,0:T(8,128)(2,1)S(1)}, bf16[64,1792]{1,0:T(8,128)(2,1)S(1)}, u32[]{:S(2)}, u32[]{:S(2)}) %collective-permute-start.22) | collective-permute-done | bytes 229408 | tf_op jit(solution)/shard_map/ppermute | solution.py:273
  86.3 1.6 %shard_map.119 = f32[1,1,176,1792]{3,2,1,0:T(8,128)} custom-call(bf16[176,128]{1,0:T(8,128)(2,1)S(1)} %get-tuple-element.42.refs_0_, bf16[176,128]{1,0:T(8,128)(2,1)S(1)} %collective-permute-done.15.refs_1_, bf16[176,128]{1,0:T(8,128)(2,1)S(1)} %collective-permute-done.16.refs_2_, bf16[176,128]{1,0:T(8,128)(2,1)S(1)} %collective-permute-done.17.refs_3_, ...), custom_call_target="tpu_custom_call" | custom-call | flops 322961408 | bytes 3096576 | tf_op jit(solution)/shard_map/pallas_call | solution.py:18
  (26 shorter events, 0.1 us)
Async XLA Ops:
  0.6 1.0 %copy-start.4 = (bf16[1,2,1,64,1408]{4,3,2,1,0:T(8,128)(2,1)S(1)}, bf16[1,2,1,64,1408]{4,3,2,1,0:T(8,128)(2,1)}, u32[]{:S(2)}) copy-start(bf16[1,2,1,64,1408]{4,3,2,1,0:T(8,128)(2,1)} %stored_ref.5) | copy-start | bytes 1081348
  2.1 48.8 %collective-permute-start.15 = (bf16[176,128]{1,0:T(8,128)(2,1)S(1)}, bf16[176,128]{1,0:T(8,128)(2,1)S(1)}, u32[]{:S(2)}, u32[]{:S(2)}) collective-permute-start(bf16[176,128]{1,0:T(8,128)(2,1)S(1)} %get-tuple-element.43), channel_id=1, source_target_pairs={{0,1},{1,0},{2,3},{3,2},{4,5},{5,4},{6,7},{7,6},{8,9},{9,8},{10,11... | collective-permute-start | bytes 135176 | tf_op jit(solution)/shard_map/ppermute | solution.py:273
  7.5 0.9 %copy-start.8 = (bf16[1,64,1792]{2,1,0:T(8,128)(2,1)S(1)}, bf16[1,64,1792]{2,1,0:T(8,128)(2,1)}, u32[]{:S(2)}) copy-start(bf16[1,64,1792]{2,1,0:T(8,128)(2,1)} %param.10) | copy-start | bytes 688132
  8.4 20.5 %copy-start.9 = (bf16[1,64,1792]{2,1,0:T(8,128)(2,1)S(1)}, bf16[1,64,1792]{2,1,0:T(8,128)(2,1)}, u32[]{:S(2)}) copy-start(bf16[1,64,1792]{2,1,0:T(8,128)(2,1)} %param.10) | copy-start | bytes 688132
  8.4 20.5 %copy-start.10 = (bf16[64,1792]{1,0:T(8,128)(2,1)S(1)}, bf16[64,1792]{1,0:T(8,128)(2,1)}, u32[]{:S(2)}) copy-start(bf16[64,1792]{1,0:T(8,128)(2,1)} %tail_ref.3) | copy-start | bytes 688132
  8.8 16.6 %collective-permute-start = (f32[64,2]{1,0:T(8,128)S(1)}, f32[64,2]{1,0:T(8,128)S(1)}, u32[]{:S(2)}, u32[]{:S(2)}) collective-permute-start(f32[64,2]{1,0:T(8,128)S(1)} %get-tuple-element.24), channel_id=1, source_target_pairs={{0,16},{16,0},{1,17},{17,1},{2,18},{18,2},{3,19},{19,3},{4,20},{20... | collective-permute-start | bytes 1544 | tf_op jit(solution)/shard_map/ppermute | solution.py:337
  10.3 1.9 %collective-permute-start.1 = (bf16[16,1792]{1,0:T(8,128)(2,1)S(1)}, bf16[16,1792]{1,0:T(8,128)(2,1)S(1)}, u32[]{:S(2)}, u32[]{:S(2)}) collective-permute-start(bf16[16,1792]{1,0:T(8,128)(2,1)S(1)} %get-tuple-element.26), channel_id=1, source_target_pairs={{0,4},{4,0},{8,12},{12,8},{1,5},{5,1},{9,13},{13,9},{2,6},{6,2},{1... | collective-permute-start | bytes 172040 | tf_op jit(solution)/shard_map/ppermute | solution.py:273
  10.3 4.3 %collective-permute-start.2 = (bf16[16,1792]{1,0:T(8,128)(2,1)S(1)}, bf16[16,1792]{1,0:T(8,128)(2,1)S(1)}, u32[]{:S(2)}, u32[]{:S(2)}) collective-permute-start(bf16[16,1792]{1,0:T(8,128)(2,1)S(1)} %get-tuple-element.27), channel_id=1, source_target_pairs={{0,8},{4,12},{8,0},{12,4},{1,9},{5,13},{9,1},{13,5},{2,10},{6,14},... | collective-permute-start | bytes 172040 | tf_op jit(solution)/shard_map/ppermute | solution.py:273
  11.9 3.9 %collective-permute-start.3 = (bf16[16,1792]{1,0:T(8,128)(2,1)S(1)}, bf16[16,1792]{1,0:T(8,128)(2,1)S(1)}, u32[]{:S(2)}, u32[]{:S(2)}) collective-permute-start(bf16[16,1792]{1,0:T(8,128)(2,1)S(1)} %get-tuple-element.28), channel_id=1, source_target_pairs={{0,12},{4,8},{8,4},{12,0},{1,13},{5,9},{9,5},{13,1},{2,14},{6,10},... | collective-permute-start | bytes 172040 | tf_op jit(solution)/shard_map/ppermute | solution.py:273
  15.8 2.4 %copy-start = (bf16[1,1,1792,1408]{3,2,1,0:T(8,128)(2,1)S(1)}, bf16[1,1,1792,1408]{3,2,1,0:T(8,128)(2,1)}, u32[]{:S(2)}) copy-start(bf16[1,1,1792,1408]{3,2,1,0:T(8,128)(2,1)} %param.18) | copy-start | bytes 15138820
  18.2 1.7 %copy-start.2 = (bf16[1,1,704,1792]{3,2,1,0:T(8,128)(2,1)S(1)}, bf16[1,1,704,1792]{3,2,1,0:T(8,128)(2,1)}, u32[]{:S(2)}) copy-start(bf16[1,1,704,1792]{3,2,1,0:T(8,128)(2,1)} %param.19) | copy-start | bytes 7569412
  19.9 1.0 %copy-start.5 = (bf16[1,2,1,64,1408]{4,3,2,1,0:T(8,128)(2,1)S(1)}, bf16[1,2,1,64,1408]{4,3,2,1,0:T(8,128)(2,1)}, u32[]{:S(2)}) copy-start(bf16[1,2,1,64,1408]{4,3,2,1,0:T(8,128)(2,1)} %stored_ref.5) | copy-start | bytes 1081348
  20.9 8.1 %copy-start.7 = (bf16[1,2,64,1792]{3,2,1,0:T(8,128)(2,1)S(1)}, bf16[1,2,64,1792]{3,2,1,0:T(8,128)(2,1)}, u32[]{:S(2)}) copy-start(bf16[1,2,64,1792]{3,2,1,0:T(8,128)(2,1)} %saved_ref.3) | copy-start | bytes 1376260
  20.9 8.1 %copy-start.11 = (f32[1,1792]{1,0:T(1,128)S(1)}, f32[1,1792]{1,0:T(1,128)}, u32[]{:S(2)}) copy-start(f32[1,1792]{1,0:T(1,128)} %gain_ref.3) | copy-start | bytes 21508
  20.9 27.4 %copy-start.1 = (bf16[1,1,1792,1408]{3,2,1,0:T(8,128)(2,1)S(1)}, bf16[1,1,1792,1408]{3,2,1,0:T(8,128)(2,1)}, u32[]{:S(2)}) copy-start(bf16[1,1,1792,1408]{3,2,1,0:T(8,128)(2,1)} %param.18) | copy-start | bytes 15138820
  20.9 27.4 %copy-start.3 = (bf16[1,1,704,1792]{3,2,1,0:T(8,128)(2,1)S(1)}, bf16[1,1,704,1792]{3,2,1,0:T(8,128)(2,1)}, u32[]{:S(2)}) copy-start(bf16[1,1,704,1792]{3,2,1,0:T(8,128)(2,1)} %param.19) | copy-start | bytes 7569412
  20.9 27.4 %copy-start.6 = (bf16[1,2,1,64,1408]{4,3,2,1,0:T(8,128)(2,1)S(1)}, bf16[1,2,1,64,1408]{4,3,2,1,0:T(8,128)(2,1)}, u32[]{:S(2)}) copy-start(bf16[1,2,1,64,1408]{4,3,2,1,0:T(8,128)(2,1)} %stored_ref.5) | copy-start | bytes 1081348
  23.4 4.6 %collective-permute-start.4 = (bf16[16,1792]{1,0:T(8,128)(2,1)S(1)}, bf16[16,1792]{1,0:T(8,128)(2,1)S(1)}, u32[]{:S(2)}, u32[]{:S(2)}) collective-permute-start(bf16[16,1792]{1,0:T(8,128)(2,1)S(1)} %get-tuple-element.30), channel_id=1, source_target_pairs={{0,4},{4,0},{8,12},{12,8},{1,5},{5,1},{9,13},{13,9},{2,6},{6,2},{1... | collective-permute-start | bytes 172040 | tf_op jit(solution)/shard_map/ppermute | solution.py:273
  23.6 4.6 %collective-permute-start.5 = (bf16[16,1792]{1,0:T(8,128)(2,1)S(1)}, bf16[16,1792]{1,0:T(8,128)(2,1)S(1)}, u32[]{:S(2)}, u32[]{:S(2)}) collective-permute-start(bf16[16,1792]{1,0:T(8,128)(2,1)S(1)} %get-tuple-element.31), channel_id=1, source_target_pairs={{0,8},{4,12},{8,0},{12,4},{1,9},{5,13},{9,1},{13,5},{2,10},{6,14},... | collective-permute-start | bytes 172040 | tf_op jit(solution)/shard_map/ppermute | solution.py:273
  25.0 4.0 %collective-permute-start.6 = (bf16[16,1792]{1,0:T(8,128)(2,1)S(1)}, bf16[16,1792]{1,0:T(8,128)(2,1)S(1)}, u32[]{:S(2)}, u32[]{:S(2)}) collective-permute-start(bf16[16,1792]{1,0:T(8,128)(2,1)S(1)} %get-tuple-element.32), channel_id=1, source_target_pairs={{0,12},{4,8},{8,4},{12,0},{1,13},{5,9},{9,5},{13,1},{2,14},{6,10},... | collective-permute-start | bytes 172040 | tf_op jit(solution)/shard_map/ppermute | solution.py:273
  25.4 25.6 %collective-permute-start.16 = (bf16[176,128]{1,0:T(8,128)(2,1)S(1)}, bf16[176,128]{1,0:T(8,128)(2,1)S(1)}, u32[]{:S(2)}, u32[]{:S(2)}) collective-permute-start(bf16[176,128]{1,0:T(8,128)(2,1)S(1)} %get-tuple-element.44), channel_id=1, source_target_pairs={{0,2},{1,3},{2,0},{3,1},{4,6},{5,7},{6,4},{7,5},{8,10},{9,11},{10,... | collective-permute-start | bytes 135176 | tf_op jit(solution)/shard_map/ppermute | solution.py:273
  28.0 24.0 %collective-permute-start.17 = (bf16[176,128]{1,0:T(8,128)(2,1)S(1)}, bf16[176,128]{1,0:T(8,128)(2,1)S(1)}, u32[]{:S(2)}, u32[]{:S(2)}) collective-permute-start(bf16[176,128]{1,0:T(8,128)(2,1)S(1)} %get-tuple-element.45), channel_id=1, source_target_pairs={{0,3},{1,2},{2,1},{3,0},{4,7},{5,6},{6,5},{7,4},{8,11},{9,10},{10,... | collective-permute-start | bytes 135176 | tf_op jit(solution)/shard_map/ppermute | solution.py:273
  29.7 4.2 %collective-permute-start.8 = (bf16[16,1792]{1,0:T(8,128)(2,1)S(1)}, bf16[16,1792]{1,0:T(8,128)(2,1)S(1)}, u32[]{:S(2)}, u32[]{:S(2)}) collective-permute-start(bf16[16,1792]{1,0:T(8,128)(2,1)S(1)} %get-tuple-element.34), channel_id=1, source_target_pairs={{0,16},{4,20},{8,24},{12,28},{16,0},{20,4},{24,8},{28,12},{1,17},{... | collective-permute-start | bytes 172040 | tf_op jit(solution)/shard_map/ppermute | solution.py:281
  30.3 29.3 %collective-permute-start.20 = (bf16[64,1792]{1,0:T(8,128)(2,1)S(1)}, bf16[64,1792]{1,0:T(8,128)(2,1)S(1)}, u32[]{:S(2)}, u32[]{:S(2)}) collective-permute-start(bf16[64,1792]{1,0:T(8,128)(2,1)S(1)} %constant_dynamic-update-slice_fusion.refs_4_), channel_id=1, source_target_pairs={{0,3},{1,2},{2,1},{3,0},{4,7},{5,6},{6,5},{7,4},{8,11},{9,10},{10,... | collective-permute-start | bytes 688136 | tf_op jit(solution)/shard_map/ppermute | solution.py:273
  33.9 3.7 %collective-permute-start.9 = (bf16[16,1792]{1,0:T(8,128)(2,1)S(1)}, bf16[16,1792]{1,0:T(8,128)(2,1)S(1)}, u32[]{:S(2)}, u32[]{:S(2)}) collective-permute-start(bf16[16,1792]{1,0:T(8,128)(2,1)S(1)} %get-tuple-element.35), channel_id=1, source_target_pairs={{0,20},{4,16},{8,28},{12,24},{16,4},{20,0},{24,12},{28,8},{1,21},{... | collective-permute-start | bytes 172040 | tf_op jit(solution)/shard_map/ppermute | solution.py:281
  37.6 5.1 %collective-permute-start.10 = (bf16[16,1792]{1,0:T(8,128)(2,1)S(1)}, bf16[16,1792]{1,0:T(8,128)(2,1)S(1)}, u32[]{:S(2)}, u32[]{:S(2)}) collective-permute-start(bf16[16,1792]{1,0:T(8,128)(2,1)S(1)} %get-tuple-element.36), channel_id=1, source_target_pairs={{0,24},{4,28},{8,16},{12,20},{16,8},{20,12},{24,0},{28,4},{1,25},{... | collective-permute-start | bytes 172040 | tf_op jit(solution)/shard_map/ppermute | solution.py:281
  42.7 4.5 %collective-permute-start.11 = (bf16[16,1792]{1,0:T(8,128)(2,1)S(1)}, bf16[16,1792]{1,0:T(8,128)(2,1)S(1)}, u32[]{:S(2)}, u32[]{:S(2)}) collective-permute-start(bf16[16,1792]{1,0:T(8,128)(2,1)S(1)} %get-tuple-element.37), channel_id=1, source_target_pairs={{0,28},{4,24},{8,20},{12,16},{16,12},{20,8},{24,4},{28,0},{1,29},{... | collective-permute-start | bytes 172040 | tf_op jit(solution)/shard_map/ppermute | solution.py:281
  47.2 12.5 %collective-permute-start.7 = (bf16[64,1792]{1,0:T(8,128)(2,1)S(1)}, bf16[64,1792]{1,0:T(8,128)(2,1)S(1)}, u32[]{:S(2)}, u32[]{:S(2)}) collective-permute-start(bf16[64,1792]{1,0:T(8,128)(2,1)S(1)} %get-tuple-element.33.first_ref), channel_id=1, source_target_pairs={{0,16},{16,0},{1,17},{17,1},{2,18},{18,2},{3,19},{19,3},{4,20},{20... | collective-permute-start | bytes 688136 | tf_op jit(solution)/shard_map/ppermute | solution.py:358
  50.8 2.0 %collective-permute-start.12 = (bf16[16,1792]{1,0:T(8,128)(2,1)S(1)}, bf16[16,1792]{1,0:T(8,128)(2,1)S(1)}, u32[]{:S(2)}, u32[]{:S(2)}) collective-permute-start(bf16[16,1792]{1,0:T(8,128)(2,1)S(1)} %get-tuple-element.39), channel_id=1, source_target_pairs={{0,4},{4,0},{8,12},{12,8},{1,5},{5,1},{9,13},{13,9},{2,6},{6,2},{1... | collective-permute-start | bytes 172040 | tf_op jit(solution)/shard_map/ppermute | solution.py:273
  50.9 4.7 %collective-permute-start.13 = (bf16[16,1792]{1,0:T(8,128)(2,1)S(1)}, bf16[16,1792]{1,0:T(8,128)(2,1)S(1)}, u32[]{:S(2)}, u32[]{:S(2)}) collective-permute-start(bf16[16,1792]{1,0:T(8,128)(2,1)S(1)} %get-tuple-element.40), channel_id=1, source_target_pairs={{0,8},{4,12},{8,0},{12,4},{1,9},{5,13},{9,1},{13,5},{2,10},{6,14},... | collective-permute-start | bytes 172040 | tf_op jit(solution)/shard_map/ppermute | solution.py:273
  52.0 4.2 %collective-permute-start.14 = (bf16[16,1792]{1,0:T(8,128)(2,1)S(1)}, bf16[16,1792]{1,0:T(8,128)(2,1)S(1)}, u32[]{:S(2)}, u32[]{:S(2)}) collective-permute-start(bf16[16,1792]{1,0:T(8,128)(2,1)S(1)} %get-tuple-element.41), channel_id=1, source_target_pairs={{0,12},{4,8},{8,4},{12,0},{1,13},{5,9},{9,5},{13,1},{2,14},{6,10},... | collective-permute-start | bytes 172040 | tf_op jit(solution)/shard_map/ppermute | solution.py:273
  52.8 14.4 %collective-permute-start.19 = (bf16[64,1792]{1,0:T(8,128)(2,1)S(1)}, bf16[64,1792]{1,0:T(8,128)(2,1)S(1)}, u32[]{:S(2)}, u32[]{:S(2)}) collective-permute-start(bf16[64,1792]{1,0:T(8,128)(2,1)S(1)} %constant_dynamic-update-slice_fusion.refs_4_), channel_id=1, source_target_pairs={{0,2},{1,3},{2,0},{3,1},{4,6},{5,7},{6,4},{7,5},{8,10},{9,11},{10,... | collective-permute-start | bytes 688136 | tf_op jit(solution)/shard_map/ppermute | solution.py:273
  55.6 18.0 %collective-permute-start.18 = (bf16[64,1792]{1,0:T(8,128)(2,1)S(1)}, bf16[64,1792]{1,0:T(8,128)(2,1)S(1)}, u32[]{:S(2)}, u32[]{:S(2)}) collective-permute-start(bf16[64,1792]{1,0:T(8,128)(2,1)S(1)} %constant_dynamic-update-slice_fusion.refs_4_), channel_id=1, source_target_pairs={{0,1},{1,0},{2,3},{3,2},{4,5},{5,4},{6,7},{7,6},{8,9},{9,8},{10,11... | collective-permute-start | bytes 688136 | tf_op jit(solution)/shard_map/ppermute | solution.py:273
  56.2 17.4 %collective-permute-start.23 = (bf16[64,1792]{1,0:T(8,128)(2,1)S(1)}, bf16[64,1792]{1,0:T(8,128)(2,1)S(1)}, u32[]{:S(2)}, u32[]{:S(2)}) collective-permute-start(bf16[64,1792]{1,0:T(8,128)(2,1)S(1)} %constant_dynamic-update-slice_fusion.4.refs_8_), channel_id=1, source_target_pairs={{0,3},{1,2},{2,1},{3,0},{4,7},{5,6},{6,5},{7,4},{8,11},{9,10},{10,... | collective-permute-start | bytes 688136 | tf_op jit(solution)/shard_map/ppermute | solution.py:273
  59.6 26.6 %collective-permute-start.22 = (bf16[64,1792]{1,0:T(8,128)(2,1)S(1)}, bf16[64,1792]{1,0:T(8,128)(2,1)S(1)}, u32[]{:S(2)}, u32[]{:S(2)}) collective-permute-start(bf16[64,1792]{1,0:T(8,128)(2,1)S(1)} %constant_dynamic-update-slice_fusion.4.refs_8_), channel_id=1, source_target_pairs={{0,2},{1,3},{2,0},{3,1},{4,6},{5,7},{6,4},{7,5},{8,10},{9,11},{10,... | collective-permute-start | bytes 688136 | tf_op jit(solution)/shard_map/ppermute | solution.py:273
  59.6 26.6 %collective-permute-start.21 = (bf16[64,1792]{1,0:T(8,128)(2,1)S(1)}, bf16[64,1792]{1,0:T(8,128)(2,1)S(1)}, u32[]{:S(2)}, u32[]{:S(2)}) collective-permute-start(bf16[64,1792]{1,0:T(8,128)(2,1)S(1)} %constant_dynamic-update-slice_fusion.4.refs_8_), channel_id=1, source_target_pairs={{0,1},{1,0},{2,3},{3,2},{4,5},{5,4},{6,7},{7,6},{8,9},{9,8},{10,11... | collective-permute-start | bytes 688136 | tf_op jit(solution)/shard_map/ppermute | solution.py:273

commit v2 on v1

v2 whole, which is shorter than its diff:
```python
import jax
import jax.numpy as jnp
from jax import lax
from jax.experimental import pallas as pl
from jax.experimental.pallas import tpu as pltpu
from jax.sharding import PartitionSpec as P

ROUNDS = 2
NORM_EPS = 1e-06
VMEM_LIMIT = 24 * 2**20

bf16 = jnp.bfloat16
f32 = jnp.float32


def on_chip(body, outs, args, fetched=(), after=(), scratch=(), flops=0, moved=0):
    whole = pl.BlockSpec(memory_space=pltpu.VMEM)
    there = pl.BlockSpec(memory_space=pltpu.HBM)
    anywhere = pl.BlockSpec(memory_space=pl.ANY)
    first, last = len(fetched), len(fetched) + len(after)

    def run(*refs):
        body(*refs[:first], *refs[last:])

    return pl.pallas_call(
        run,
        out_shape=outs,
        in_specs=[there] * first + [anywhere] * len(after) + [whole] * len(args),
        out_specs=jax.tree.map(lambda _: whole, outs),
        scratch_shapes=scratch,
        compiler_params=pltpu.CompilerParams(vmem_limit_bytes=VMEM_LIMIT),
        cost_estimate=pl.CostEstimate(flops=flops, bytes_accessed=moved, transcendentals=0),
    )(*[pltpu.with_memory_space_constraint(value, pltpu.HBM) for value in fetched], *after, *args)


def fetch(copies, sems):
    started = [
        pltpu.make_async_copy(source, target, sems.at[index])
        for index, (source, target) in enumerate(copies)
    ]
    for copy in started:
        copy.start()
    return started


def dot(left, right, left_dim, right_dim):
    return lax.dot_general(
        left, right, (((left_dim,), (right_dim,)), ((), ())), preferred_element_type=f32
    )


def split_rows(value, refs, rows):
    for index, ref in enumerate(refs):
        ref[...] = value[index * rows : (index + 1) * rows].astype(ref.dtype)


def join_rows(refs):
    if len(refs) == 1:
        return refs[0][...]
    return jnp.concatenate([ref[...] for ref in refs], axis=0)


def column(row):
    count = row.shape[1]
    down = lax.broadcasted_iota(jnp.int32, (count, count), 0)
    along = lax.broadcasted_iota(jnp.int32, (count, count), 1)
    return jnp.sum(jnp.where(down == along, row, jnp.zeros_like(row)), axis=1, keepdims=True)


def one_hot(target, rows):
    down = lax.broadcasted_iota(jnp.int32, (rows, target.shape[1]), 0)
    return jnp.where(target == down, 1.0, 0.0).astype(bf16)


def target_of(expert, slot, capacity):
    mine = lax.axis_index("expert")
    return (expert ^ mine) * capacity + slot


def dispatch_rows(grad, gate, target, rows):
    scaled = (grad.astype(f32) * column(gate)).astype(bf16)
    return dot(one_hot(target, rows), scaled, 1, 0)


def stored_rows(stored_ref, round_index, senders, capacity):
    mine = lax.axis_index("expert")
    if capacity % 16 == 0:
        return jnp.concatenate(
            [
                stored_ref[
                    0,
                    round_index,
                    0,
                    pl.ds(pl.multiple_of((mine ^ step) * capacity, 16), capacity),
                    :,
                ]
                for step in range(senders)
            ],
            axis=0,
        ).astype(f32)
    rows = senders * capacity
    row = lax.broadcasted_iota(jnp.int32, (rows, rows), 0)
    column = lax.broadcasted_iota(jnp.int32, (rows, rows), 1)
    moved = ((row // capacity) ^ mine) * capacity + row % capacity
    order = jnp.where(moved == column, 1.0, 0.0).astype(bf16)
    return dot(order, stored_ref[0, round_index, 0], 1, 0)


def rides_along(block, rows, width, replicas):
    return (
        replicas == 4
        and block % 16 == 0
        and ROUNDS * rows == 128
        and block // 16 * 128 <= width
    )


def join(arrived, hidden, after):
    rows, width = sum(part.shape[0] for part in arrived), arrived[0].shape[1]

    def body(*refs):
        hidden_refs, refs = refs[:3], refs[3:]
        in_refs, (rows_ref, near_ref, far_ref) = refs[: len(arrived)], refs[len(arrived) :]
        value = join_rows(in_refs)
        rows_ref[...] = value
        near_ref[0:rows, :] = value
        near_ref[rows : rows + 16, :] = hidden_refs[0][...]
        far_ref[0:16, :] = hidden_refs[1][...]
        far_ref[16 : rows + 16, :] = value
        far_ref[rows + 16 : rows + 32, :] = hidden_refs[2][...]

    return on_chip(
        body,
        [
            jax.ShapeDtypeStruct((rows, width), bf16),
            jax.ShapeDtypeStruct((rows + 16, width), bf16),
            jax.ShapeDtypeStruct((rows + 32, width), bf16),
        ],
        (*hidden[1:], *arrived),
        after=after,
        moved=8 * rows * width,
    )


def unpack(ref, start, block, columns):
    return jnp.concatenate(
        [
            ref[start : start + 16, 128 * part : 128 * (part + 1)][:, columns]
            for part in range(block // 16)
        ],
        axis=0,
    )


def first_dispatch(
    grad, route_expert, route_slot, gates, saved_pre, capacity, senders, pieces, replicas
):
    tokens, width = grad.shape
    rows = senders * capacity
    hidden_width = saved_pre.shape[4] // 2
    block = hidden_width // replicas
    packed = rides_along(block, rows, width, replicas)
    hidden_shapes = (
        [jax.ShapeDtypeStruct((16, width), bf16)] * replicas
        if packed
        else [jax.ShapeDtypeStruct((hidden_width, ROUNDS * rows), bf16)]
    )

    def body(grad_in, expert_in, slot_in, gate_in, stored_in, *refs):
        table_ref, stored_ref, *refs = refs
        sent_refs, refs = refs[:pieces], refs[pieces:]
        hidden_refs, refs = refs[: len(hidden_shapes)], refs[len(hidden_shapes) :]
        grad_ref, expert_ref, slot_ref, gate_ref, held, sems = refs
        copies = fetch(
            (
                (expert_in, expert_ref),
                (slot_in, slot_ref),
                (gate_in, gate_ref),
                (grad_in, grad_ref),
                (stored_in, stored_ref),
            ),
            sems,
        )
        for copy in copies[:4]:
            copy.wait()
        target = target_of(expert_ref[0, 0], slot_ref[0, 0], capacity)
        sent = dispatch_rows(grad_ref[...], gate_ref[0, 0], target, rows)
        split_rows(sent, sent_refs, rows // pieces)
        later = target_of(expert_ref[0, 1], slot_ref[0, 1], capacity).astype(f32)
        table_ref[0:1, :] = later
        table_ref[1:2, :] = gate_ref[0, 1]
        copies[4].wait()
        for round_index in range(ROUNDS):
            stored = stored_rows(stored_ref, round_index, senders, capacity)
            gate_pre, up_value = stored[:, :hidden_width], stored[:, hidden_width:]
            hidden = (gate_pre * up_value) / (1.0 + jnp.exp(-gate_pre))
            held[:, round_index * rows : (round_index + 1) * rows] = hidden.T.astype(bf16)
        if not packed:
            hidden_refs[0][...] = held[...]
            return
        mine = lax.axis_index("edp")
        for step, ref in enumerate(hidden_refs):
            ref[...] = jnp.zeros_like(ref)
            for part in range(block // 16):
                start = pl.multiple_of((mine ^ step) * block + 16 * part, 16)
                ref[:, 128 * part : 128 * (part + 1)] = held[pl.ds(start, 16), :]

    table, stored, *made = on_chip(
        body,
        [jax.ShapeDtypeStruct((2, tokens), f32), jax.ShapeDtypeStruct(saved_pre.shape, bf16)]
        + [jax.ShapeDtypeStruct((rows // pieces, width), bf16)] * pieces
        + hidden_shapes,
        (),
        fetched=(grad, route_expert, route_slot, gates, saved_pre),
        scratch=[
            pltpu.VMEM(grad.shape, bf16),
            pltpu.VMEM(route_expert.shape, jnp.int32),
            pltpu.VMEM(route_slot.shape, jnp.int32),
            pltpu.VMEM(gates.shape, f32),
            pltpu.VMEM((hidden_width, ROUNDS * rows), bf16),
            pltpu.SemaphoreType.DMA((5,)),
        ],
        moved=3 * tokens * width * 2,
    )
    sent, hidden = made[:pieces], made[pieces:]
    if not packed:
        mine = lax.axis_index("edp")
        hidden = [
            lax.dynamic_slice_in_dim(hidden[0], (mine ^ step) * block, block, 0)
            for step in range(replicas)
        ]
    return table, sent, stored, hidden


def prepare(w_gate_up, w_down, after):
    def body(up_in, down_in, up_ref, down_ref, sems):
        for copy in fetch(((down_in, down_ref), (up_in, up_ref)), sems):
            copy.wait()

    return on_chip(
        body,
        [
            jax.ShapeDtypeStruct(w_gate_up.shape, bf16),
            jax.ShapeDtypeStruct(w_down.shape, bf16),
        ],
        (),
        fetched=(w_gate_up, w_down),
        after=after,
        scratch=[pltpu.SemaphoreType.DMA((2,))],
        moved=2 * (w_gate_up.size + w_down.size),
    )


def expert_rows(
    pieces_in, saved_pre, w_gate_up, w_down, round_index, senders, capacity, pieces, after=()
):
    rows = senders * capacity
    hidden_width, width = w_down.shape

    def body(stored_ref, up_ref, down_ref, *refs):
        in_refs, out_refs = refs[: len(pieces_in)], refs[len(pieces_in) :]
        routed = join_rows(in_refs)
        hidden_grad = dot(routed, down_ref[...], 1, 1)
        stored = stored_rows(stored_ref, round_index, senders, capacity)
        gate_pre, up_value = stored[:, :hidden_width], stored[:, hidden_width:]
        gate = 1.0 / (1.0 + jnp.exp(-gate_pre))
        act_grad = jnp.concatenate(
            [
                hidden_grad * up_value * gate * (1.0 + gate_pre * (1.0 - gate)),
                hidden_grad * gate_pre * gate,
            ],
            axis=1,
        ).astype(bf16)
        split_rows(dot(act_grad, up_ref[...], 1, 1), out_refs, rows // pieces)

    return on_chip(
        body,
        [jax.ShapeDtypeStruct((rows // pieces, width), bf16)] * pieces,
        (saved_pre, w_gate_up, w_down, *pieces_in),
        after=after,
        flops=6 * rows * hidden_width * width,
        moved=6 * hidden_width * width,
    )


def norm_backward(grad_out, branch, saved, gain):
    normed_in = saved.astype(f32)
    inverse = lax.rsqrt(jnp.mean(normed_in * normed_in, axis=1, keepdims=True) + NORM_EPS)
    scaled_in = normed_in * inverse
    norm_grad = branch * gain
    result = grad_out.astype(f32) + inverse * (
        norm_grad - scaled_in * jnp.mean(norm_grad * scaled_in, axis=1, keepdims=True)
    )
    return result.astype(bf16)


def first_combine(
    returned, grad, tail, saved_input, gain, route_expert, route_slot, table, capacity, senders, after=()
):
    tokens, width = grad.shape
    rows = senders * capacity
    pieces = len(returned)

    def body(grad_ref, tail_ref, saved_ref, gain_ref, expert_ref, slot_ref, table_ref, *refs):
        in_refs, (result_ref, *out_refs) = refs[:pieces], refs[pieces:]
        target = target_of(expert_ref[0, 0], slot_ref[0, 0], capacity)
        branch = dot(one_hot(target, rows), join_rows(in_refs), 0, 0)
        result = norm_backward(grad_ref[...], branch, saved_ref[0, 0], gain_ref[...])
        result_ref[...] = result
        first = lax.axis_index("pipe") == 0
        passed = jnp.where(first, tail_ref[...].astype(f32), result.astype(f32))
        later = table_ref[0:1, :].astype(jnp.int32)
        split_rows(
            dispatch_rows(passed, table_ref[1:2, :], later, rows), out_refs, rows // pieces
        )

    result, *sent = on_chip(
        body,
        [jax.ShapeDtypeStruct((tokens, width), bf16)]
        + [jax.ShapeDtypeStruct((rows // pieces, width), bf16)] * pieces,
        (grad, tail, saved_input, gain, route_expert, route_slot, table, *returned),
        after=after,
        moved=8 * tokens * width * 2,
    )
    return result, sent


def second_combine(
    returned, first_out, passed, tail, saved_input, gain, route_expert, route_slot, capacity, senders, after=()
):
    tokens, width = first_out.shape
    rows = senders * capacity
    pieces = len(returned)

    def body(first_ref, passed_ref, tail_ref, saved_ref, gain_ref, expert_ref, slot_ref, *refs):
        in_refs, (out_ref,) = refs[:pieces], refs[pieces:]
        out_ref[0, 0] = first_ref[...]
        target = target_of(expert_ref[0, 1], slot_ref[0, 1], capacity)
        branch = dot(one_hot(target, rows), join_rows(in_refs), 0, 0)
        last = lax.axis_index("pipe") == lax.axis_size("pipe") - 1
        grad = jnp.where(last, tail_ref[...].astype(f32), passed_ref[...].astype(f32))
        out_ref[0, 1] = norm_backward(grad, branch, saved_ref[0, 1], gain_ref[...])

    return on_chip(
        body,
        [jax.ShapeDtypeStruct((1, ROUNDS, tokens, width), bf16)],
        (first_out, passed, tail, saved_input, gain, route_expert, route_slot, *returned),
        after=after,
        moved=8 * tokens * width * 2,
    )[0]


def weight_grad(left, right, round_index, rows, block, scale=None, earlier=None):
    lefts, rights = [array for array, _ in left], [array for array, _ in right]
    width = rights[0].shape[1]
    arrays = []
    for array in lefts + rights:
        if not any(array is other for other in arrays):
            arrays.append(array)
    place = [next(i for i, other in enumerate(arrays) if other is a) for a in lefts + rights]

    def body(*refs):
        columns = slice(round_index * rows, (round_index + 1) * rows)
        left_value = jnp.concatenate(
            [
                refs[where][:, columns]
                if start is None
                else unpack(refs[where], start, block, columns)
                for where, (_, start) in zip(place, left)
            ],
            axis=1,
        )
        right_value = jnp.concatenate(
            [
                refs[where][start : start + rows, :]
                for where, (_, start) in zip(place[len(left) :], right)
            ],
            axis=0,
        )
        total = dot(left_value, right_value, 1, 0)
        if earlier is not None:
            total = (refs[len(arrays)][0, 0] + total) / scale
        refs[-1][0, 0] = total

    return on_chip(
        body,
        [jax.ShapeDtypeStruct((1, 1, block, width), f32)],
        tuple(arrays) + (() if earlier is None else (earlier,)),
        flops=2 * len(left) * rows * block * width,
        moved=8 * block * width,
    )[0]


def steps_over(axis, values):
    count = lax.axis_size(axis)
    return [values[0]] + [
        lax.ppermute(values[step], axis, [(source, source ^ step) for source in range(count)])
        for step in range(1, count)
    ]


def step_over(value, step):
    count = lax.axis_size("edp")
    return lax.ppermute(value, "edp", [(source, source ^ step) for source in range(count)])


def behind(values):
    sections, count = lax.axis_size("pipe"), lax.axis_size("expert")
    return [
        lax.ppermute(
            value,
            ("pipe", "expert"),
            [
                (section * count + source, (section - 1) % sections * count + (source ^ step))
                for section in range(sections)
                for source in range(count)
            ],
        )
        for step, value in enumerate(values)
    ]


def local(
    head_grads,
    tail_grad,
    saved_input,
    norm_gain,
    route_expert,
    route_slot,
    gates,
    saved_pre,
    w_gate_up,
    w_down,
):
    senders = lax.axis_size("expert")
    replicas = lax.axis_size("edp")
    sections = lax.axis_size("pipe")
    rows = saved_pre.shape[3]
    capacity = rows // senders
    width = w_down.shape[3]
    hidden_width = w_down.shape[2]
    pieces = senders if capacity % 16 == 0 else 1
    grad = head_grads[0]
    up, down = w_gate_up[0, 0], w_down[0, 0]

    def apart(parts):
        if pieces == senders:
            return parts
        return [parts[0][k * capacity : (k + 1) * capacity] for k in range(senders)]

    def together(parts):
        return parts if pieces == senders else [jnp.concatenate(parts, axis=0)]

    def whole(parts):
        return parts[0] if len(parts) == 1 else jnp.concatenate(parts, axis=0)

    def over_experts(parts):
        return together(steps_over("expert", apart(parts)))

    route_expert, route_slot, gates = (
        jnp.transpose(value, (0, 1, 3, 2)) for value in (route_expert, route_slot, gates)
    )
    table, sent, stored, hidden = first_dispatch(
        grad,
        route_expert,
        route_slot,
        gates,
        saved_pre,
        capacity,
        senders,
        pieces,
        replicas,
    )
    up, down = prepare(up, down, after=(table,))
    table = lax.ppermute(
        table, "pipe", [(source, (source + 1) % sections) for source in range(sections)]
    )
    arrived = over_experts(sent)
    block = hidden_width // replicas
    if rides_along(block, rows, width, replicas):
        joined, near_load, far_load = join(arrived, hidden, after=(up, down, table))
        far = step_over(far_load, 2)
        near = step_over(near_load, 1)
        last = step_over(far[16:], 1)
        left = [(hidden[0], 0), (near, rows), (far, 0), (last, rows)]
        right = [(joined, 0), (near, 0), (far, 16), (last, 0)]
        arrived = [joined]
        early, late = (near,), (last,)
    else:
        first_rows = [whole(arrived)] * replicas
        left = [(value, None) for value in steps_over("edp", hidden)]
        right = [(value, 0) for value in steps_over("edp", first_rows)]
        early = late = ()
    returned = over_experts(
        expert_rows(arrived, stored, up, down, 0, senders, capacity, pieces)
    )
    first_out, sent = first_combine(
        returned,
        grad,
        tail_grad,
        saved_input,
        norm_gain,
        route_expert,
        route_slot,
        table,
        capacity,
        senders,
        after=early,
    )
    arrived = together(behind(apart(sent)))
    passed = lax.ppermute(
        first_out, "pipe", [(source, (source - 1) % sections) for source in range(sections)]
    )
    joined = whole(arrived)
    if replicas == 4:
        far = step_over(joined, 2)
        near = step_over(joined, 1)
        second_right = [joined, near, far, step_over(far, 1)]
    else:
        second_right = steps_over("edp", [joined] * replicas)
    first_share = weight_grad(left, right, 0, rows, block)
    returned = over_experts(
        expert_rows(
            arrived, stored, up, down, 1, senders, capacity, pieces, after=late
        )
    )
    input_out = second_combine(
        returned,
        first_out,
        passed,
        tail_grad,
        saved_input,
        norm_gain,
        route_expert,
        route_slot,
        capacity,
        senders,
        after=(first_share,),
    )
    grad_shard = weight_grad(
        left,
        [(value, 0) for value in second_right],
        1,
        rows,
        block,
        scale=float(replicas * ROUNDS),
        earlier=first_share,
    )
    return (input_out, grad_shard)


def solution(mesh):
    return jax.shard_map(
        local,
        mesh=mesh,
        in_specs=(
            P("pipe", ("expert", "edp"), None),
            P(("expert", "edp"), None),
            P("pipe", None, ("expert", "edp"), None),
            P("pipe", None),
            P("pipe", None, ("expert", "edp"), None),
            P("pipe", None, ("expert", "edp"), None),
            P("pipe", None, ("expert", "edp"), None),
            P("pipe", None, "expert", "edp", None),
            P("pipe", "expert", None, None),
            P("pipe", "expert", None, None),
        ),
        out_specs=(P("pipe", None, ("expert", "edp"), None), P("pipe", "expert", "edp", None)),
        check_vma=False,
    )
```

time: 88.1 us -> 67.2 us (0.76)
  waiting for transfers between devices: 41.3 us -> 31 us
  local copies, waits for them, and re-layouts: 9.44 us -> 0.07 us
  starting transfers between devices: 27.1 us -> 21.5 us
  Pallas kernels: 9.2 us -> 13.7 us
    ppermute x18 -> x9, waiting for transfers between devices: 28.9 us -> 6.59 us  [steps_over(): lax.ppermute(values[step], axis, [(source, source ^ step) for source in r...]
    ppermute x0 -> x6, waiting for transfers between devices: none -> 21 us  [step_over(): lax.ppermute(value, 'edp', [(source, source ^ step) for source in range(c...]
    ppermute x18 -> x9, starting transfers between devices: 22.2 us -> 7.05 us  [steps_over(): lax.ppermute(values[step], axis, [(source, source ^ step) for source in r...]
    unnamed x33 -> x15, local copies, waits for them, and re-layouts: 9.43 us -> 0.04 us
    ppermute x4, waiting for transfers between devices: 12.4 us -> 3.42 us  [behind(): lax.ppermute(value, ('pipe', 'expert'), [(section * count + source, (sect...]
    ppermute x0 -> x6, starting transfers between devices: none -> 6.75 us  [step_over(): lax.ppermute(value, 'edp', [(source, source ^ step) for source in range(c...]
    pallas_call x7 -> x9, Pallas kernels: 9.2 us -> 13.7 us  [on_chip(): pl.pallas_call(run, out_shape=outs, in_specs=[there] * first + [anywhere]...]
    ppermute x4, starting transfers between devices: 2.19 us -> 4.46 us  [behind(): lax.ppermute(value, ('pipe', 'expert'), [(section * count + source, (sect...]
  transfers between devices with their start and end apart: 24 -> 21, of which waited for: 11 -> 11; matrix products, arithmetic and copies ran while one was open for 3% -> 0% of each run, Pallas kernels for 8% -> 15%
where the time goes in v2:
time: 67.2 us; the launch traced here: 67.1 us
  waiting for transfers between devices  31 us (46%)
  starting transfers between devices  21.5 us (32%)
  Pallas kernels  13.7 us (20%)
  between operations  0.82 us (1%)
    ppermute x6, waiting for transfers between devices, step_over(): lax.ppermute(value, 'edp', [(source, source ^ step) for source in range(c...  21 us
    pallas_call x9, Pallas kernels, on_chip(): pl.pallas_call(run, out_shape=outs, in_specs=[there] * first + [anywhere]...  13.7 us
    ppermute x9, starting transfers between devices, steps_over(): lax.ppermute(values[step], axis, [(source, source ^ step) for source in r...  7.05 us
    ppermute x6, starting transfers between devices, step_over(): lax.ppermute(value, 'edp', [(source, source ^ step) for source in range(c...  6.75 us
    ppermute x9, waiting for transfers between devices, steps_over(): lax.ppermute(values[step], axis, [(source, source ^ step) for source in r...  6.59 us
    ppermute x4, starting transfers between devices, behind(): lax.ppermute(value, ('pipe', 'expert'), [(section * count + source, (sect...  4.46 us
    ppermute x4, waiting for transfers between devices, behind(): lax.ppermute(value, ('pipe', 'expert'), [(section * count + source, (sect...  3.42 us
    ppermute x1, starting transfers between devices, local(): lax.ppermute(table, 'pipe', [(source, (source + 1) % sections) for source...  1.7 us
  transfers between devices with their start and end apart: 21, of which 11 were waited for; matrix products, arithmetic and copies ran while one was open for 0% of the time, Pallas kernels for 15%

profile of v2, /device:TPU:0, one launch (start us, length us, event | category | flops | bytes accessed | tf_op | source)
XLA Modules:
  0.0 67.1 jit_solution(11588980911427329925)
XLA Ops:
  0.6 1.8 %shard_map.113 = (f32[2,64]{1,0:T(2,128)S(1)}, bf16[1,2,1,64,1408]{4,3,2,1,0:T(8,128)(2,1)S(1)}, bf16[16,1792]{1,0:T(8,128)(2,1)S(1)}, bf16[16,1792]{1,0:T(8,128...) custom-call(bf16[64,1792]{1,0:T(8,128)(2,1)} %bitcast.12, ...), custom_call_target="tpu_custom_call" | custom-call | bytes 688128 | tf_op jit(solution)/shard_map/pallas_call | solution.py:25
  2.4 0.5 collective-permute-start.1
  2.9 2.6 %collective-permute-start.2 = (bf16[16,1792]{1,0:T(8,128)(2,1)S(1)}, bf16[16,1792]{1,0:T(8,128)(2,1)S(1)}, u32[]{:S(2)}, u32[]{:S(2)}) collective-permute-start(bf16[16,1792]{1,0:T(8,128)(2,1)S(1)} %get-tuple-element.39), channel_id=1, source_target_pairs={{0,8},{4,12},{8,0},{12,4},{1,9},{5,13},{9,1},{13,5},{2,10},{6,14},... | collective-permute-start | bytes 172040 | tf_op jit(solution)/shard_map/ppermute | solution.py:397
  5.5 0.1 collective-permute-start.3
  5.6 1.7 %collective-permute-start = (f32[2,64]{1,0:T(2,128)S(1)}, f32[2,64]{1,0:T(2,128)S(1)}, u32[]{:S(2)}, u32[]{:S(2)}) collective-permute-start(f32[2,64]{1,0:T(2,128)S(1)} %get-tuple-element.31.refs_2_), channel_id=1, source_target_pairs={{0,16},{16,0},{1,17},{17,1},{2,18},{18,2},{3,19},{19,3},{4,20},{20... | collective-permute-start | bytes 1544 | tf_op jit(solution)/shard_map/ppermute | solution.py:475
  7.3 3.2 %shard_map.114 = (bf16[1792,1408]{1,0:T(8,128)(2,1)S(1)}, bf16[704,1792]{1,0:T(8,128)(2,1)S(1)}) custom-call(bf16[1792,1408]{1,0:T(8,128)(2,1)} %bitcast.20, bf16[704,1792]{1,0:T(8,128)(2,1)} %bitcast.21, f32[2,64]{1,0:T(2,128)S(1)} %get-tuple-element.31.refs_2_), custom_call_target="tpu_custom_call" | custom-call | bytes 7569408 | tf_op jit(solution)/shard_map/pallas_call | solution.py:25
  10.5 0.0 collective-permute-done.refs_2_.refs_7_
  10.5 0.0 collective-permute-done.1.refs_7_
  10.6 0.0 collective-permute-done.2.refs_8_
  10.6 0.0 collective-permute-done.3.refs_9_
  10.6 0.1 shard_map.115
  10.6 1.6 %collective-permute-start.4 = (bf16[80,1792]{1,0:T(8,128)(2,1)S(1)}, bf16[80,1792]{1,0:T(8,128)(2,1)S(1)}, u32[]{:S(2)}, u32[]{:S(2)}) collective-permute-start(bf16[80,1792]{1,0:T(8,128)(2,1)S(1)} %get-tuple-element.41), channel_id=1, source_target_pairs={{0,1},{1,0},{2,3},{3,2},{4,5},{5,4},{6,7},{7,6},{8,9},{9,8},{10,11... | collective-permute-start | bytes 860168 | tf_op jit(solution)/shard_map/ppermute | solution.py:404
  12.3 0.0 copy-start
  12.3 0.0 copy-start.1
  12.3 0.0 copy-start.2
  12.3 0.0 copy-start.3
  12.3 0.0 copy-start.4
  12.3 0.0 copy-start.5
  12.3 2.5 %shard_map.117 = (bf16[16,1792]{1,0:T(8,128)(2,1)S(1)}, bf16[16,1792]{1,0:T(8,128)(2,1)S(1)}, bf16[16,1792]{1,0:T(8,128)(2,1)S(1)}, bf16[16,1792]{1,0:T(8,128)(2,1)S(1)}) custom-call(bf16[1,2,1,64,1408]{4,3,2,1,0:T(8,128)(2,1)S(1)} %get-tuple-element.44.refs_0_.refs_1_, bf16[1792,1408]{1,0:T(8,128)(2,1)S(1)} %get-tuple-element.32.refs_0_.refs_1_.refs_2_, ...), custom_call_target="tpu_custom_call" | custom-call | flops 484442112 | bytes 7569408 | tf_op jit(solution)/shard_map/pallas_call | solution.py:25
  14.8 0.1 collective-permute-start.7
  14.9 1.6 %collective-permute-start.8 = (bf16[16,1792]{1,0:T(8,128)(2,1)S(1)}, bf16[16,1792]{1,0:T(8,128)(2,1)S(1)}, u32[]{:S(2)}, u32[]{:S(2)}) collective-permute-start(bf16[16,1792]{1,0:T(8,128)(2,1)S(1)} %get-tuple-element.47), channel_id=1, source_target_pairs={{0,8},{4,12},{8,0},{12,4},{1,9},{5,13},{9,1},{13,5},{2,10},{6,14},... | collective-permute-start | bytes 172040 | tf_op jit(solution)/shard_map/ppermute | solution.py:397
  16.5 0.3 collective-permute-start.9
  16.8 0.0 collective-permute-done.7.refs_9_
  16.8 2.5 %collective-permute-done.8.refs_10_ = bf16[16,1792]{1,0:T(8,128)(2,1)S(1)} collective-permute-done((bf16[16,1792]{1,0:T(8,128)(2,1)S(1)}, bf16[16,1792]{1,0:T(8,128)(2,1)S(1)}, u32[]{:S(2)}, u32[]{:S(2)}) %collective-permute-start.8) | collective-permute-done | bytes 57376 | tf_op jit(solution)/shard_map/ppermute | solution.py:397
  19.2 1.1 %collective-permute-done.9.refs_11_ = bf16[16,1792]{1,0:T(8,128)(2,1)S(1)} collective-permute-done((bf16[16,1792]{1,0:T(8,128)(2,1)S(1)}, bf16[16,1792]{1,0:T(8,128)(2,1)S(1)}, u32[]{:S(2)}, u32[]{:S(2)}) %collective-permute-start.9) | collective-permute-done | bytes 57376 | tf_op jit(solution)/shard_map/ppermute | solution.py:397
  20.4 0.0 collective-permute-done.4.refs_1_.refs_0_
  20.4 0.0 copy-done
  20.4 0.0 copy-done.1
  20.4 0.0 copy-done.2
  20.4 0.0 copy-done.3
  20.4 0.0 copy-done.4
  20.4 0.0 copy-done.5
  20.4 0.7 %shard_map.118 = (bf16[64,1792]{1,0:T(8,128)(2,1)S(1)}, bf16[16,1792]{1,0:T(8,128)(2,1)S(1)}, bf16[16,1792]{1,0:T(8,128)(2,1)S(1)}, bf16[16,1792]{1,0:T(8,128)(2,1)S(1)}, bf16[16,1792]{1,0:T(8,128)(2,1)S(1)}) custom-call(bf16[80,1792]{1,0:T(8,128)(2,1)S(1)} %collective-permute-done.4.refs_1_.refs_0_, bf16[64,1792]{1,0:T(8,128)(2,1)S(1)} %bitcast.13, ...), custom_call_target="tpu_custom_call" | custom-call | bytes 1835008 | tf_op jit(solution)/shard_map/pallas_call | solution.py:25
  21.1 0.6 collective-permute-start.11
  21.7 2.6 %collective-permute-start.5 = (bf16[96,1792]{1,0:T(8,128)(2,1)S(1)}, bf16[96,1792]{1,0:T(8,128)(2,1)S(1)}, u32[]{:S(2)}, u32[]{:S(2)}) collective-permute-start(bf16[96,1792]{1,0:T(8,128)(2,1)S(1)} %get-tuple-element.42), channel_id=1, source_target_pairs={{0,2},{1,3},{2,0},{3,1},{4,6},{5,7},{6,4},{7,5},{8,10},{9,11},{10,... | collective-permute-start | bytes 1032200 | tf_op jit(solution)/shard_map/ppermute | solution.py:404
  24.3 0.7 %collective-permute-start.12 = (bf16[16,1792]{1,0:T(8,128)(2,1)S(1)}, bf16[16,1792]{1,0:T(8,128)(2,1)S(1)}, u32[]{:S(2)}, u32[]{:S(2)}) collective-permute-start(bf16[16,1792]{1,0:T(8,128)(2,1)S(1)} %get-tuple-element.51), channel_id=1, source_target_pairs={{0,20},{4,16},{8,28},{12,24},{16,4},{20,0},{24,12},{28,8},{1,21},{... | collective-permute-start | bytes 172040 | tf_op jit(solution)/shard_map/ppermute | solution.py:410
  25.0 1.4 %collective-permute-start.13 = (bf16[16,1792]{1,0:T(8,128)(2,1)S(1)}, bf16[16,1792]{1,0:T(8,128)(2,1)S(1)}, u32[]{:S(2)}, u32[]{:S(2)}) collective-permute-start(bf16[16,1792]{1,0:T(8,128)(2,1)S(1)} %get-tuple-element.52), channel_id=1, source_target_pairs={{0,24},{4,28},{8,16},{12,20},{16,8},{20,12},{24,0},{28,4},{1,25},{... | collective-permute-start | bytes 172040 | tf_op jit(solution)/shard_map/ppermute | solution.py:410
  26.4 1.8 %collective-permute-start.14 = (bf16[16,1792]{1,0:T(8,128)(2,1)S(1)}, bf16[16,1792]{1,0:T(8,128)(2,1)S(1)}, u32[]{:S(2)}, u32[]{:S(2)}) collective-permute-start(bf16[16,1792]{1,0:T(8,128)(2,1)S(1)} %get-tuple-element.53), channel_id=1, source_target_pairs={{0,28},{4,24},{8,20},{12,16},{16,12},{20,8},{24,4},{28,0},{1,29},{... | collective-permute-start | bytes 172040 | tf_op jit(solution)/shard_map/ppermute | solution.py:410
  28.2 0.0 collective-permute-done.11.refs_4_
  28.2 0.3 collective-permute-done.12.refs_5_
  28.5 2.2 %collective-permute-done.13.refs_6_ = bf16[16,1792]{1,0:T(8,128)(2,1)S(1)} collective-permute-done((bf16[16,1792]{1,0:T(8,128)(2,1)S(1)}, bf16[16,1792]{1,0:T(8,128)(2,1)S(1)}, u32[]{:S(2)}, u32[]{:S(2)}) %collective-permute-start.13) | collective-permute-done | bytes 57376 | tf_op jit(solution)/shard_map/ppermute | solution.py:410
  30.7 0.9 %collective-permute-done.14.refs_7_ = bf16[16,1792]{1,0:T(8,128)(2,1)S(1)} collective-permute-done((bf16[16,1792]{1,0:T(8,128)(2,1)S(1)}, bf16[16,1792]{1,0:T(8,128)(2,1)S(1)}, u32[]{:S(2)}, u32[]{:S(2)}) %collective-permute-start.14) | collective-permute-done | bytes 57376 | tf_op jit(solution)/shard_map/ppermute | solution.py:410
  31.6 0.4 collective-permute-start.19
  32.0 12.9 %collective-permute-done.5.refs_2_ = bf16[96,1792]{1,0:T(8,128)(2,1)S(1)} collective-permute-done((bf16[96,1792]{1,0:T(8,128)(2,1)S(1)}, bf16[96,1792]{1,0:T(8,128)(2,1)S(1)}, u32[]{:S(2)}, u32[]{:S(2)}) %collective-permute-start.5) | collective-permute-done | bytes 344096 | tf_op jit(solution)/shard_map/ppermute | solution.py:404
  45.0 0.7 collective-permute-start.6
  45.6 1.5 %collective-permute-start.10 = (bf16[64,1792]{1,0:T(8,128)(2,1)S(1)}, bf16[64,1792]{1,0:T(8,128)(2,1)S(1)}, u32[]{:S(2)}, u32[]{:S(2)}) collective-permute-start(bf16[64,1792]{1,0:T(8,128)(2,1)S(1)} %get-tuple-element.49.refs_1_), channel_id=1, source_target_pairs={{0,16},{16,0},{1,17},{17,1},{2,18},{18,2},{3,19},{19,3},{4,20},{20... | collective-permute-start | bytes 688136 | tf_op jit(solution)/shard_map/ppermute | solution.py:511
  47.1 1.4 %collective-permute-start.18 = (bf16[64,1792]{1,0:T(8,128)(2,1)S(1)}, bf16[64,1792]{1,0:T(8,128)(2,1)S(1)}, u32[]{:S(2)}, u32[]{:S(2)}) collective-permute-start(bf16[64,1792]{1,0:T(8,128)(2,1)S(1)} %constant_dynamic-update-slice_fusion.refs_4_), channel_id=1, source_target_pairs={{0,1},{1,0},{2,3},{3,2},{4,5},{5,4},{6,7},{7,6},{8,9},{9,8},{10,11... | collective-permute-start | bytes 688136 | tf_op jit(solution)/shard_map/ppermute | solution.py:404
  48.6 1.2 %collective-permute-done.19.refs_6_ = bf16[64,1792]{1,0:T(8,128)(2,1)S(1)} collective-permute-done((bf16[64,1792]{1,0:T(8,128)(2,1)S(1)}, bf16[64,1792]{1,0:T(8,128)(2,1)S(1)}, u32[]{:S(2)}, u32[]{:S(2)}) %collective-permute-start.19) | collective-permute-done | bytes 229408 | tf_op jit(solution)/shard_map/ppermute | solution.py:404
  49.8 0.0 collective-permute-start.20
  49.8 6.1 %collective-permute-done.6.refs_3_.refs_0_ = bf16[80,1792]{1,0:T(8,128)(2,1)S(1)} collective-permute-done((bf16[80,1792]{1,0:T(8,128)(2,1)S(1)}, bf16[80,1792]{1,0:T(8,128)(2,1)S(1)}, u32[]{:S(2)}, u32[]{:S(2)}) %collective-permute-start.6) | collective-permute-done | bytes 286752 | tf_op jit(solution)/shard_map/ppermute | solution.py:404
  55.9 2.5 %shard_map.119 = (bf16[16,1792]{1,0:T(8,128)(2,1)S(1)}, bf16[16,1792]{1,0:T(8,128)(2,1)S(1)}, bf16[16,1792]{1,0:T(8,128)(2,1)S(1)}, bf16[16,1792]{1,0:T(8,128)(2,1)S(1)}) custom-call(bf16[80,1792]{1,0:T(8,128)(2,1)S(1)} %collective-permute-done.6.refs_3_.refs_0_, bf16[1,2,1,64,1408]{4,3,2,1,0:T(8,128)(2,1)S(1)} %get-tuple-element.44.refs_0_.refs_1_, ...), custom_call_target="tpu_custom_call" | custom-call | flops 484442112 | bytes 7569408 | tf_op jit(solution)/shard_map/pallas_call | solution.py:25
  58.4 0.1 collective-permute-start.15
  58.5 1.3 %collective-permute-start.16 = (bf16[16,1792]{1,0:T(8,128)(2,1)S(1)}, bf16[16,1792]{1,0:T(8,128)(2,1)S(1)}, u32[]{:S(2)}, u32[]{:S(2)}) collective-permute-start(bf16[16,1792]{1,0:T(8,128)(2,1)S(1)} %get-tuple-element.56), channel_id=1, source_target_pairs={{0,8},{4,12},{8,0},{12,4},{1,9},{5,13},{9,1},{13,5},{2,10},{6,14},... | collective-permute-start | bytes 172040 | tf_op jit(solution)/shard_map/ppermute | solution.py:397
  59.8 0.0 collective-permute-done.10.refs_2_
  59.8 0.5 collective-permute-start.17
  60.4 0.4 shard_map.116.refs_0_.refs_8_
  60.7 0.0 collective-permute-done.15.refs_9_
  60.7 2.1 %collective-permute-done.16.refs_10_ = bf16[16,1792]{1,0:T(8,128)(2,1)S(1)} collective-permute-done((bf16[16,1792]{1,0:T(8,128)(2,1)S(1)}, bf16[16,1792]{1,0:T(8,128)(2,1)S(1)}, u32[]{:S(2)}, u32[]{:S(2)}) %collective-permute-start.16) | collective-permute-done | bytes 57376 | tf_op jit(solution)/shard_map/ppermute | solution.py:397
  62.8 0.9 %collective-permute-done.17.refs_11_ = bf16[16,1792]{1,0:T(8,128)(2,1)S(1)} collective-permute-done((bf16[16,1792]{1,0:T(8,128)(2,1)S(1)}, bf16[16,1792]{1,0:T(8,128)(2,1)S(1)}, u32[]{:S(2)}, u32[]{:S(2)}) %collective-permute-start.17) | collective-permute-done | bytes 57376 | tf_op jit(solution)/shard_map/ppermute | solution.py:397
  63.7 1.2 %shard_map.120 = bf16[1,2,64,1792]{3,2,1,0:T(8,128)(2,1)} custom-call(f32[1,1,176,1792]{3,2,1,0:T(8,128)S(1)} %shard_map.116.refs_0_.refs_8_, bf16[64,1792]{1,0:T(8,128)(2,1)S(1)} %get-tuple-element.49.refs_1_, bf16[64,1792]{1,0:T(8,128)(2,1)S(1)} %collective-permute-done.10.refs_2_, bf16[64,1792]{1,0:T(8,128)(2,1)S(1)} %copy-done.1, ...), custom_call_target="tpu_custom_call" | custom-call | bytes 1835008 | tf_op jit(solution)/shard_map/pallas_call | solution.py:25
  64.9 0.0 collective-permute-done.18.refs_5_
  64.9 0.7 %collective-permute-done.20.refs_7_ = bf16[64,1792]{1,0:T(8,128)(2,1)S(1)} collective-permute-done((bf16[64,1792]{1,0:T(8,128)(2,1)S(1)}, bf16[64,1792]{1,0:T(8,128)(2,1)S(1)}, u32[]{:S(2)}, u32[]{:S(2)}) %collective-permute-start.20) | collective-permute-done | bytes 229408 | tf_op jit(solution)/shard_map/ppermute | solution.py:404
  65.6 1.4 %shard_map.121 = f32[1,1,176,1792]{3,2,1,0:T(8,128)} custom-call(bf16[16,1792]{1,0:T(8,128)(2,1)S(1)} %get-tuple-element.30.refs_0_, bf16[80,1792]{1,0:T(8,128)(2,1)S(1)} %collective-permute-done.4.refs_1_.refs_0_, bf16[96,1792]{1,0:T(8,128)(2,1)S(1)} %collective-permute-done.5.refs_2_, bf16[80,1792]{1,0:T(8,128)(2,1)S(1)} %collective-permute-done.6.refs_3_.refs_0_, ...), custom_call_target="tpu_custom_call" | custom-call | flops 161480704 | bytes 2523136 | tf_op jit(solution)/shard_map/pallas_call | solution.py:25
  (5 shorter events, 0.0 us)
Async XLA Ops:
  2.4 8.1 %collective-permute-start.1 = (bf16[16,1792]{1,0:T(8,128)(2,1)S(1)}, bf16[16,1792]{1,0:T(8,128)(2,1)S(1)}, u32[]{:S(2)}, u32[]{:S(2)}) collective-permute-start(bf16[16,1792]{1,0:T(8,128)(2,1)S(1)} %get-tuple-element.38), channel_id=1, source_target_pairs={{0,4},{4,0},{8,12},{12,8},{1,5},{5,1},{9,13},{13,9},{2,6},{6,2},{1... | collective-permute-start | bytes 172040 | tf_op jit(solution)/shard_map/ppermute | solution.py:397
  2.9 7.6 %collective-permute-start.2 = (bf16[16,1792]{1,0:T(8,128)(2,1)S(1)}, bf16[16,1792]{1,0:T(8,128)(2,1)S(1)}, u32[]{:S(2)}, u32[]{:S(2)}) collective-permute-start(bf16[16,1792]{1,0:T(8,128)(2,1)S(1)} %get-tuple-element.39), channel_id=1, source_target_pairs={{0,8},{4,12},{8,0},{12,4},{1,9},{5,13},{9,1},{13,5},{2,10},{6,14},... | collective-permute-start | bytes 172040 | tf_op jit(solution)/shard_map/ppermute | solution.py:397
  5.5 5.0 %collective-permute-start.3 = (bf16[16,1792]{1,0:T(8,128)(2,1)S(1)}, bf16[16,1792]{1,0:T(8,128)(2,1)S(1)}, u32[]{:S(2)}, u32[]{:S(2)}) collective-permute-start(bf16[16,1792]{1,0:T(8,128)(2,1)S(1)} %get-tuple-element.40), channel_id=1, source_target_pairs={{0,12},{4,8},{8,4},{12,0},{1,13},{5,9},{9,5},{13,1},{2,14},{6,10},... | collective-permute-start | bytes 172040 | tf_op jit(solution)/shard_map/ppermute | solution.py:397
  5.6 4.9 %collective-permute-start = (f32[2,64]{1,0:T(2,128)S(1)}, f32[2,64]{1,0:T(2,128)S(1)}, u32[]{:S(2)}, u32[]{:S(2)}) collective-permute-start(f32[2,64]{1,0:T(2,128)S(1)} %get-tuple-element.31.refs_2_), channel_id=1, source_target_pairs={{0,16},{16,0},{1,17},{17,1},{2,18},{18,2},{3,19},{19,3},{4,20},{20... | collective-permute-start | bytes 1544 | tf_op jit(solution)/shard_map/ppermute | solution.py:475
  10.6 9.7 %collective-permute-start.4 = (bf16[80,1792]{1,0:T(8,128)(2,1)S(1)}, bf16[80,1792]{1,0:T(8,128)(2,1)S(1)}, u32[]{:S(2)}, u32[]{:S(2)}) collective-permute-start(bf16[80,1792]{1,0:T(8,128)(2,1)S(1)} %get-tuple-element.41), channel_id=1, source_target_pairs={{0,1},{1,0},{2,3},{3,2},{4,5},{5,4},{6,7},{7,6},{8,9},{9,8},{10,11... | collective-permute-start | bytes 860168 | tf_op jit(solution)/shard_map/ppermute | solution.py:404
  12.3 8.1 %copy-start = (bf16[1,2,64,1792]{3,2,1,0:T(8,128)(2,1)S(1)}, bf16[1,2,64,1792]{3,2,1,0:T(8,128)(2,1)}, u32[]{:S(2)}) copy-start(bf16[1,2,64,1792]{3,2,1,0:T(8,128)(2,1)} %refs_4_.5) | copy-start | bytes 1376260
  12.3 8.1 %copy-start.1 = (bf16[64,1792]{1,0:T(8,128)(2,1)S(1)}, bf16[64,1792]{1,0:T(8,128)(2,1)}, u32[]{:S(2)}) copy-start(bf16[64,1792]{1,0:T(8,128)(2,1)} %refs_3_.3) | copy-start | bytes 688132
  12.3 8.1 %copy-start.2 = (bf16[1,64,1792]{2,1,0:T(8,128)(2,1)S(1)}, bf16[1,64,1792]{2,1,0:T(8,128)(2,1)}, u32[]{:S(2)}) copy-start(bf16[1,64,1792]{2,1,0:T(8,128)(2,1)} %param.10) | copy-start | bytes 688132
  12.3 8.1 %copy-start.3 = (f32[1,1792]{1,0:T(1,128)S(1)}, f32[1,1792]{1,0:T(1,128)}, u32[]{:S(2)}) copy-start(f32[1,1792]{1,0:T(1,128)} %refs_5_.1) | copy-start | bytes 21508
  12.3 8.1 %copy-start.4 = (s32[1,2,64,1]{2,3,1,0:T(1,128)S(1)}, s32[1,2,64,1]{2,3,1,0:T(1,128)}, u32[]{:S(2)}) copy-start(s32[1,2,64,1]{2,3,1,0:T(1,128)} %param.14) | copy-start | bytes 1540
  12.3 8.1 %copy-start.5 = (s32[1,2,64,1]{2,3,1,0:T(1,128)S(1)}, s32[1,2,64,1]{2,3,1,0:T(1,128)}, u32[]{:S(2)}) copy-start(s32[1,2,64,1]{2,3,1,0:T(1,128)} %param.15) | copy-start | bytes 1540
  14.8 1.9 %collective-permute-start.7 = (bf16[16,1792]{1,0:T(8,128)(2,1)S(1)}, bf16[16,1792]{1,0:T(8,128)(2,1)S(1)}, u32[]{:S(2)}, u32[]{:S(2)}) collective-permute-start(bf16[16,1792]{1,0:T(8,128)(2,1)S(1)} %get-tuple-element.46), channel_id=1, source_target_pairs={{0,4},{4,0},{8,12},{12,8},{1,5},{5,1},{9,13},{13,9},{2,6},{6,2},{1... | collective-permute-start | bytes 172040 | tf_op jit(solution)/shard_map/ppermute | solution.py:397
  14.9 4.3 %collective-permute-start.8 = (bf16[16,1792]{1,0:T(8,128)(2,1)S(1)}, bf16[16,1792]{1,0:T(8,128)(2,1)S(1)}, u32[]{:S(2)}, u32[]{:S(2)}) collective-permute-start(bf16[16,1792]{1,0:T(8,128)(2,1)S(1)} %get-tuple-element.47), channel_id=1, source_target_pairs={{0,8},{4,12},{8,0},{12,4},{1,9},{5,13},{9,1},{13,5},{2,10},{6,14},... | collective-permute-start | bytes 172040 | tf_op jit(solution)/shard_map/ppermute | solution.py:397
  16.5 3.9 %collective-permute-start.9 = (bf16[16,1792]{1,0:T(8,128)(2,1)S(1)}, bf16[16,1792]{1,0:T(8,128)(2,1)S(1)}, u32[]{:S(2)}, u32[]{:S(2)}) collective-permute-start(bf16[16,1792]{1,0:T(8,128)(2,1)S(1)} %get-tuple-element.48), channel_id=1, source_target_pairs={{0,12},{4,8},{8,4},{12,0},{1,13},{5,9},{9,5},{13,1},{2,14},{6,10},... | collective-permute-start | bytes 172040 | tf_op jit(solution)/shard_map/ppermute | solution.py:397
  21.1 7.1 %collective-permute-start.11 = (bf16[16,1792]{1,0:T(8,128)(2,1)S(1)}, bf16[16,1792]{1,0:T(8,128)(2,1)S(1)}, u32[]{:S(2)}, u32[]{:S(2)}) collective-permute-start(bf16[16,1792]{1,0:T(8,128)(2,1)S(1)} %get-tuple-element.50), channel_id=1, source_target_pairs={{0,16},{4,20},{8,24},{12,28},{16,0},{20,4},{24,8},{28,12},{1,17},{... | collective-permute-start | bytes 172040 | tf_op jit(solution)/shard_map/ppermute | solution.py:410
  21.7 23.2 %collective-permute-start.5 = (bf16[96,1792]{1,0:T(8,128)(2,1)S(1)}, bf16[96,1792]{1,0:T(8,128)(2,1)S(1)}, u32[]{:S(2)}, u32[]{:S(2)}) collective-permute-start(bf16[96,1792]{1,0:T(8,128)(2,1)S(1)} %get-tuple-element.42), channel_id=1, source_target_pairs={{0,2},{1,3},{2,0},{3,1},{4,6},{5,7},{6,4},{7,5},{8,10},{9,11},{10,... | collective-permute-start | bytes 1032200 | tf_op jit(solution)/shard_map/ppermute | solution.py:404
  24.3 4.2 %collective-permute-start.12 = (bf16[16,1792]{1,0:T(8,128)(2,1)S(1)}, bf16[16,1792]{1,0:T(8,128)(2,1)S(1)}, u32[]{:S(2)}, u32[]{:S(2)}) collective-permute-start(bf16[16,1792]{1,0:T(8,128)(2,1)S(1)} %get-tuple-element.51), channel_id=1, source_target_pairs={{0,20},{4,16},{8,28},{12,24},{16,4},{20,0},{24,12},{28,8},{1,21},{... | collective-permute-start | bytes 172040 | tf_op jit(solution)/shard_map/ppermute | solution.py:410
  25.0 5.7 %collective-permute-start.13 = (bf16[16,1792]{1,0:T(8,128)(2,1)S(1)}, bf16[16,1792]{1,0:T(8,128)(2,1)S(1)}, u32[]{:S(2)}, u32[]{:S(2)}) collective-permute-start(bf16[16,1792]{1,0:T(8,128)(2,1)S(1)} %get-tuple-element.52), channel_id=1, source_target_pairs={{0,24},{4,28},{8,16},{12,20},{16,8},{20,12},{24,0},{28,4},{1,25},{... | collective-permute-start | bytes 172040 | tf_op jit(solution)/shard_map/ppermute | solution.py:410
  26.4 5.2 %collective-permute-start.14 = (bf16[16,1792]{1,0:T(8,128)(2,1)S(1)}, bf16[16,1792]{1,0:T(8,128)(2,1)S(1)}, u32[]{:S(2)}, u32[]{:S(2)}) collective-permute-start(bf16[16,1792]{1,0:T(8,128)(2,1)S(1)} %get-tuple-element.53), channel_id=1, source_target_pairs={{0,28},{4,24},{8,20},{12,16},{16,12},{20,8},{24,4},{28,0},{1,29},{... | collective-permute-start | bytes 172040 | tf_op jit(solution)/shard_map/ppermute | solution.py:410
  31.6 18.2 %collective-permute-start.19 = (bf16[64,1792]{1,0:T(8,128)(2,1)S(1)}, bf16[64,1792]{1,0:T(8,128)(2,1)S(1)}, u32[]{:S(2)}, u32[]{:S(2)}) collective-permute-start(bf16[64,1792]{1,0:T(8,128)(2,1)S(1)} %constant_dynamic-update-slice_fusion.refs_4_), channel_id=1, source_target_pairs={{0,2},{1,3},{2,0},{3,1},{4,6},{5,7},{6,4},{7,5},{8,10},{9,11},{10,... | collective-permute-start | bytes 688136 | tf_op jit(solution)/shard_map/ppermute | solution.py:404
  45.0 10.9 %collective-permute-start.6 = (bf16[80,1792]{1,0:T(8,128)(2,1)S(1)}, bf16[80,1792]{1,0:T(8,128)(2,1)S(1)}, u32[]{:S(2)}, u32[]{:S(2)}) collective-permute-start(bf16[80,1792]{1,0:T(8,128)(2,1)S(1)} %slice.4), channel_id=1, source_target_pairs={{0,1},{1,0},{2,3},{3,2},{4,5},{5,4},{6,7},{7,6},{8,9},{9,8},{10,11... | collective-permute-start | bytes 860168 | tf_op jit(solution)/shard_map/ppermute | solution.py:404
  45.6 14.2 %collective-permute-start.10 = (bf16[64,1792]{1,0:T(8,128)(2,1)S(1)}, bf16[64,1792]{1,0:T(8,128)(2,1)S(1)}, u32[]{:S(2)}, u32[]{:S(2)}) collective-permute-start(bf16[64,1792]{1,0:T(8,128)(2,1)S(1)} %get-tuple-element.49.refs_1_), channel_id=1, source_target_pairs={{0,16},{16,0},{1,17},{17,1},{2,18},{18,2},{3,19},{19,3},{4,20},{20... | collective-permute-start | bytes 688136 | tf_op jit(solution)/shard_map/ppermute | solution.py:511
  47.1 17.8 %collective-permute-start.18 = (bf16[64,1792]{1,0:T(8,128)(2,1)S(1)}, bf16[64,1792]{1,0:T(8,128)(2,1)S(1)}, u32[]{:S(2)}, u32[]{:S(2)}) collective-permute-start(bf16[64,1792]{1,0:T(8,128)(2,1)S(1)} %constant_dynamic-update-slice_fusion.refs_4_), channel_id=1, source_target_pairs={{0,1},{1,0},{2,3},{3,2},{4,5},{5,4},{6,7},{7,6},{8,9},{9,8},{10,11... | collective-permute-start | bytes 688136 | tf_op jit(solution)/shard_map/ppermute | solution.py:404
  49.8 15.9 %collective-permute-start.20 = (bf16[64,1792]{1,0:T(8,128)(2,1)S(1)}, bf16[64,1792]{1,0:T(8,128)(2,1)S(1)}, u32[]{:S(2)}, u32[]{:S(2)}) collective-permute-start(bf16[64,1792]{1,0:T(8,128)(2,1)S(1)} %collective-permute-done.19.refs_6_), channel_id=1, source_target_pairs={{0,1},{1,0},{2,3},{3,2},{4,5},{5,4},{6,7},{7,6},{8,9},{9,8},{10,11... | collective-permute-start | bytes 688136 | tf_op jit(solution)/shard_map/ppermute | solution.py:404
  58.4 2.3 %collective-permute-start.15 = (bf16[16,1792]{1,0:T(8,128)(2,1)S(1)}, bf16[16,1792]{1,0:T(8,128)(2,1)S(1)}, u32[]{:S(2)}, u32[]{:S(2)}) collective-permute-start(bf16[16,1792]{1,0:T(8,128)(2,1)S(1)} %get-tuple-element.55), channel_id=1, source_target_pairs={{0,4},{4,0},{8,12},{12,8},{1,5},{5,1},{9,13},{13,9},{2,6},{6,2},{1... | collective-permute-start | bytes 172040 | tf_op jit(solution)/shard_map/ppermute | solution.py:397
  58.5 4.3 %collective-permute-start.16 = (bf16[16,1792]{1,0:T(8,128)(2,1)S(1)}, bf16[16,1792]{1,0:T(8,128)(2,1)S(1)}, u32[]{:S(2)}, u32[]{:S(2)}) collective-permute-start(bf16[16,1792]{1,0:T(8,128)(2,1)S(1)} %get-tuple-element.56), channel_id=1, source_target_pairs={{0,8},{4,12},{8,0},{12,4},{1,9},{5,13},{9,1},{13,5},{2,10},{6,14},... | collective-permute-start | bytes 172040 | tf_op jit(solution)/shard_map/ppermute | solution.py:397
  59.8 3.9 %collective-permute-start.17 = (bf16[16,1792]{1,0:T(8,128)(2,1)S(1)}, bf16[16,1792]{1,0:T(8,128)(2,1)S(1)}, u32[]{:S(2)}, u32[]{:S(2)}) collective-permute-start(bf16[16,1792]{1,0:T(8,128)(2,1)S(1)} %get-tuple-element.57), channel_id=1, source_target_pairs={{0,12},{4,8},{8,4},{12,0},{1,13},{5,9},{9,5},{13,1},{2,14},{6,10},... | collective-permute-start | bytes 172040 | tf_op jit(solution)/shard_map/ppermute | solution.py:397

commit v3 on v2

v3 whole, which is shorter than its diff:
```python
import jax
import jax.numpy as jnp
from jax import lax
from jax.experimental import pallas as pl
from jax.experimental.pallas import tpu as pltpu
from jax.sharding import PartitionSpec as P

ROUNDS = 2
NORM_EPS = 1e-06
VMEM_LIMIT = 24 * 2**20

bf16 = jnp.bfloat16
f32 = jnp.float32


def on_chip(body, outs, args, fetched=(), after=(), scratch=(), flops=0, moved=0):
    whole = pl.BlockSpec(memory_space=pltpu.VMEM)
    there = pl.BlockSpec(memory_space=pltpu.HBM)
    anywhere = pl.BlockSpec(memory_space=pl.ANY)
    first, last = len(fetched), len(fetched) + len(after)

    def run(*refs):
        body(*refs[:first], *refs[last:])

    return pl.pallas_call(
        run,
        out_shape=outs,
        in_specs=[there] * first + [anywhere] * len(after) + [whole] * len(args),
        out_specs=jax.tree.map(lambda _: whole, outs),
        scratch_shapes=scratch,
        compiler_params=pltpu.CompilerParams(vmem_limit_bytes=VMEM_LIMIT),
        cost_estimate=pl.CostEstimate(flops=flops, bytes_accessed=moved, transcendentals=0),
    )(*[pltpu.with_memory_space_constraint(value, pltpu.HBM) for value in fetched], *after, *args)


def fetch(copies, sems):
    started = [
        pltpu.make_async_copy(source, target, sems.at[index])
        for index, (source, target) in enumerate(copies)
    ]
    for copy in started:
        copy.start()
    return started


def dot(left, right, left_dim, right_dim):
    return lax.dot_general(
        left, right, (((left_dim,), (right_dim,)), ((), ())), preferred_element_type=f32
    )


def even(senders, capacity):
    return senders == 4 and capacity % 16 == 0


def sent_shapes(senders, capacity, width, pairs=False):
    if not even(senders, capacity):
        return [jax.ShapeDtypeStruct((senders * capacity, width), bf16)]
    if pairs:
        return [jax.ShapeDtypeStruct((2 * capacity, width), bf16)] * 2
    return [jax.ShapeDtypeStruct((capacity, width), bf16)] * senders


def spread(value, refs, capacity):
    count = len(refs)
    if count == 1:
        refs[0][...] = value.astype(bf16)
        return
    for first, ref in enumerate(refs):
        for place in range(4 // count):
            start = (first + count * place) * capacity
            ref[place * capacity : (place + 1) * capacity] = value[
                start : start + capacity
            ].astype(bf16)


def collect(refs, capacity):
    if len(refs) == 1:
        return refs[0][...]
    if len(refs) == 3:
        return jnp.concatenate(
            [refs[0][0:capacity], refs[1][0:capacity], refs[2][...]], axis=0
        )
    return jnp.concatenate([ref[...] for ref in refs], axis=0)


def pair_up(stays, came, capacity, places, after=()):
    def body(stays_ref, came_ref, *refs):
        for place, ref in zip(places, refs):
            part = slice(place * capacity, (place + 1) * capacity)
            ref[0:capacity] = stays_ref[part]
            ref[capacity : 2 * capacity] = came_ref[part]

    return on_chip(
        body,
        [jax.ShapeDtypeStruct(stays.shape, bf16)] * len(places),
        (stays, came),
        after=after,
        moved=8 * capacity * stays.shape[1],
    )


def column(row):
    count = row.shape[1]
    down = lax.broadcasted_iota(jnp.int32, (count, count), 0)
    along = lax.broadcasted_iota(jnp.int32, (count, count), 1)
    return jnp.sum(jnp.where(down == along, row, jnp.zeros_like(row)), axis=1, keepdims=True)


def one_hot(target, rows):
    down = lax.broadcasted_iota(jnp.int32, (rows, target.shape[1]), 0)
    return jnp.where(target == down, 1.0, 0.0).astype(bf16)


def target_of(expert, slot, capacity):
    mine = lax.axis_index("expert")
    return (expert ^ mine) * capacity + slot


def dispatch_rows(grad, gate, target, rows):
    scaled = (grad.astype(f32) * column(gate)).astype(bf16)
    return dot(one_hot(target, rows), scaled, 1, 0)


def stored_rows(stored_ref, round_index, senders, capacity):
    mine = lax.axis_index("expert")
    if capacity % 16 == 0:
        return jnp.concatenate(
            [
                stored_ref[
                    0,
                    round_index,
                    0,
                    pl.ds(pl.multiple_of((mine ^ step) * capacity, 16), capacity),
                    :,
                ]
                for step in range(senders)
            ],
            axis=0,
        ).astype(f32)
    rows = senders * capacity
    row = lax.broadcasted_iota(jnp.int32, (rows, rows), 0)
    column = lax.broadcasted_iota(jnp.int32, (rows, rows), 1)
    moved = ((row // capacity) ^ mine) * capacity + row % capacity
    order = jnp.where(moved == column, 1.0, 0.0).astype(bf16)
    return dot(order, stored_ref[0, round_index, 0], 1, 0)


def rides_along(block, rows, width, replicas):
    return (
        replicas == 4
        and block % 16 == 0
        and ROUNDS * rows == 128
        and block // 16 * 128 <= width
    )


def join(arrived, hidden, capacity, rows, after=()):
    width = arrived[0].shape[1]

    def body(*refs):
        hidden_refs, refs = refs[: len(hidden)], refs[len(hidden) :]
        in_refs, (rows_ref, *load_refs) = refs[: len(arrived)], refs[len(arrived) :]
        value = collect(in_refs, capacity)
        rows_ref[...] = value
        for hidden_ref, load_ref in zip(hidden_refs, load_refs):
            load_ref[0:rows, :] = value
            load_ref[rows : rows + 16, :] = hidden_ref[...]

    joined, *loads = on_chip(
        body,
        [jax.ShapeDtypeStruct((rows, width), bf16)]
        + [jax.ShapeDtypeStruct((rows + 16, width), bf16)] * len(hidden),
        (*hidden, *arrived),
        after=after,
        moved=8 * rows * width,
    )
    return joined, loads


def first_rows_of(value, rows, after):
    def body(value_ref, out_ref):
        out_ref[...] = value_ref[0:rows, :]

    return on_chip(
        body,
        [jax.ShapeDtypeStruct((rows, value.shape[1]), value.dtype)],
        (value,),
        after=after,
        moved=4 * rows * value.shape[1],
    )[0]


def unpack(ref, start, block, columns):
    return jnp.concatenate(
        [
            ref[start : start + 16, 128 * part : 128 * (part + 1)][:, columns]
            for part in range(block // 16)
        ],
        axis=0,
    )


def first_dispatch(
    grad, route_expert, route_slot, gates, saved_pre, w_down, capacity, senders, replicas
):
    tokens, width = grad.shape
    rows = senders * capacity
    hidden_width = saved_pre.shape[4] // 2
    block = hidden_width // replicas
    packed = rides_along(block, rows, width, replicas)
    sent_to = sent_shapes(senders, capacity, width)
    hidden_shapes = (
        [jax.ShapeDtypeStruct((16, width), bf16)] * 4
        if packed
        else [jax.ShapeDtypeStruct((hidden_width, ROUNDS * rows), bf16)]
    )

    def body(grad_in, expert_in, slot_in, gate_in, stored_in, down_in, *refs):
        table_ref, stored_ref, down_ref, *refs = refs
        sent_refs, refs = refs[: len(sent_to)], refs[len(sent_to) :]
        hidden_refs, refs = refs[: len(hidden_shapes)], refs[len(hidden_shapes) :]
        grad_ref, expert_ref, slot_ref, gate_ref, held, sems = refs
        copies = fetch(
            (
                (expert_in, expert_ref),
                (slot_in, slot_ref),
                (gate_in, gate_ref),
                (grad_in, grad_ref),
                (stored_in, stored_ref),
                (down_in, down_ref),
            ),
            sems,
        )
        for copy in copies[:4]:
            copy.wait()
        target = target_of(expert_ref[0, 0], slot_ref[0, 0], capacity)
        sent = dispatch_rows(grad_ref[...], gate_ref[0, 0], target, rows)
        spread(sent, sent_refs, capacity)
        later = target_of(expert_ref[0, 1], slot_ref[0, 1], capacity).astype(f32)
        table_ref[0:1, :] = later
        table_ref[1:2, :] = gate_ref[0, 1]
        copies[4].wait()
        for round_index in range(ROUNDS):
            stored = stored_rows(stored_ref, round_index, senders, capacity)
            gate_pre, up_value = stored[:, :hidden_width], stored[:, hidden_width:]
            hidden = (gate_pre * up_value) / (1.0 + jnp.exp(-gate_pre))
            held[:, round_index * rows : (round_index + 1) * rows] = hidden.T.astype(bf16)
        if not packed:
            hidden_refs[0][...] = held[...]
            copies[5].wait()
            return
        mine = lax.axis_index("edp")
        for step, ref in enumerate(hidden_refs):
            ref[...] = jnp.zeros_like(ref)
            for part in range(block // 16):
                start = pl.multiple_of((mine ^ step) * block + 16 * part, 16)
                ref[:, 128 * part : 128 * (part + 1)] = held[pl.ds(start, 16), :]
        copies[5].wait()

    table, stored, down, *made = on_chip(
        body,
        [
            jax.ShapeDtypeStruct((2, tokens), f32),
            jax.ShapeDtypeStruct(saved_pre.shape, bf16),
            jax.ShapeDtypeStruct(w_down.shape, bf16),
        ]
        + sent_to
        + hidden_shapes,
        (),
        fetched=(grad, route_expert, route_slot, gates, saved_pre, w_down),
        scratch=[
            pltpu.VMEM(grad.shape, bf16),
            pltpu.VMEM(route_expert.shape, jnp.int32),
            pltpu.VMEM(route_slot.shape, jnp.int32),
            pltpu.VMEM(gates.shape, f32),
            pltpu.VMEM((hidden_width, ROUNDS * rows), bf16),
            pltpu.SemaphoreType.DMA((6,)),
        ],
        moved=3 * tokens * width * 2,
    )
    sent, hidden = made[: len(sent_to)], made[len(sent_to) :]
    if not packed:
        mine = lax.axis_index("edp")
        hidden = [
            lax.dynamic_slice_in_dim(hidden[0], (mine ^ step) * block, block, 0)
            for step in range(replicas)
        ]
    return table, sent, stored, down, hidden


def bring(value, after):
    def body(value_in, value_ref, sems):
        for copy in fetch(((value_in, value_ref),), sems):
            copy.wait()

    return on_chip(
        body,
        [jax.ShapeDtypeStruct(value.shape, value.dtype)],
        (),
        fetched=(value,),
        after=after,
        scratch=[pltpu.SemaphoreType.DMA((1,))],
        moved=2 * value.size,
    )[0]


def expert_rows(
    pieces_in, saved_pre, w_gate_up, w_down, round_index, senders, capacity, pairs=False, after=()
):
    rows = senders * capacity
    hidden_width, width = w_down.shape

    def body(stored_ref, up_ref, down_ref, *refs):
        in_refs, out_refs = refs[: len(pieces_in)], refs[len(pieces_in) :]
        routed = collect(in_refs, capacity)
        hidden_grad = dot(routed, down_ref[...], 1, 1)
        stored = stored_rows(stored_ref, round_index, senders, capacity)
        gate_pre, up_value = stored[:, :hidden_width], stored[:, hidden_width:]
        gate = 1.0 / (1.0 + jnp.exp(-gate_pre))
        act_grad = jnp.concatenate(
            [
                hidden_grad * up_value * gate * (1.0 + gate_pre * (1.0 - gate)),
                hidden_grad * gate_pre * gate,
            ],
            axis=1,
        ).astype(bf16)
        spread(dot(act_grad, up_ref[...], 1, 1), out_refs, capacity)

    return on_chip(
        body,
        sent_shapes(senders, capacity, width, pairs),
        (saved_pre, w_gate_up, w_down, *pieces_in),
        after=after,
        flops=6 * rows * hidden_width * width,
        moved=6 * hidden_width * width,
    )


def norm_backward(grad_out, branch, saved, gain):
    normed_in = saved.astype(f32)
    inverse = lax.rsqrt(jnp.mean(normed_in * normed_in, axis=1, keepdims=True) + NORM_EPS)
    scaled_in = normed_in * inverse
    norm_grad = branch * gain
    result = grad_out.astype(f32) + inverse * (
        norm_grad - scaled_in * jnp.mean(norm_grad * scaled_in, axis=1, keepdims=True)
    )
    return result.astype(bf16)


def first_combine(
    returned, grad, tail, saved_input, gain, route_expert, route_slot, table, capacity, senders, after=()
):
    tokens, width = grad.shape
    rows = senders * capacity
    pieces = len(returned)

    def body(grad_ref, tail_ref, saved_ref, gain_ref, expert_ref, slot_ref, table_ref, *refs):
        in_refs, (result_ref, *out_refs) = refs[:pieces], refs[pieces:]
        target = target_of(expert_ref[0, 0], slot_ref[0, 0], capacity)
        branch = dot(one_hot(target, rows), collect(in_refs, capacity), 0, 0)
        result = norm_backward(grad_ref[...], branch, saved_ref[0, 0], gain_ref[...])
        result_ref[...] = result
        first = lax.axis_index("pipe") == 0
        passed = jnp.where(first, tail_ref[...].astype(f32), result.astype(f32))
        later = table_ref[0:1, :].astype(jnp.int32)
        spread(dispatch_rows(passed, table_ref[1:2, :], later, rows), out_refs, capacity)

    result, *sent = on_chip(
        body,
        [jax.ShapeDtypeStruct((tokens, width), bf16)]
        + sent_shapes(senders, capacity, width),
        (grad, tail, saved_input, gain, route_expert, route_slot, table, *returned),
        after=after,
        moved=8 * tokens * width * 2,
    )
    return result, sent


def second_combine(
    returned, first_out, passed, tail, saved_input, gain, route_expert, route_slot, capacity, senders, after=()
):
    tokens, width = first_out.shape
    rows = senders * capacity
    pieces = len(returned)

    def body(first_ref, passed_ref, tail_ref, saved_ref, gain_ref, expert_ref, slot_ref, *refs):
        in_refs, (out_ref, token_ref) = refs[:pieces], refs[pieces:]
        token_ref[...] = jnp.zeros_like(token_ref)
        out_ref[0, 0] = first_ref[...]
        target = target_of(expert_ref[0, 1], slot_ref[0, 1], capacity)
        branch = dot(one_hot(target, rows), collect(in_refs, capacity), 0, 0)
        last = lax.axis_index("pipe") == lax.axis_size("pipe") - 1
        grad = jnp.where(last, tail_ref[...].astype(f32), passed_ref[...].astype(f32))
        out_ref[0, 1] = norm_backward(grad, branch, saved_ref[0, 1], gain_ref[...])

    return on_chip(
        body,
        [
            jax.ShapeDtypeStruct((1, ROUNDS, tokens, width), bf16),
            jax.ShapeDtypeStruct((8, 128), f32),
        ],
        (first_out, passed, tail, saved_input, gain, route_expert, route_slot, *returned),
        after=after,
        moved=8 * tokens * width * 2,
    )


def weight_grad(terms, rows, block, scale=None, earlier=None, after=()):
    width = terms[0][3].shape[1]
    arrays = []
    for term in terms:
        for array in (term[0], term[3]):
            if not any(array is other for other in arrays):
                arrays.append(array)

    def place(array):
        return next(index for index, other in enumerate(arrays) if other is array)

    places = [(place(left), start, number, place(right)) for left, start, number, right in terms]

    def body(*refs):
        lefts, rights = [], []
        for left, start, number, right in places:
            columns = slice(number * rows, (number + 1) * rows)
            if start is None:
                lefts.append(refs[left][:, columns])
            else:
                lefts.append(unpack(refs[left], start, block, columns))
            rights.append(refs[right][0:rows, :])
        total = dot(jnp.concatenate(lefts, axis=1), jnp.concatenate(rights, axis=0), 1, 0)
        if earlier is not None:
            total = (refs[len(arrays)][0, 0] + total) / scale
        refs[-1][0, 0] = total

    return on_chip(
        body,
        [jax.ShapeDtypeStruct((1, 1, block, width), f32)],
        tuple(arrays) + (() if earlier is None else (earlier,)),
        after=after,
        flops=2 * len(terms) * rows * block * width,
        moved=8 * block * width,
    )[0]


def at_distance(value, axis, step):
    count = lax.axis_size(axis)
    return lax.ppermute(value, axis, [(source, source ^ step) for source in range(count)])


def steps_over(axis, values):
    return [values[0]] + [
        at_distance(value, axis, step) for step, value in enumerate(values) if step
    ]


def behind(values):
    sections, count = lax.axis_size("pipe"), lax.axis_size("expert")
    return [
        lax.ppermute(
            value,
            ("pipe", "expert"),
            [
                (section * count + source, (section - 1) % sections * count + (source ^ step))
                for section in range(sections)
                for source in range(count)
            ],
        )
        for step, value in values
    ]


def local(
    head_grads,
    tail_grad,
    saved_input,
    norm_gain,
    route_expert,
    route_slot,
    gates,
    saved_pre,
    w_gate_up,
    w_down,
):
    senders = lax.axis_size("expert")
    replicas = lax.axis_size("edp")
    sections = lax.axis_size("pipe")
    rows = saved_pre.shape[3]
    capacity = rows // senders
    width = w_down.shape[3]
    hidden_width = w_down.shape[2]
    grad = head_grads[0]
    up, down = w_gate_up[0, 0], w_down[0, 0]

    def apart(parts):
        if len(parts) == senders:
            return parts
        return [parts[0][k * capacity : (k + 1) * capacity] for k in range(senders)]

    def together(parts, like):
        return parts if len(like) == senders else [jnp.concatenate(parts, axis=0)]

    def over_experts(parts, after=()):
        if even(senders, capacity) and len(parts) == 2:
            stays, turns = parts
            came = at_distance(turns, "expert", 1)
            (load,) = pair_up(stays, came, capacity, (1,), after)
            return [stays, came, at_distance(load, "expert", 2)]
        return together(steps_over("expert", apart(parts)), parts)

    def back(parts):
        return together(behind(list(enumerate(apart(parts)))), parts)

    route_expert, route_slot, gates = (
        jnp.transpose(value, (0, 1, 3, 2)) for value in (route_expert, route_slot, gates)
    )
    table, sent, stored, down, hidden = first_dispatch(
        grad,
        route_expert,
        route_slot,
        gates,
        saved_pre,
        down,
        capacity,
        senders,
        replicas,
    )
    up = bring(up, after=(table,))
    table = lax.ppermute(
        table, "pipe", [(source, (source + 1) % sections) for source in range(sections)]
    )
    arrived = over_experts(sent)
    block = hidden_width // replicas
    if rides_along(block, rows, width, replicas):
        joined, (near_load,) = join(
            arrived, hidden[1:2], capacity, rows, after=(up, table)
        )
        far = at_distance(joined, "edp", 2)
        near = at_distance(near_load, "edp", 1)
        arrived = [joined]
        early = (near, far)
        arrived = [joined]
    else:
        left = steps_over("edp", hidden)
        right = steps_over("edp", arrived * replicas)
        early = ()
    sent = expert_rows(
        arrived, stored, up, down, 0, senders, capacity
    )
    returned = over_experts(sent)
    first_out, sent = first_combine(
        returned,
        grad,
        tail_grad,
        saved_input,
        norm_gain,
        route_expert,
        route_slot,
        table,
        capacity,
        senders,
        after=early,
    )
    if early:
        last = at_distance(first_rows_of(far, rows, (sent[0],)), "edp", 1)
    arrived = back(sent)
    passed = lax.ppermute(
        first_out, "pipe", [(source, (source - 1) % sections) for source in range(sections)]
    )
    if rides_along(block, rows, width, replicas):
        again, _ = join(arrived, (), capacity, rows)
        second = at_distance(again, "edp", 2)
        first = at_distance(again, "edp", 1)
        third = at_distance(second, "edp", 1)
        units = [at_distance(hidden[step], "edp", step) for step in (2, 3)]
        arrived, late, tail = [again], (last,), (first,)
        now = [(hidden[0], 0, 0, joined), (near, rows, 0, near), (units[0], 0, 0, far)]
        then = [
            (hidden[0], 0, 1, again),
            (near, rows, 1, first),
            (units[0], 0, 1, second),
            (units[1], 0, 1, third),
            (units[1], 0, 0, last),
        ]
    else:
        late = tail = ()
        again = steps_over("edp", arrived * replicas)
        now = [(units, None, 0, value) for units, value in zip(left, right)]
        then = [(units, None, 1, value) for units, value in zip(left, again)]
    first_share = weight_grad(now, rows, block)
    returned = over_experts(
        expert_rows(
            arrived, stored, up, down, 1, senders, capacity, pairs=True, after=late
        ),
        after=tail,
    )
    input_out, done = second_combine(
        returned,
        first_out,
        passed,
        tail_grad,
        saved_input,
        norm_gain,
        route_expert,
        route_slot,
        capacity,
        senders,
        after=(first_share,),
    )
    grad_shard = weight_grad(
        then, rows, block, scale=float(replicas * ROUNDS), earlier=first_share, after=(done,)
    )
    return (input_out, grad_shard)


def solution(mesh):
    return jax.shard_map(
        local,
        mesh=mesh,
        in_specs=(
            P("pipe", ("expert", "edp"), None),
            P(("expert", "edp"), None),
            P("pipe", None, ("expert", "edp"), None),
            P("pipe", None),
            P("pipe", None, ("expert", "edp"), None),
            P("pipe", None, ("expert", "edp"), None),
            P("pipe", None, ("expert", "edp"), None),
            P("pipe", None, "expert", "edp", None),
            P("pipe", "expert", None, None),
            P("pipe", "expert", None, None),
        ),
        out_specs=(P("pipe", None, ("expert", "edp"), None), P("pipe", "expert", "edp", None)),
        check_vma=False,
    )
```

time: 67.2 us -> 59.6 us (0.89)
  waiting for transfers between devices: 31 us -> 14.9 us
  starting transfers between devices: 21.5 us -> 30.3 us
    ppermute x15 -> x16, waiting for transfers between devices: 27.6 us -> 13.7 us  [at_distance(): lax.ppermute(value, axis, [(source, source ^ step) for source in range(co...]
    ppermute x15 -> x16, starting transfers between devices: 13.8 us -> 23.2 us  [at_distance(): lax.ppermute(value, axis, [(source, source ^ step) for source in range(co...]
    ppermute x4, waiting for transfers between devices: 3.42 us -> 1.2 us  [behind(): lax.ppermute(value, ('pipe', 'expert'), [(section * count + source, (sect...]
    pallas_call x9 -> x12, Pallas kernels: 13.7 us -> 13.4 us  [on_chip(): pl.pallas_call(run, out_shape=outs, in_specs=[there] * first + [anywhere]...]
  transfers between devices with their start and end apart: 21 -> 22, of which waited for: 11 -> 9; matrix products, arithmetic and copies ran while one was open for 0% -> 0% of each run, Pallas kernels for 15% -> 15%
where the time goes in v3:
time: 59.6 us; the launch traced here: 59.4 us
  starting transfers between devices  30.3 us (51%)
  waiting for transfers between devices  14.9 us (25%)
  Pallas kernels  13.4 us (22%)
  between operations  0.83 us (1%)
    ppermute x16, starting transfers between devices, at_distance(): lax.ppermute(value, axis, [(source, source ^ step) for source in range(co...  23.2 us
    ppermute x16, waiting for transfers between devices, at_distance(): lax.ppermute(value, axis, [(source, source ^ step) for source in range(co...  13.7 us
    pallas_call x12, Pallas kernels, on_chip(): pl.pallas_call(run, out_shape=outs, in_specs=[there] * first + [anywhere]...  13.4 us
    ppermute x4, starting transfers between devices, behind(): lax.ppermute(value, ('pipe', 'expert'), [(section * count + source, (sect...  4.46 us
    ppermute x1, starting transfers between devices, local(): lax.ppermute(table, 'pipe', [(source, (source + 1) % sections) for source...  1.7 us
    ppermute x4, waiting for transfers between devices, behind(): lax.ppermute(value, ('pipe', 'expert'), [(section * count + source, (sect...  1.2 us
  transfers between devices with their start and end apart: 22, of which 9 were waited for; matrix products, arithmetic and copies ran while one was open for 0% of the time, Pallas kernels for 15%

profile of v3, /device:TPU:0, one launch (start us, length us, event | category | flops | bytes accessed | tf_op | source)
XLA Modules:
  0.0 59.4 jit_solution(8536331255338243150)
XLA Ops:
  0.6 2.1 %shard_map.113 = (f32[2,64]{1,0:T(2,128)S(1)}, bf16[1,2,1,64,1408]{4,3,2,1,0:T(8,128)(2,1)S(1)}, bf16[704,1792]{1,0:T(8,128)(2,1)S(1)}, bf16[16,1792]{1,0:T(8,12...) custom-call(bf16[64,1792]{1,0:T(8,128)(2,1)} %bitcast.12, ...), custom_call_target="tpu_custom_call" | custom-call | bytes 688128 | tf_op jit(solution)/shard_map/pallas_call | solution.py:25
  2.7 0.5 collective-permute-start.1
  3.2 2.6 %collective-permute-start.2 = (bf16[16,1792]{1,0:T(8,128)(2,1)S(1)}, bf16[16,1792]{1,0:T(8,128)(2,1)S(1)}, u32[]{:S(2)}, u32[]{:S(2)}) collective-permute-start(bf16[16,1792]{1,0:T(8,128)(2,1)S(1)} %get-tuple-element.33), channel_id=1, source_target_pairs={{0,8},{4,12},{8,0},{12,4},{1,9},{5,13},{9,1},{13,5},{2,10},{6,14},... | collective-permute-start | bytes 172040 | tf_op jit(solution)/shard_map/ppermute | solution.py:448
  5.8 0.1 collective-permute-start.3
  5.9 1.7 %collective-permute-start = (f32[2,64]{1,0:T(2,128)S(1)}, f32[2,64]{1,0:T(2,128)S(1)}, u32[]{:S(2)}, u32[]{:S(2)}) collective-permute-start(f32[2,64]{1,0:T(2,128)S(1)} %get-tuple-element.29.refs_1_), channel_id=1, source_target_pairs={{0,16},{16,0},{1,17},{17,1},{2,18},{18,2},{3,19},{19,3},{4,20},{20... | collective-permute-start | bytes 1544 | tf_op jit(solution)/shard_map/ppermute | solution.py:529
  7.6 2.4 %shard_map.114.refs_0_.refs_1_.refs_2_ = bf16[1792,1408]{1,0:T(8,128)(2,1)S(1)} custom-call(bf16[1792,1408]{1,0:T(8,128)(2,1)} %bitcast.20, f32[2,64]{1,0:T(2,128)S(1)} %get-tuple-element.29.refs_1_), custom_call_target="tpu_custom_call" | custom-call | bytes 5046272 | tf_op jit(solution)/shard_map/pallas_call | solution.py:25
  10.0 0.0 collective-permute-done.refs_1_.refs_8_
  10.0 0.0 collective-permute-done.1.refs_4_
  10.0 0.0 collective-permute-done.2.refs_5_
  10.1 0.0 collective-permute-done.3.refs_6_
  10.1 1.6 %collective-permute-start.4 = (bf16[80,1792]{1,0:T(8,128)(2,1)S(1)}, bf16[80,1792]{1,0:T(8,128)(2,1)S(1)}, u32[]{:S(2)}, u32[]{:S(2)}) collective-permute-start(bf16[80,1792]{1,0:T(8,128)(2,1)S(1)} %get-tuple-element.36), channel_id=1, source_target_pairs={{0,1},{1,0},{2,3},{3,2},{4,5},{5,4},{6,7},{7,6},{8,9},{9,8},{10,11... | collective-permute-start | bytes 860168 | tf_op jit(solution)/shard_map/ppermute | solution.py:448
  11.8 2.6 %collective-permute-start.6 = (bf16[64,1792]{1,0:T(8,128)(2,1)S(1)}, bf16[64,1792]{1,0:T(8,128)(2,1)S(1)}, u32[]{:S(2)}, u32[]{:S(2)}) collective-permute-start(bf16[64,1792]{1,0:T(8,128)(2,1)S(1)} %get-tuple-element.35.refs_1_.refs_3_), channel_id=1, source_target_pairs={{0,2},{1,3},{2,0},{3,1},{4,6},{5,7},{6,4},{7,5},{8,10},{9,11},{10,... | collective-permute-start | bytes 688136 | tf_op jit(solution)/shard_map/ppermute | solution.py:448
  14.3 0.0 copy-start
  14.3 0.0 copy-start.1
  14.3 0.0 copy-start.2
  14.3 0.0 copy-start.3
  14.4 0.0 copy-start.4
  14.4 0.0 copy-start.5
  14.4 2.5 %shard_map.117 = (bf16[16,1792]{1,0:T(8,128)(2,1)S(1)}, bf16[16,1792]{1,0:T(8,128)(2,1)S(1)}, bf16[16,1792]{1,0:T(8,128)(2,1)S(1)}, bf16[16,1792]{1,0:T(8,128)(2,1)S(1)}) custom-call(bf16[1,2,1,64,1408]{4,3,2,1,0:T(8,128)(2,1)S(1)} %get-tuple-element.38.refs_0_.refs_1_, bf16[1792,1408]{1,0:T(8,128)(2,1)S(1)} %shard_map.114.refs_0_.refs_1_.refs_2_, ...), custom_call_target="tpu_custom_call" | custom-call | flops 484442112 | bytes 7569408 | tf_op jit(solution)/shard_map/pallas_call | solution.py:25
  16.9 0.1 collective-permute-start.7
  17.0 1.6 %collective-permute-start.8 = (bf16[16,1792]{1,0:T(8,128)(2,1)S(1)}, bf16[16,1792]{1,0:T(8,128)(2,1)S(1)}, u32[]{:S(2)}, u32[]{:S(2)}) collective-permute-start(bf16[16,1792]{1,0:T(8,128)(2,1)S(1)} %get-tuple-element.42), channel_id=1, source_target_pairs={{0,8},{4,12},{8,0},{12,4},{1,9},{5,13},{9,1},{13,5},{2,10},{6,14},... | collective-permute-start | bytes 172040 | tf_op jit(solution)/shard_map/ppermute | solution.py:448
  18.5 0.3 collective-permute-start.9
  18.8 0.0 collective-permute-done.7.refs_10_
  18.8 2.5 %collective-permute-done.8.refs_11_ = bf16[16,1792]{1,0:T(8,128)(2,1)S(1)} collective-permute-done((bf16[16,1792]{1,0:T(8,128)(2,1)S(1)}, bf16[16,1792]{1,0:T(8,128)(2,1)S(1)}, u32[]{:S(2)}, u32[]{:S(2)}) %collective-permute-start.8) | collective-permute-done | bytes 57376 | tf_op jit(solution)/shard_map/ppermute | solution.py:448
  21.3 1.1 %collective-permute-done.9.refs_12_ = bf16[16,1792]{1,0:T(8,128)(2,1)S(1)} collective-permute-done((bf16[16,1792]{1,0:T(8,128)(2,1)S(1)}, bf16[16,1792]{1,0:T(8,128)(2,1)S(1)}, u32[]{:S(2)}, u32[]{:S(2)}) %collective-permute-start.9) | collective-permute-done | bytes 57376 | tf_op jit(solution)/shard_map/ppermute | solution.py:448
  22.4 0.6 %collective-permute-done.6.refs_4_.refs_1_ = bf16[64,1792]{1,0:T(8,128)(2,1)S(1)} collective-permute-done((bf16[64,1792]{1,0:T(8,128)(2,1)S(1)}, bf16[64,1792]{1,0:T(8,128)(2,1)S(1)}, u32[]{:S(2)}, u32[]{:S(2)}) %collective-permute-start.6) | collective-permute-done | bytes 229408 | tf_op jit(solution)/shard_map/ppermute | solution.py:448
  23.0 0.9 %collective-permute-done.4.refs_2_.refs_0_.refs_3_ = bf16[80,1792]{1,0:T(8,128)(2,1)S(1)} collective-permute-done((bf16[80,1792]{1,0:T(8,128)(2,1)S(1)}, bf16[80,1792]{1,0:T(8,128)(2,1)S(1)}, u32[]{:S(2)}, u32[]{:S(2)}) %collective-permute-start.4) | collective-permute-done | bytes 286752 | tf_op jit(solution)/shard_map/ppermute | solution.py:448
  23.9 0.0 copy-done
  23.9 0.0 copy-done.1
  23.9 0.0 copy-done.2
  23.9 0.0 copy-done.3
  23.9 0.0 copy-done.4
  23.9 0.0 copy-done.5
  23.9 0.7 %shard_map.118 = (bf16[64,1792]{1,0:T(8,128)(2,1)S(1)}, bf16[16,1792]{1,0:T(8,128)(2,1)S(1)}, bf16[16,1792]{1,0:T(8,128)(2,1)S(1)}, bf16[16,1792]{1,0:T(8,128)(2,1)S(1)}, bf16[16,1792]{1,0:T(8,128)(2,1)S(1)}) custom-call(bf16[80,1792]{1,0:T(8,128)(2,1)S(1)} %collective-permute-done.4.refs_2_.refs_0_.refs_3_, ...), custom_call_target="tpu_custom_call" | custom-call | bytes 1835008 | tf_op jit(solution)/shard_map/pallas_call | solution.py:25
  24.6 0.2 collective-permute-start.13
  24.8 2.0 %collective-permute-start.14 = (bf16[16,1792]{1,0:T(8,128)(2,1)S(1)}, bf16[16,1792]{1,0:T(8,128)(2,1)S(1)}, u32[]{:S(2)}, u32[]{:S(2)}) collective-permute-start(bf16[16,1792]{1,0:T(8,128)(2,1)S(1)} %get-tuple-element.47), channel_id=1, source_target_pairs={{0,24},{4,28},{8,16},{12,20},{16,8},{20,12},{24,0},{28,4},{1,25},{... | collective-permute-start | bytes 172040 | tf_op jit(solution)/shard_map/ppermute | solution.py:460
  26.8 1.4 %collective-permute-start.15 = (bf16[16,1792]{1,0:T(8,128)(2,1)S(1)}, bf16[16,1792]{1,0:T(8,128)(2,1)S(1)}, u32[]{:S(2)}, u32[]{:S(2)}) collective-permute-start(bf16[16,1792]{1,0:T(8,128)(2,1)S(1)} %get-tuple-element.48), channel_id=1, source_target_pairs={{0,28},{4,24},{8,20},{12,16},{16,12},{20,8},{24,4},{28,0},{1,29},{... | collective-permute-start | bytes 172040 | tf_op jit(solution)/shard_map/ppermute | solution.py:460
  28.3 0.8 %collective-permute-start.12 = (bf16[16,1792]{1,0:T(8,128)(2,1)S(1)}, bf16[16,1792]{1,0:T(8,128)(2,1)S(1)}, u32[]{:S(2)}, u32[]{:S(2)}) collective-permute-start(bf16[16,1792]{1,0:T(8,128)(2,1)S(1)} %get-tuple-element.45.refs_0_), channel_id=1, source_target_pairs={{0,16},{4,20},{8,24},{12,28},{16,0},{20,4},{24,8},{28,12},{1,17},{... | collective-permute-start | bytes 172040 | tf_op jit(solution)/shard_map/ppermute | solution.py:460
  29.1 2.7 %collective-permute-start.11 = (bf16[64,1792]{1,0:T(8,128)(2,1)S(1)}, bf16[64,1792]{1,0:T(8,128)(2,1)S(1)}, u32[]{:S(2)}, u32[]{:S(2)}) collective-permute-start(bf16[64,1792]{1,0:T(8,128)(2,1)S(1)} %shard_map.119), channel_id=1, source_target_pairs={{0,1},{1,0},{2,3},{3,2},{4,5},{5,4},{6,7},{7,6},{8,9},{9,8},{10,11... | collective-permute-start | bytes 688136 | tf_op jit(solution)/shard_map/ppermute | solution.py:448
  31.8 0.0 collective-permute-done.13.refs_1_
  31.8 0.0 collective-permute-done.14.refs_2_
  31.8 0.0 collective-permute-done.15.refs_3_
  31.8 1.2 %collective-permute-done.12.refs_0_ = bf16[16,1792]{1,0:T(8,128)(2,1)S(1)} collective-permute-done((bf16[16,1792]{1,0:T(8,128)(2,1)S(1)}, bf16[16,1792]{1,0:T(8,128)(2,1)S(1)}, u32[]{:S(2)}, u32[]{:S(2)}) %collective-permute-start.12) | collective-permute-done | bytes 57376 | tf_op jit(solution)/shard_map/ppermute | solution.py:460
  33.0 2.7 %collective-permute-start.19 = (bf16[64,1792]{1,0:T(8,128)(2,1)S(1)}, bf16[64,1792]{1,0:T(8,128)(2,1)S(1)}, u32[]{:S(2)}, u32[]{:S(2)}) collective-permute-start(bf16[64,1792]{1,0:T(8,128)(2,1)S(1)} %shard_map.120.refs_4_.refs_2_), channel_id=1, source_target_pairs={{0,2},{1,3},{2,0},{3,1},{4,6},{5,7},{6,4},{7,5},{8,10},{9,11},{10,... | collective-permute-start | bytes 688136 | tf_op jit(solution)/shard_map/ppermute | solution.py:448
  35.6 1.6 %collective-permute-start.17 = (bf16[64,1792]{1,0:T(8,128)(2,1)S(1)}, bf16[64,1792]{1,0:T(8,128)(2,1)S(1)}, u32[]{:S(2)}, u32[]{:S(2)}) collective-permute-start(bf16[64,1792]{1,0:T(8,128)(2,1)S(1)} %shard_map.120.refs_4_.refs_2_), channel_id=1, source_target_pairs={{0,1},{1,0},{2,3},{3,2},{4,5},{5,4},{6,7},{7,6},{8,9},{9,8},{10,11... | collective-permute-start | bytes 688136 | tf_op jit(solution)/shard_map/ppermute | solution.py:448
  37.2 2.5 %collective-permute-done.11.refs_0_.refs_9_ = bf16[64,1792]{1,0:T(8,128)(2,1)S(1)} collective-permute-done((bf16[64,1792]{1,0:T(8,128)(2,1)S(1)}, bf16[64,1792]{1,0:T(8,128)(2,1)S(1)}, u32[]{:S(2)}, u32[]{:S(2)}) %collective-permute-start.11) | collective-permute-done | bytes 229408 | tf_op jit(solution)/shard_map/ppermute | solution.py:448
  39.7 2.5 %shard_map.121 = (bf16[32,1792]{1,0:T(8,128)(2,1)S(1)}, bf16[32,1792]{1,0:T(8,128)(2,1)S(1)}) custom-call(bf16[64,1792]{1,0:T(8,128)(2,1)S(1)} %collective-permute-done.11.refs_0_.refs_9_, bf16[1,2,1,64,1408]{4,3,2,1,0:T(8,128)(2,1)S(1)} %get-tuple-element.38.refs_0_.refs_1_, bf16[1792,1408]{1,0:T(8,128)(2,1)S(1)} %shard_map.114.refs_0_.refs_1_.refs_2_, ...), custom_call_target="tpu_custom_call" | custom-call | flops 484442112 | bytes 7569408 | tf_op jit(solution)/shard_map/pallas_call | solution.py:25
  42.3 0.1 collective-permute-start.16
  42.3 0.9 %collective-permute-start.10 = (bf16[64,1792]{1,0:T(8,128)(2,1)S(1)}, bf16[64,1792]{1,0:T(8,128)(2,1)S(1)}, u32[]{:S(2)}, u32[]{:S(2)}) collective-permute-start(bf16[64,1792]{1,0:T(8,128)(2,1)S(1)} %get-tuple-element.44.refs_1_), channel_id=1, source_target_pairs={{0,16},{16,0},{1,17},{17,1},{2,18},{18,2},{3,19},{19,3},{4,20},{20... | collective-permute-start | bytes 688136 | tf_op jit(solution)/shard_map/ppermute | solution.py:567
  43.2 3.3 %collective-permute-done.19.refs_6_ = bf16[64,1792]{1,0:T(8,128)(2,1)S(1)} collective-permute-done((bf16[64,1792]{1,0:T(8,128)(2,1)S(1)}, bf16[64,1792]{1,0:T(8,128)(2,1)S(1)}, u32[]{:S(2)}, u32[]{:S(2)}) %collective-permute-start.19) | collective-permute-done | bytes 229408 | tf_op jit(solution)/shard_map/ppermute | solution.py:448
  46.5 0.7 %collective-permute-start.21 = (bf16[64,1792]{1,0:T(8,128)(2,1)S(1)}, bf16[64,1792]{1,0:T(8,128)(2,1)S(1)}, u32[]{:S(2)}, u32[]{:S(2)}) collective-permute-start(bf16[64,1792]{1,0:T(8,128)(2,1)S(1)} %collective-permute-done.19.refs_6_), channel_id=1, source_target_pairs={{0,1},{1,0},{2,3},{3,2},{4,5},{5,4},{6,7},{7,6},{8,9},{9,8},{10,11... | collective-permute-start | bytes 688136 | tf_op jit(solution)/shard_map/ppermute | solution.py:448
  47.2 0.0 collective-permute-done.17.refs_0_.refs_4_
  47.2 0.0 collective-permute-done.16.refs_2_.refs_9_
  47.2 1.4 %collective-permute-start.18 = (bf16[32,1792]{1,0:T(8,128)(2,1)S(1)}, bf16[32,1792]{1,0:T(8,128)(2,1)S(1)}, u32[]{:S(2)}, u32[]{:S(2)}) collective-permute-start(bf16[32,1792]{1,0:T(8,128)(2,1)S(1)} %shard_map.122), channel_id=1, source_target_pairs={{0,8},{4,12},{8,0},{12,4},{1,9},{5,13},{9,1},{13,5},{2,10},{6,14},... | collective-permute-start | bytes 344072 | tf_op jit(solution)/shard_map/ppermute | solution.py:448
  48.6 2.3 %collective-permute-start.5 = (bf16[16,1792]{1,0:T(8,128)(2,1)S(1)}, bf16[16,1792]{1,0:T(8,128)(2,1)S(1)}, u32[]{:S(2)}, u32[]{:S(2)}) collective-permute-start(bf16[16,1792]{1,0:T(8,128)(2,1)S(1)} %get-tuple-element.37), channel_id=1, source_target_pairs={{0,2},{1,3},{2,0},{3,1},{4,6},{5,7},{6,4},{7,5},{8,10},{9,11},{10,... | collective-permute-start | bytes 172040 | tf_op jit(solution)/shard_map/ppermute | solution.py:448
  51.0 2.5 %collective-permute-start.20 = (bf16[16,1792]{1,0:T(8,128)(2,1)S(1)}, bf16[16,1792]{1,0:T(8,128)(2,1)S(1)}, u32[]{:S(2)}, u32[]{:S(2)}) collective-permute-start(bf16[16,1792]{1,0:T(8,128)(2,1)S(1)} %get-tuple-element.53), channel_id=1, source_target_pairs={{0,3},{1,2},{2,1},{3,0},{4,7},{5,6},{6,5},{7,4},{8,11},{9,10},{10,... | collective-permute-start | bytes 172040 | tf_op jit(solution)/shard_map/ppermute | solution.py:448
  53.5 0.4 collective-permute-done.5.refs_3_.refs_5_
  53.9 0.4 shard_map.116.refs_0_.refs_10_
  54.3 0.0 collective-permute-done.10.refs_2_
  54.3 0.0 collective-permute-done.18.refs_10_
  54.3 1.2 %shard_map.123 = (bf16[1,2,64,1792]{3,2,1,0:T(8,128)(2,1)}, f32[8,128]{1,0:T(8,128)S(1)}) custom-call(f32[1,1,176,1792]{3,2,1,0:T(8,128)S(1)} %shard_map.116.refs_0_.refs_10_, bf16[64,1792]{1,0:T(8,128)(2,1)S(1)} %get-tuple-element.44.refs_1_, bf16[64,1792]{1,0:T(8,128)(2,1)S(1)} %collective-permute-done.10.refs_2_, bf16[64,1792]{1,0:T(8,128)(2,1)S(1)} %copy-done.2, ...), custom_call_target="tpu_custom_call" | custom-call | bytes 1835008 | tf_op jit(solution)/shard_map/pallas_call | solution.py:25
  55.5 2.4 %collective-permute-done.20.refs_7_ = bf16[16,1792]{1,0:T(8,128)(2,1)S(1)} collective-permute-done((bf16[16,1792]{1,0:T(8,128)(2,1)S(1)}, bf16[16,1792]{1,0:T(8,128)(2,1)S(1)}, u32[]{:S(2)}, u32[]{:S(2)}) %collective-permute-start.20) | collective-permute-done | bytes 57376 | tf_op jit(solution)/shard_map/ppermute | solution.py:448
  57.9 0.0 collective-permute-done.21.refs_8_
  57.9 1.6 %shard_map.124 = f32[1,1,176,1792]{3,2,1,0:T(8,128)} custom-call(f32[8,128]{1,0:T(8,128)S(1)} %get-tuple-element.52.refs_0_, bf16[16,1792]{1,0:T(8,128)(2,1)S(1)} %get-tuple-element.28.refs_0_.refs_1_, bf16[64,1792]{1,0:T(8,128)(2,1)S(1)} %shard_map.120.refs_4_.refs_2_, bf16[80,1792]{1,0:T(8,128)(2,1)S(1)} %collective-permute-done.4.refs_2_.refs_0_.refs_3_, ...), custom_call_target="tpu_custom_call" | custom-call | flops 201850880 | bytes 2523136 | tf_op jit(solution)/shard_map/pallas_call | solution.py:25
  (4 shorter events, 0.1 us)
Async XLA Ops:
  2.7 7.3 %collective-permute-start.1 = (bf16[16,1792]{1,0:T(8,128)(2,1)S(1)}, bf16[16,1792]{1,0:T(8,128)(2,1)S(1)}, u32[]{:S(2)}, u32[]{:S(2)}) collective-permute-start(bf16[16,1792]{1,0:T(8,128)(2,1)S(1)} %get-tuple-element.32), channel_id=1, source_target_pairs={{0,4},{4,0},{8,12},{12,8},{1,5},{5,1},{9,13},{13,9},{2,6},{6,2},{1... | collective-permute-start | bytes 172040 | tf_op jit(solution)/shard_map/ppermute | solution.py:448
  3.2 6.8 %collective-permute-start.2 = (bf16[16,1792]{1,0:T(8,128)(2,1)S(1)}, bf16[16,1792]{1,0:T(8,128)(2,1)S(1)}, u32[]{:S(2)}, u32[]{:S(2)}) collective-permute-start(bf16[16,1792]{1,0:T(8,128)(2,1)S(1)} %get-tuple-element.33), channel_id=1, source_target_pairs={{0,8},{4,12},{8,0},{12,4},{1,9},{5,13},{9,1},{13,5},{2,10},{6,14},... | collective-permute-start | bytes 172040 | tf_op jit(solution)/shard_map/ppermute | solution.py:448
  5.8 4.2 %collective-permute-start.3 = (bf16[16,1792]{1,0:T(8,128)(2,1)S(1)}, bf16[16,1792]{1,0:T(8,128)(2,1)S(1)}, u32[]{:S(2)}, u32[]{:S(2)}) collective-permute-start(bf16[16,1792]{1,0:T(8,128)(2,1)S(1)} %get-tuple-element.34), channel_id=1, source_target_pairs={{0,12},{4,8},{8,4},{12,0},{1,13},{5,9},{9,5},{13,1},{2,14},{6,10},... | collective-permute-start | bytes 172040 | tf_op jit(solution)/shard_map/ppermute | solution.py:448
  5.9 4.1 %collective-permute-start = (f32[2,64]{1,0:T(2,128)S(1)}, f32[2,64]{1,0:T(2,128)S(1)}, u32[]{:S(2)}, u32[]{:S(2)}) collective-permute-start(f32[2,64]{1,0:T(2,128)S(1)} %get-tuple-element.29.refs_1_), channel_id=1, source_target_pairs={{0,16},{16,0},{1,17},{17,1},{2,18},{18,2},{3,19},{19,3},{4,20},{20... | collective-permute-start | bytes 1544 | tf_op jit(solution)/shard_map/ppermute | solution.py:529
  10.1 13.8 %collective-permute-start.4 = (bf16[80,1792]{1,0:T(8,128)(2,1)S(1)}, bf16[80,1792]{1,0:T(8,128)(2,1)S(1)}, u32[]{:S(2)}, u32[]{:S(2)}) collective-permute-start(bf16[80,1792]{1,0:T(8,128)(2,1)S(1)} %get-tuple-element.36), channel_id=1, source_target_pairs={{0,1},{1,0},{2,3},{3,2},{4,5},{5,4},{6,7},{7,6},{8,9},{9,8},{10,11... | collective-permute-start | bytes 860168 | tf_op jit(solution)/shard_map/ppermute | solution.py:448
  11.8 11.3 %collective-permute-start.6 = (bf16[64,1792]{1,0:T(8,128)(2,1)S(1)}, bf16[64,1792]{1,0:T(8,128)(2,1)S(1)}, u32[]{:S(2)}, u32[]{:S(2)}) collective-permute-start(bf16[64,1792]{1,0:T(8,128)(2,1)S(1)} %get-tuple-element.35.refs_1_.refs_3_), channel_id=1, source_target_pairs={{0,2},{1,3},{2,0},{3,1},{4,6},{5,7},{6,4},{7,5},{8,10},{9,11},{10,... | collective-permute-start | bytes 688136 | tf_op jit(solution)/shard_map/ppermute | solution.py:448
  14.3 9.6 %copy-start = (bf16[1,2,64,1792]{3,2,1,0:T(8,128)(2,1)S(1)}, bf16[1,2,64,1792]{3,2,1,0:T(8,128)(2,1)}, u32[]{:S(2)}) copy-start(bf16[1,2,64,1792]{3,2,1,0:T(8,128)(2,1)} %refs_4_.5) | copy-start | bytes 1376260
  14.3 9.6 %copy-start.1 = (bf16[1,64,1792]{2,1,0:T(8,128)(2,1)S(1)}, bf16[1,64,1792]{2,1,0:T(8,128)(2,1)}, u32[]{:S(2)}) copy-start(bf16[1,64,1792]{2,1,0:T(8,128)(2,1)} %param.10) | copy-start | bytes 688132
  14.3 9.6 %copy-start.2 = (bf16[64,1792]{1,0:T(8,128)(2,1)S(1)}, bf16[64,1792]{1,0:T(8,128)(2,1)}, u32[]{:S(2)}) copy-start(bf16[64,1792]{1,0:T(8,128)(2,1)} %refs_3_.3) | copy-start | bytes 688132
  14.3 9.6 %copy-start.3 = (f32[1,1792]{1,0:T(1,128)S(1)}, f32[1,1792]{1,0:T(1,128)}, u32[]{:S(2)}) copy-start(f32[1,1792]{1,0:T(1,128)} %refs_5_.3) | copy-start | bytes 21508
  14.4 9.6 %copy-start.4 = (s32[1,2,64,1]{2,3,1,0:T(1,128)S(1)}, s32[1,2,64,1]{2,3,1,0:T(1,128)}, u32[]{:S(2)}) copy-start(s32[1,2,64,1]{2,3,1,0:T(1,128)} %param.14) | copy-start | bytes 1540
  14.4 9.6 %copy-start.5 = (s32[1,2,64,1]{2,3,1,0:T(1,128)S(1)}, s32[1,2,64,1]{2,3,1,0:T(1,128)}, u32[]{:S(2)}) copy-start(s32[1,2,64,1]{2,3,1,0:T(1,128)} %param.15) | copy-start | bytes 1540
  16.9 1.9 %collective-permute-start.7 = (bf16[16,1792]{1,0:T(8,128)(2,1)S(1)}, bf16[16,1792]{1,0:T(8,128)(2,1)S(1)}, u32[]{:S(2)}, u32[]{:S(2)}) collective-permute-start(bf16[16,1792]{1,0:T(8,128)(2,1)S(1)} %get-tuple-element.41), channel_id=1, source_target_pairs={{0,4},{4,0},{8,12},{12,8},{1,5},{5,1},{9,13},{13,9},{2,6},{6,2},{1... | collective-permute-start | bytes 172040 | tf_op jit(solution)/shard_map/ppermute | solution.py:448
  17.0 4.3 %collective-permute-start.8 = (bf16[16,1792]{1,0:T(8,128)(2,1)S(1)}, bf16[16,1792]{1,0:T(8,128)(2,1)S(1)}, u32[]{:S(2)}, u32[]{:S(2)}) collective-permute-start(bf16[16,1792]{1,0:T(8,128)(2,1)S(1)} %get-tuple-element.42), channel_id=1, source_target_pairs={{0,8},{4,12},{8,0},{12,4},{1,9},{5,13},{9,1},{13,5},{2,10},{6,14},... | collective-permute-start | bytes 172040 | tf_op jit(solution)/shard_map/ppermute | solution.py:448
  18.5 3.9 %collective-permute-start.9 = (bf16[16,1792]{1,0:T(8,128)(2,1)S(1)}, bf16[16,1792]{1,0:T(8,128)(2,1)S(1)}, u32[]{:S(2)}, u32[]{:S(2)}) collective-permute-start(bf16[16,1792]{1,0:T(8,128)(2,1)S(1)} %get-tuple-element.43), channel_id=1, source_target_pairs={{0,12},{4,8},{8,4},{12,0},{1,13},{5,9},{9,5},{13,1},{2,14},{6,10},... | collective-permute-start | bytes 172040 | tf_op jit(solution)/shard_map/ppermute | solution.py:448
  24.6 7.1 %collective-permute-start.13 = (bf16[16,1792]{1,0:T(8,128)(2,1)S(1)}, bf16[16,1792]{1,0:T(8,128)(2,1)S(1)}, u32[]{:S(2)}, u32[]{:S(2)}) collective-permute-start(bf16[16,1792]{1,0:T(8,128)(2,1)S(1)} %get-tuple-element.46), channel_id=1, source_target_pairs={{0,20},{4,16},{8,28},{12,24},{16,4},{20,0},{24,12},{28,8},{1,21},{... | collective-permute-start | bytes 172040 | tf_op jit(solution)/shard_map/ppermute | solution.py:460
  24.8 6.9 %collective-permute-start.14 = (bf16[16,1792]{1,0:T(8,128)(2,1)S(1)}, bf16[16,1792]{1,0:T(8,128)(2,1)S(1)}, u32[]{:S(2)}, u32[]{:S(2)}) collective-permute-start(bf16[16,1792]{1,0:T(8,128)(2,1)S(1)} %get-tuple-element.47), channel_id=1, source_target_pairs={{0,24},{4,28},{8,16},{12,20},{16,8},{20,12},{24,0},{28,4},{1,25},{... | collective-permute-start | bytes 172040 | tf_op jit(solution)/shard_map/ppermute | solution.py:460
  26.8 4.9 %collective-permute-start.15 = (bf16[16,1792]{1,0:T(8,128)(2,1)S(1)}, bf16[16,1792]{1,0:T(8,128)(2,1)S(1)}, u32[]{:S(2)}, u32[]{:S(2)}) collective-permute-start(bf16[16,1792]{1,0:T(8,128)(2,1)S(1)} %get-tuple-element.48), channel_id=1, source_target_pairs={{0,28},{4,24},{8,20},{12,16},{16,12},{20,8},{24,4},{28,0},{1,29},{... | collective-permute-start | bytes 172040 | tf_op jit(solution)/shard_map/ppermute | solution.py:460
  28.3 4.7 %collective-permute-start.12 = (bf16[16,1792]{1,0:T(8,128)(2,1)S(1)}, bf16[16,1792]{1,0:T(8,128)(2,1)S(1)}, u32[]{:S(2)}, u32[]{:S(2)}) collective-permute-start(bf16[16,1792]{1,0:T(8,128)(2,1)S(1)} %get-tuple-element.45.refs_0_), channel_id=1, source_target_pairs={{0,16},{4,20},{8,24},{12,28},{16,0},{20,4},{24,8},{28,12},{1,17},{... | collective-permute-start | bytes 172040 | tf_op jit(solution)/shard_map/ppermute | solution.py:460
  29.1 10.7 %collective-permute-start.11 = (bf16[64,1792]{1,0:T(8,128)(2,1)S(1)}, bf16[64,1792]{1,0:T(8,128)(2,1)S(1)}, u32[]{:S(2)}, u32[]{:S(2)}) collective-permute-start(bf16[64,1792]{1,0:T(8,128)(2,1)S(1)} %shard_map.119), channel_id=1, source_target_pairs={{0,1},{1,0},{2,3},{3,2},{4,5},{5,4},{6,7},{7,6},{8,9},{9,8},{10,11... | collective-permute-start | bytes 688136 | tf_op jit(solution)/shard_map/ppermute | solution.py:448
  33.0 13.5 %collective-permute-start.19 = (bf16[64,1792]{1,0:T(8,128)(2,1)S(1)}, bf16[64,1792]{1,0:T(8,128)(2,1)S(1)}, u32[]{:S(2)}, u32[]{:S(2)}) collective-permute-start(bf16[64,1792]{1,0:T(8,128)(2,1)S(1)} %shard_map.120.refs_4_.refs_2_), channel_id=1, source_target_pairs={{0,2},{1,3},{2,0},{3,1},{4,6},{5,7},{6,4},{7,5},{8,10},{9,11},{10,... | collective-permute-start | bytes 688136 | tf_op jit(solution)/shard_map/ppermute | solution.py:448
  35.6 11.5 %collective-permute-start.17 = (bf16[64,1792]{1,0:T(8,128)(2,1)S(1)}, bf16[64,1792]{1,0:T(8,128)(2,1)S(1)}, u32[]{:S(2)}, u32[]{:S(2)}) collective-permute-start(bf16[64,1792]{1,0:T(8,128)(2,1)S(1)} %shard_map.120.refs_4_.refs_2_), channel_id=1, source_target_pairs={{0,1},{1,0},{2,3},{3,2},{4,5},{5,4},{6,7},{7,6},{8,9},{9,8},{10,11... | collective-permute-start | bytes 688136 | tf_op jit(solution)/shard_map/ppermute | solution.py:448
  42.3 4.9 %collective-permute-start.16 = (bf16[32,1792]{1,0:T(8,128)(2,1)S(1)}, bf16[32,1792]{1,0:T(8,128)(2,1)S(1)}, u32[]{:S(2)}, u32[]{:S(2)}) collective-permute-start(bf16[32,1792]{1,0:T(8,128)(2,1)S(1)} %get-tuple-element.50), channel_id=1, source_target_pairs={{0,4},{4,0},{8,12},{12,8},{1,5},{5,1},{9,13},{13,9},{2,6},{6,2},{1... | collective-permute-start | bytes 344072 | tf_op jit(solution)/shard_map/ppermute | solution.py:448
  42.3 11.9 %collective-permute-start.10 = (bf16[64,1792]{1,0:T(8,128)(2,1)S(1)}, bf16[64,1792]{1,0:T(8,128)(2,1)S(1)}, u32[]{:S(2)}, u32[]{:S(2)}) collective-permute-start(bf16[64,1792]{1,0:T(8,128)(2,1)S(1)} %get-tuple-element.44.refs_1_), channel_id=1, source_target_pairs={{0,16},{16,0},{1,17},{17,1},{2,18},{18,2},{3,19},{19,3},{4,20},{20... | collective-permute-start | bytes 688136 | tf_op jit(solution)/shard_map/ppermute | solution.py:567
  46.5 11.3 %collective-permute-start.21 = (bf16[64,1792]{1,0:T(8,128)(2,1)S(1)}, bf16[64,1792]{1,0:T(8,128)(2,1)S(1)}, u32[]{:S(2)}, u32[]{:S(2)}) collective-permute-start(bf16[64,1792]{1,0:T(8,128)(2,1)S(1)} %collective-permute-done.19.refs_6_), channel_id=1, source_target_pairs={{0,1},{1,0},{2,3},{3,2},{4,5},{5,4},{6,7},{7,6},{8,9},{9,8},{10,11... | collective-permute-start | bytes 688136 | tf_op jit(solution)/shard_map/ppermute | solution.py:448
  47.2 7.1 %collective-permute-start.18 = (bf16[32,1792]{1,0:T(8,128)(2,1)S(1)}, bf16[32,1792]{1,0:T(8,128)(2,1)S(1)}, u32[]{:S(2)}, u32[]{:S(2)}) collective-permute-start(bf16[32,1792]{1,0:T(8,128)(2,1)S(1)} %shard_map.122), channel_id=1, source_target_pairs={{0,8},{4,12},{8,0},{12,4},{1,9},{5,13},{9,1},{13,5},{2,10},{6,14},... | collective-permute-start | bytes 344072 | tf_op jit(solution)/shard_map/ppermute | solution.py:448
  48.6 5.2 %collective-permute-start.5 = (bf16[16,1792]{1,0:T(8,128)(2,1)S(1)}, bf16[16,1792]{1,0:T(8,128)(2,1)S(1)}, u32[]{:S(2)}, u32[]{:S(2)}) collective-permute-start(bf16[16,1792]{1,0:T(8,128)(2,1)S(1)} %get-tuple-element.37), channel_id=1, source_target_pairs={{0,2},{1,3},{2,0},{3,1},{4,6},{5,7},{6,4},{7,5},{8,10},{9,11},{10,... | collective-permute-start | bytes 172040 | tf_op jit(solution)/shard_map/ppermute | solution.py:448
  51.0 6.9 %collective-permute-start.20 = (bf16[16,1792]{1,0:T(8,128)(2,1)S(1)}, bf16[16,1792]{1,0:T(8,128)(2,1)S(1)}, u32[]{:S(2)}, u32[]{:S(2)}) collective-permute-start(bf16[16,1792]{1,0:T(8,128)(2,1)S(1)} %get-tuple-element.53), channel_id=1, source_target_pairs={{0,3},{1,2},{2,1},{3,0},{4,7},{5,6},{6,5},{7,4},{8,11},{9,10},{10,... | collective-permute-start | bytes 172040 | tf_op jit(solution)/shard_map/ppermute | solution.py:448

commit v4 on v3

--- a/solution.py
+++ b/solution.py
@@ -13,7 +13,9 @@
 f32 = jnp.float32
 
 
-def on_chip(body, outs, args, fetched=(), after=(), scratch=(), flops=0, moved=0):
+def on_chip(
+    body, outs, args, fetched=(), after=(), scratch=(), flops=0, moved=0, sends=False
+):
     whole = pl.BlockSpec(memory_space=pltpu.VMEM)
     there = pl.BlockSpec(memory_space=pltpu.HBM)
     anywhere = pl.BlockSpec(memory_space=pl.ANY)
@@ -26,7 +28,7 @@
         run,
         out_shape=outs,
         in_specs=[there] * first + [anywhere] * len(after) + [whole] * len(args),
-        out_specs=jax.tree.map(lambda _: whole, outs),
+        out_specs=jax.tree.map(lambda _: anywhere if sends else whole, outs),
         scratch_shapes=scratch,
         compiler_params=pltpu.CompilerParams(vmem_limit_bytes=VMEM_LIMIT),
         cost_estimate=pl.CostEstimate(flops=flops, bytes_accessed=moved, transcendentals=0),
@@ -417,6 +419,9 @@
     def place(array):
         return next(index for index, other in enumerate(arrays) if other is array)
 
+    sends = earlier is not None and block % 8 == 0 and width % 256 == 0
+    parts = width // 256
+    part = 256
     places = [(place(left), start, number, place(right)) for left, start, number, right in terms]
 
     def body(*refs):
@@ -428,16 +433,40 @@
             else:
                 lefts.append(unpack(refs[left], start, block, columns))
             rights.append(refs[right][0:rows, :])
-        total = dot(jnp.concatenate(lefts, axis=1), jnp.concatenate(rights, axis=0), 1, 0)
-        if earlier is not None:
-            total = (refs[len(arrays)][0, 0] + total) / scale
-        refs[-1][0, 0] = total
+        left_value = jnp.concatenate(lefts, axis=1)
+        right_value = jnp.concatenate(rights, axis=0)
+        if not sends:
+            total = dot(left_value, right_value, 1, 0)
+            if earlier is not None:
+                total = (refs[len(arrays)][0, 0] + total) / scale
+            refs[-1][0, 0] = total
+            return
+        out_ref, held, sems = refs[-3:]
+        copies = []
+        for index in range(parts):
+            columns = slice(index * part, (index + 1) * part)
+            total = dot(left_value, right_value[:, columns], 1, 0)
+            held[:, columns] = (refs[len(arrays)][0, 0, :, columns] + total) / scale
+            copies.append(
+                pltpu.make_async_copy(
+                    held.at[:, pl.ds(index * part, part)],
+                    out_ref.at[0, 0, :, pl.ds(index * part, part)],
+                    sems.at[index],
+                )
+            )
+            copies[-1].start()
+        for copy in copies:
+            copy.wait()
 
     return on_chip(
         body,
         [jax.ShapeDtypeStruct((1, 1, block, width), f32)],
         tuple(arrays) + (() if earlier is None else (earlier,)),
         after=after,
+        scratch=[pltpu.VMEM((block, width), f32), pltpu.SemaphoreType.DMA((parts,))]
+        if sends
+        else (),
+        sends=sends,
         flops=2 * len(terms) * rows * block * width,
         moved=8 * block * width,
     )[0]
@@ -574,14 +603,15 @@
         third = at_distance(second, "edp", 1)
         units = [at_distance(hidden[step], "edp", step) for step in (2, 3)]
         arrived, late, tail = [again], (last,), (first,)
-        now = [(hidden[0], 0, 0, joined), (near, rows, 0, near), (units[0], 0, 0, far)]
-        then = [
+        now = [
+            (hidden[0], 0, 0, joined),
+            (near, rows, 0, near),
+            (units[0], 0, 0, far),
             (hidden[0], 0, 1, again),
             (near, rows, 1, first),
             (units[0], 0, 1, second),
-            (units[1], 0, 1, third),
-            (units[1], 0, 0, last),
         ]
+        then = [(units[1], 0, 0, last), (units[1], 0, 1, third)]
     else:
         late = tail = ()
         again = steps_over("edp", arrived * replicas)

time: 59.6 us -> 59.3 us (level)
  transfers between devices with their start and end apart: 22 -> 22, of which waited for: 9 -> 9; matrix products, arithmetic and copies ran while one was open for 0% -> 0% of each run, Pallas kernels for 15% -> 16%
where the time goes in v4:
time: 59.3 us; the launch traced here: 59.1 us
  starting transfers between devices  30.3 us (51%)
  waiting for transfers between devices  14.7 us (25%)
  Pallas kernels  13.2 us (22%)
  between operations  0.82 us (1%)
    ppermute x16, starting transfers between devices, at_distance(): lax.ppermute(value, axis, [(source, source ^ step) for source in range(co...  23.2 us
    ppermute x16, waiting for transfers between devices, at_distance(): lax.ppermute(value, axis, [(source, source ^ step) for source in range(co...  13.5 us
    pallas_call x12, Pallas kernels, on_chip(): pl.pallas_call(run, out_shape=outs, in_specs=[there] * first + [anywhere]...  13.2 us
    ppermute x4, starting transfers between devices, behind(): lax.ppermute(value, ('pipe', 'expert'), [(section * count + source, (sect...  4.46 us
    ppermute x1, starting transfers between devices, local(): lax.ppermute(table, 'pipe', [(source, (source + 1) % sections) for source...  1.7 us
    ppermute x4, waiting for transfers between devices, behind(): lax.ppermute(value, ('pipe', 'expert'), [(section * count + source, (sect...  1.2 us
  transfers between devices with their start and end apart: 22, of which 9 were waited for; matrix products, arithmetic and copies ran while one was open for 0% of the time, Pallas kernels for 16%

profile of v4, /device:TPU:0, one launch (start us, length us, event | category | flops | bytes accessed | tf_op | source)
XLA Modules:
  0.0 59.1 jit_solution(1416939910216797353)
XLA Ops:
  0.6 2.1 %shard_map.113 = (f32[2,64]{1,0:T(2,128)S(1)}, bf16[1,2,1,64,1408]{4,3,2,1,0:T(8,128)(2,1)S(1)}, bf16[704,1792]{1,0:T(8,128)(2,1)S(1)}, bf16[16,1792]{1,0:T(8,12...) custom-call(bf16[64,1792]{1,0:T(8,128)(2,1)} %bitcast.12, ...), custom_call_target="tpu_custom_call" | custom-call | bytes 688128 | tf_op jit(solution)/shard_map/pallas_call | solution.py:27
  2.7 0.5 collective-permute-start.1
  3.2 2.6 %collective-permute-start.2 = (bf16[16,1792]{1,0:T(8,128)(2,1)S(1)}, bf16[16,1792]{1,0:T(8,128)(2,1)S(1)}, u32[]{:S(2)}, u32[]{:S(2)}) collective-permute-start(bf16[16,1792]{1,0:T(8,128)(2,1)S(1)} %get-tuple-element.33), channel_id=1, source_target_pairs={{0,8},{4,12},{8,0},{12,4},{1,9},{5,13},{9,1},{13,5},{2,10},{6,14},... | collective-permute-start | bytes 172040 | tf_op jit(solution)/shard_map/ppermute | solution.py:477
  5.8 0.1 collective-permute-start.3
  5.9 1.7 %collective-permute-start = (f32[2,64]{1,0:T(2,128)S(1)}, f32[2,64]{1,0:T(2,128)S(1)}, u32[]{:S(2)}, u32[]{:S(2)}) collective-permute-start(f32[2,64]{1,0:T(2,128)S(1)} %get-tuple-element.29.refs_1_), channel_id=1, source_target_pairs={{0,16},{16,0},{1,17},{17,1},{2,18},{18,2},{3,19},{19,3},{4,20},{20... | collective-permute-start | bytes 1544 | tf_op jit(solution)/shard_map/ppermute | solution.py:558
  7.6 2.4 %shard_map.114.refs_0_.refs_1_.refs_2_ = bf16[1792,1408]{1,0:T(8,128)(2,1)S(1)} custom-call(bf16[1792,1408]{1,0:T(8,128)(2,1)} %bitcast.20, f32[2,64]{1,0:T(2,128)S(1)} %get-tuple-element.29.refs_1_), custom_call_target="tpu_custom_call" | custom-call | bytes 5046272 | tf_op jit(solution)/shard_map/pallas_call | solution.py:27
  10.0 0.0 collective-permute-done.refs_1_.refs_8_
  10.0 0.0 collective-permute-done.1.refs_4_
  10.0 0.0 collective-permute-done.2.refs_5_
  10.1 0.0 collective-permute-done.3.refs_6_
  10.1 1.6 %collective-permute-start.4 = (bf16[80,1792]{1,0:T(8,128)(2,1)S(1)}, bf16[80,1792]{1,0:T(8,128)(2,1)S(1)}, u32[]{:S(2)}, u32[]{:S(2)}) collective-permute-start(bf16[80,1792]{1,0:T(8,128)(2,1)S(1)} %get-tuple-element.36), channel_id=1, source_target_pairs={{0,1},{1,0},{2,3},{3,2},{4,5},{5,4},{6,7},{7,6},{8,9},{9,8},{10,11... | collective-permute-start | bytes 860168 | tf_op jit(solution)/shard_map/ppermute | solution.py:477
  11.8 2.6 %collective-permute-start.6 = (bf16[64,1792]{1,0:T(8,128)(2,1)S(1)}, bf16[64,1792]{1,0:T(8,128)(2,1)S(1)}, u32[]{:S(2)}, u32[]{:S(2)}) collective-permute-start(bf16[64,1792]{1,0:T(8,128)(2,1)S(1)} %get-tuple-element.35.refs_3_.refs_1_), channel_id=1, source_target_pairs={{0,2},{1,3},{2,0},{3,1},{4,6},{5,7},{6,4},{7,5},{8,10},{9,11},{10,... | collective-permute-start | bytes 688136 | tf_op jit(solution)/shard_map/ppermute | solution.py:477
  14.3 0.0 copy-start
  14.3 0.0 copy-start.1
  14.3 0.0 copy-start.2
  14.3 0.0 copy-start.3
  14.4 0.0 copy-start.4
  14.4 0.0 copy-start.5
  14.4 2.5 %shard_map.116 = (bf16[16,1792]{1,0:T(8,128)(2,1)S(1)}, bf16[16,1792]{1,0:T(8,128)(2,1)S(1)}, bf16[16,1792]{1,0:T(8,128)(2,1)S(1)}, bf16[16,1792]{1,0:T(8,128)(2,1)S(1)}) custom-call(bf16[1,2,1,64,1408]{4,3,2,1,0:T(8,128)(2,1)S(1)} %get-tuple-element.38.refs_0_.refs_1_, bf16[1792,1408]{1,0:T(8,128)(2,1)S(1)} %shard_map.114.refs_0_.refs_1_.refs_2_, ...), custom_call_target="tpu_custom_call" | custom-call | flops 484442112 | bytes 7569408 | tf_op jit(solution)/shard_map/pallas_call | solution.py:27
  16.9 0.1 collective-permute-start.7
  17.0 1.6 %collective-permute-start.8 = (bf16[16,1792]{1,0:T(8,128)(2,1)S(1)}, bf16[16,1792]{1,0:T(8,128)(2,1)S(1)}, u32[]{:S(2)}, u32[]{:S(2)}) collective-permute-start(bf16[16,1792]{1,0:T(8,128)(2,1)S(1)} %get-tuple-element.42), channel_id=1, source_target_pairs={{0,8},{4,12},{8,0},{12,4},{1,9},{5,13},{9,1},{13,5},{2,10},{6,14},... | collective-permute-start | bytes 172040 | tf_op jit(solution)/shard_map/ppermute | solution.py:477
  18.5 0.3 collective-permute-start.9
  18.8 0.0 collective-permute-done.7.refs_10_
  18.8 2.5 %collective-permute-done.8.refs_11_ = bf16[16,1792]{1,0:T(8,128)(2,1)S(1)} collective-permute-done((bf16[16,1792]{1,0:T(8,128)(2,1)S(1)}, bf16[16,1792]{1,0:T(8,128)(2,1)S(1)}, u32[]{:S(2)}, u32[]{:S(2)}) %collective-permute-start.8) | collective-permute-done | bytes 57376 | tf_op jit(solution)/shard_map/ppermute | solution.py:477
  21.3 1.1 %collective-permute-done.9.refs_12_ = bf16[16,1792]{1,0:T(8,128)(2,1)S(1)} collective-permute-done((bf16[16,1792]{1,0:T(8,128)(2,1)S(1)}, bf16[16,1792]{1,0:T(8,128)(2,1)S(1)}, u32[]{:S(2)}, u32[]{:S(2)}) %collective-permute-start.9) | collective-permute-done | bytes 57376 | tf_op jit(solution)/shard_map/ppermute | solution.py:477
  22.4 0.6 %collective-permute-done.6.refs_1_.refs_4_ = bf16[64,1792]{1,0:T(8,128)(2,1)S(1)} collective-permute-done((bf16[64,1792]{1,0:T(8,128)(2,1)S(1)}, bf16[64,1792]{1,0:T(8,128)(2,1)S(1)}, u32[]{:S(2)}, u32[]{:S(2)}) %collective-permute-start.6) | collective-permute-done | bytes 229408 | tf_op jit(solution)/shard_map/ppermute | solution.py:477
  23.0 0.9 %collective-permute-done.4.refs_0_.refs_2_ = bf16[80,1792]{1,0:T(8,128)(2,1)S(1)} collective-permute-done((bf16[80,1792]{1,0:T(8,128)(2,1)S(1)}, bf16[80,1792]{1,0:T(8,128)(2,1)S(1)}, u32[]{:S(2)}, u32[]{:S(2)}) %collective-permute-start.4) | collective-permute-done | bytes 286752 | tf_op jit(solution)/shard_map/ppermute | solution.py:477
  23.9 0.0 copy-done
  23.9 0.0 copy-done.1
  23.9 0.0 copy-done.2
  23.9 0.0 copy-done.3
  23.9 0.0 copy-done.4
  23.9 0.0 copy-done.5
  23.9 0.7 %shard_map.117 = (bf16[64,1792]{1,0:T(8,128)(2,1)S(1)}, bf16[16,1792]{1,0:T(8,128)(2,1)S(1)}, bf16[16,1792]{1,0:T(8,128)(2,1)S(1)}, bf16[16,1792]{1,0:T(8,128)(2,1)S(1)}, bf16[16,1792]{1,0:T(8,128)(2,1)S(1)}) custom-call(bf16[80,1792]{1,0:T(8,128)(2,1)S(1)} %collective-permute-done.4.refs_0_.refs_2_, ...), custom_call_target="tpu_custom_call" | custom-call | bytes 1835008 | tf_op jit(solution)/shard_map/pallas_call | solution.py:27
  24.6 0.2 collective-permute-start.11
  24.8 2.0 %collective-permute-start.12 = (bf16[16,1792]{1,0:T(8,128)(2,1)S(1)}, bf16[16,1792]{1,0:T(8,128)(2,1)S(1)}, u32[]{:S(2)}, u32[]{:S(2)}) collective-permute-start(bf16[16,1792]{1,0:T(8,128)(2,1)S(1)} %get-tuple-element.46), channel_id=1, source_target_pairs={{0,24},{4,28},{8,16},{12,20},{16,8},{20,12},{24,0},{28,4},{1,25},{... | collective-permute-start | bytes 172040 | tf_op jit(solution)/shard_map/ppermute | solution.py:489
  26.8 1.4 %collective-permute-start.13 = (bf16[16,1792]{1,0:T(8,128)(2,1)S(1)}, bf16[16,1792]{1,0:T(8,128)(2,1)S(1)}, u32[]{:S(2)}, u32[]{:S(2)}) collective-permute-start(bf16[16,1792]{1,0:T(8,128)(2,1)S(1)} %get-tuple-element.47), channel_id=1, source_target_pairs={{0,28},{4,24},{8,20},{12,16},{16,12},{20,8},{24,4},{28,0},{1,29},{... | collective-permute-start | bytes 172040 | tf_op jit(solution)/shard_map/ppermute | solution.py:489
  28.3 0.8 %collective-permute-start.10 = (bf16[16,1792]{1,0:T(8,128)(2,1)S(1)}, bf16[16,1792]{1,0:T(8,128)(2,1)S(1)}, u32[]{:S(2)}, u32[]{:S(2)}) collective-permute-start(bf16[16,1792]{1,0:T(8,128)(2,1)S(1)} %get-tuple-element.44.refs_0_), channel_id=1, source_target_pairs={{0,16},{4,20},{8,24},{12,28},{16,0},{20,4},{24,8},{28,12},{1,17},{... | collective-permute-start | bytes 172040 | tf_op jit(solution)/shard_map/ppermute | solution.py:489
  29.1 2.7 %collective-permute-start.17 = (bf16[64,1792]{1,0:T(8,128)(2,1)S(1)}, bf16[64,1792]{1,0:T(8,128)(2,1)S(1)}, u32[]{:S(2)}, u32[]{:S(2)}) collective-permute-start(bf16[64,1792]{1,0:T(8,128)(2,1)S(1)} %shard_map.120), channel_id=1, source_target_pairs={{0,1},{1,0},{2,3},{3,2},{4,5},{5,4},{6,7},{7,6},{8,9},{9,8},{10,11... | collective-permute-start | bytes 688136 | tf_op jit(solution)/shard_map/ppermute | solution.py:477
  31.8 0.0 collective-permute-done.11.refs_1_
  31.8 0.0 collective-permute-done.12.refs_2_
  31.8 0.0 collective-permute-done.13.refs_3_
  31.8 1.2 %collective-permute-done.10.refs_0_ = bf16[16,1792]{1,0:T(8,128)(2,1)S(1)} collective-permute-done((bf16[16,1792]{1,0:T(8,128)(2,1)S(1)}, bf16[16,1792]{1,0:T(8,128)(2,1)S(1)}, u32[]{:S(2)}, u32[]{:S(2)}) %collective-permute-start.10) | collective-permute-done | bytes 57376 | tf_op jit(solution)/shard_map/ppermute | solution.py:489
  33.0 2.7 %collective-permute-start.15 = (bf16[64,1792]{1,0:T(8,128)(2,1)S(1)}, bf16[64,1792]{1,0:T(8,128)(2,1)S(1)}, u32[]{:S(2)}, u32[]{:S(2)}) collective-permute-start(bf16[64,1792]{1,0:T(8,128)(2,1)S(1)} %shard_map.118.refs_5_.refs_4_), channel_id=1, source_target_pairs={{0,2},{1,3},{2,0},{3,1},{4,6},{5,7},{6,4},{7,5},{8,10},{9,11},{10,... | collective-permute-start | bytes 688136 | tf_op jit(solution)/shard_map/ppermute | solution.py:477
  35.6 1.6 %collective-permute-start.14 = (bf16[64,1792]{1,0:T(8,128)(2,1)S(1)}, bf16[64,1792]{1,0:T(8,128)(2,1)S(1)}, u32[]{:S(2)}, u32[]{:S(2)}) collective-permute-start(bf16[64,1792]{1,0:T(8,128)(2,1)S(1)} %shard_map.118.refs_5_.refs_4_), channel_id=1, source_target_pairs={{0,1},{1,0},{2,3},{3,2},{4,5},{5,4},{6,7},{7,6},{8,9},{9,8},{10,11... | collective-permute-start | bytes 688136 | tf_op jit(solution)/shard_map/ppermute | solution.py:477
  37.2 2.5 %collective-permute-done.17.refs_0_.refs_2_ = bf16[64,1792]{1,0:T(8,128)(2,1)S(1)} collective-permute-done((bf16[64,1792]{1,0:T(8,128)(2,1)S(1)}, bf16[64,1792]{1,0:T(8,128)(2,1)S(1)}, u32[]{:S(2)}, u32[]{:S(2)}) %collective-permute-start.17) | collective-permute-done | bytes 229408 | tf_op jit(solution)/shard_map/ppermute | solution.py:477
  39.7 2.5 %shard_map.121 = (bf16[32,1792]{1,0:T(8,128)(2,1)S(1)}, bf16[32,1792]{1,0:T(8,128)(2,1)S(1)}) custom-call(bf16[64,1792]{1,0:T(8,128)(2,1)S(1)} %collective-permute-done.17.refs_0_.refs_2_, bf16[1,2,1,64,1408]{4,3,2,1,0:T(8,128)(2,1)S(1)} %get-tuple-element.38.refs_0_.refs_1_, bf16[1792,1408]{1,0:T(8,128)(2,1)S(1)} %shard_map.114.refs_0_.refs_1_.refs_2_, ...), custom_call_target="tpu_custom_call" | custom-call | flops 484442112 | bytes 7569408 | tf_op jit(solution)/shard_map/pallas_call | solution.py:27
  42.3 0.1 collective-permute-start.18
  42.3 0.9 %collective-permute-start.16 = (bf16[64,1792]{1,0:T(8,128)(2,1)S(1)}, bf16[64,1792]{1,0:T(8,128)(2,1)S(1)}, u32[]{:S(2)}, u32[]{:S(2)}) collective-permute-start(bf16[64,1792]{1,0:T(8,128)(2,1)S(1)} %get-tuple-element.48.refs_1_), channel_id=1, source_target_pairs={{0,16},{16,0},{1,17},{17,1},{2,18},{18,2},{3,19},{19,3},{4,20},{20... | collective-permute-start | bytes 688136 | tf_op jit(solution)/shard_map/ppermute | solution.py:596
  43.2 3.3 %collective-permute-done.15.refs_7_ = bf16[64,1792]{1,0:T(8,128)(2,1)S(1)} collective-permute-done((bf16[64,1792]{1,0:T(8,128)(2,1)S(1)}, bf16[64,1792]{1,0:T(8,128)(2,1)S(1)}, u32[]{:S(2)}, u32[]{:S(2)}) %collective-permute-start.15) | collective-permute-done | bytes 229408 | tf_op jit(solution)/shard_map/ppermute | solution.py:477
  46.5 0.7 %collective-permute-start.21 = (bf16[64,1792]{1,0:T(8,128)(2,1)S(1)}, bf16[64,1792]{1,0:T(8,128)(2,1)S(1)}, u32[]{:S(2)}, u32[]{:S(2)}) collective-permute-start(bf16[64,1792]{1,0:T(8,128)(2,1)S(1)} %collective-permute-done.15.refs_7_), channel_id=1, source_target_pairs={{0,1},{1,0},{2,3},{3,2},{4,5},{5,4},{6,7},{7,6},{8,9},{9,8},{10,11... | collective-permute-start | bytes 688136 | tf_op jit(solution)/shard_map/ppermute | solution.py:477
  47.2 0.0 collective-permute-done.14.refs_6_.refs_0_
  47.2 0.0 collective-permute-done.18.refs_2_.refs_9_
  47.2 1.4 %collective-permute-start.19 = (bf16[32,1792]{1,0:T(8,128)(2,1)S(1)}, bf16[32,1792]{1,0:T(8,128)(2,1)S(1)}, u32[]{:S(2)}, u32[]{:S(2)}) collective-permute-start(bf16[32,1792]{1,0:T(8,128)(2,1)S(1)} %shard_map.122), channel_id=1, source_target_pairs={{0,8},{4,12},{8,0},{12,4},{1,9},{5,13},{9,1},{13,5},{2,10},{6,14},... | collective-permute-start | bytes 344072 | tf_op jit(solution)/shard_map/ppermute | solution.py:477
  48.6 2.3 %collective-permute-start.5 = (bf16[16,1792]{1,0:T(8,128)(2,1)S(1)}, bf16[16,1792]{1,0:T(8,128)(2,1)S(1)}, u32[]{:S(2)}, u32[]{:S(2)}) collective-permute-start(bf16[16,1792]{1,0:T(8,128)(2,1)S(1)} %get-tuple-element.37), channel_id=1, source_target_pairs={{0,2},{1,3},{2,0},{3,1},{4,6},{5,7},{6,4},{7,5},{8,10},{9,11},{10,... | collective-permute-start | bytes 172040 | tf_op jit(solution)/shard_map/ppermute | solution.py:477
  51.0 2.5 %collective-permute-start.20 = (bf16[16,1792]{1,0:T(8,128)(2,1)S(1)}, bf16[16,1792]{1,0:T(8,128)(2,1)S(1)}, u32[]{:S(2)}, u32[]{:S(2)}) collective-permute-start(bf16[16,1792]{1,0:T(8,128)(2,1)S(1)} %get-tuple-element.53), channel_id=1, source_target_pairs={{0,3},{1,2},{2,1},{3,0},{4,7},{5,6},{6,5},{7,4},{8,11},{9,10},{10,... | collective-permute-start | bytes 172040 | tf_op jit(solution)/shard_map/ppermute | solution.py:477
  53.5 0.4 collective-permute-done.5.refs_3_
  53.9 0.5 shard_map.119.refs_0_.refs_4_
  54.4 0.0 collective-permute-done.16.refs_2_
  54.4 0.0 collective-permute-done.19.refs_10_
  54.4 1.2 %shard_map.123 = (bf16[1,2,64,1792]{3,2,1,0:T(8,128)(2,1)}, f32[8,128]{1,0:T(8,128)S(1)}) custom-call(f32[1,1,176,1792]{3,2,1,0:T(8,128)S(1)} %shard_map.119.refs_0_.refs_4_, bf16[64,1792]{1,0:T(8,128)(2,1)S(1)} %get-tuple-element.48.refs_1_, bf16[64,1792]{1,0:T(8,128)(2,1)S(1)} %collective-permute-done.16.refs_2_, bf16[64,1792]{1,0:T(8,128)(2,1)S(1)} %copy-done.2, ...), custom_call_target="tpu_custom_call" | custom-call | bytes 1835008 | tf_op jit(solution)/shard_map/pallas_call | solution.py:27
  55.6 2.2 %collective-permute-done.20.refs_1_ = bf16[16,1792]{1,0:T(8,128)(2,1)S(1)} collective-permute-done((bf16[16,1792]{1,0:T(8,128)(2,1)S(1)}, bf16[16,1792]{1,0:T(8,128)(2,1)S(1)}, u32[]{:S(2)}, u32[]{:S(2)}) %collective-permute-start.20) | collective-permute-done | bytes 57376 | tf_op jit(solution)/shard_map/ppermute | solution.py:477
  57.9 0.0 collective-permute-done.21.refs_3_
  57.9 1.3 %shard_map.124 = f32[1,1,176,1792]{3,2,1,0:T(8,128)} custom-call(f32[8,128]{1,0:T(8,128)S(1)} %get-tuple-element.52.refs_0_, bf16[16,1792]{1,0:T(8,128)(2,1)S(1)} %collective-permute-done.20.refs_1_, bf16[64,1792]{1,0:T(8,128)(2,1)S(1)} %collective-permute-done.17.refs_0_.refs_2_, bf16[64,1792]{1,0:T(8,128)(2,1)S(1)} %collective-permute-done.21.refs_3_, ...), custom_call_target="tpu_custom_call" | custom-call | flops 80740352 | bytes 2523136 | tf_op jit(solution)/shard_map/pallas_call | solution.py:27
  (4 shorter events, 0.1 us)
Async XLA Ops:
  2.7 7.3 %collective-permute-start.1 = (bf16[16,1792]{1,0:T(8,128)(2,1)S(1)}, bf16[16,1792]{1,0:T(8,128)(2,1)S(1)}, u32[]{:S(2)}, u32[]{:S(2)}) collective-permute-start(bf16[16,1792]{1,0:T(8,128)(2,1)S(1)} %get-tuple-element.32), channel_id=1, source_target_pairs={{0,4},{4,0},{8,12},{12,8},{1,5},{5,1},{9,13},{13,9},{2,6},{6,2},{1... | collective-permute-start | bytes 172040 | tf_op jit(solution)/shard_map/ppermute | solution.py:477
  3.2 6.8 %collective-permute-start.2 = (bf16[16,1792]{1,0:T(8,128)(2,1)S(1)}, bf16[16,1792]{1,0:T(8,128)(2,1)S(1)}, u32[]{:S(2)}, u32[]{:S(2)}) collective-permute-start(bf16[16,1792]{1,0:T(8,128)(2,1)S(1)} %get-tuple-element.33), channel_id=1, source_target_pairs={{0,8},{4,12},{8,0},{12,4},{1,9},{5,13},{9,1},{13,5},{2,10},{6,14},... | collective-permute-start | bytes 172040 | tf_op jit(solution)/shard_map/ppermute | solution.py:477
  5.8 4.2 %collective-permute-start.3 = (bf16[16,1792]{1,0:T(8,128)(2,1)S(1)}, bf16[16,1792]{1,0:T(8,128)(2,1)S(1)}, u32[]{:S(2)}, u32[]{:S(2)}) collective-permute-start(bf16[16,1792]{1,0:T(8,128)(2,1)S(1)} %get-tuple-element.34), channel_id=1, source_target_pairs={{0,12},{4,8},{8,4},{12,0},{1,13},{5,9},{9,5},{13,1},{2,14},{6,10},... | collective-permute-start | bytes 172040 | tf_op jit(solution)/shard_map/ppermute | solution.py:477
  5.9 4.1 %collective-permute-start = (f32[2,64]{1,0:T(2,128)S(1)}, f32[2,64]{1,0:T(2,128)S(1)}, u32[]{:S(2)}, u32[]{:S(2)}) collective-permute-start(f32[2,64]{1,0:T(2,128)S(1)} %get-tuple-element.29.refs_1_), channel_id=1, source_target_pairs={{0,16},{16,0},{1,17},{17,1},{2,18},{18,2},{3,19},{19,3},{4,20},{20... | collective-permute-start | bytes 1544 | tf_op jit(solution)/shard_map/ppermute | solution.py:558
  10.1 13.8 %collective-permute-start.4 = (bf16[80,1792]{1,0:T(8,128)(2,1)S(1)}, bf16[80,1792]{1,0:T(8,128)(2,1)S(1)}, u32[]{:S(2)}, u32[]{:S(2)}) collective-permute-start(bf16[80,1792]{1,0:T(8,128)(2,1)S(1)} %get-tuple-element.36), channel_id=1, source_target_pairs={{0,1},{1,0},{2,3},{3,2},{4,5},{5,4},{6,7},{7,6},{8,9},{9,8},{10,11... | collective-permute-start | bytes 860168 | tf_op jit(solution)/shard_map/ppermute | solution.py:477
  11.8 11.3 %collective-permute-start.6 = (bf16[64,1792]{1,0:T(8,128)(2,1)S(1)}, bf16[64,1792]{1,0:T(8,128)(2,1)S(1)}, u32[]{:S(2)}, u32[]{:S(2)}) collective-permute-start(bf16[64,1792]{1,0:T(8,128)(2,1)S(1)} %get-tuple-element.35.refs_3_.refs_1_), channel_id=1, source_target_pairs={{0,2},{1,3},{2,0},{3,1},{4,6},{5,7},{6,4},{7,5},{8,10},{9,11},{10,... | collective-permute-start | bytes 688136 | tf_op jit(solution)/shard_map/ppermute | solution.py:477
  14.3 9.6 %copy-start = (bf16[1,2,64,1792]{3,2,1,0:T(8,128)(2,1)S(1)}, bf16[1,2,64,1792]{3,2,1,0:T(8,128)(2,1)}, u32[]{:S(2)}) copy-start(bf16[1,2,64,1792]{3,2,1,0:T(8,128)(2,1)} %refs_4_.5) | copy-start | bytes 1376260
  14.3 9.6 %copy-start.1 = (bf16[1,64,1792]{2,1,0:T(8,128)(2,1)S(1)}, bf16[1,64,1792]{2,1,0:T(8,128)(2,1)}, u32[]{:S(2)}) copy-start(bf16[1,64,1792]{2,1,0:T(8,128)(2,1)} %param.10) | copy-start | bytes 688132
  14.3 9.6 %copy-start.2 = (bf16[64,1792]{1,0:T(8,128)(2,1)S(1)}, bf16[64,1792]{1,0:T(8,128)(2,1)}, u32[]{:S(2)}) copy-start(bf16[64,1792]{1,0:T(8,128)(2,1)} %refs_3_.3) | copy-start | bytes 688132
  14.3 9.6 %copy-start.3 = (f32[1,1792]{1,0:T(1,128)S(1)}, f32[1,1792]{1,0:T(1,128)}, u32[]{:S(2)}) copy-start(f32[1,1792]{1,0:T(1,128)} %refs_5_.3) | copy-start | bytes 21508
  14.4 9.6 %copy-start.4 = (s32[1,2,64,1]{2,3,1,0:T(1,128)S(1)}, s32[1,2,64,1]{2,3,1,0:T(1,128)}, u32[]{:S(2)}) copy-start(s32[1,2,64,1]{2,3,1,0:T(1,128)} %param.14) | copy-start | bytes 1540
  14.4 9.6 %copy-start.5 = (s32[1,2,64,1]{2,3,1,0:T(1,128)S(1)}, s32[1,2,64,1]{2,3,1,0:T(1,128)}, u32[]{:S(2)}) copy-start(s32[1,2,64,1]{2,3,1,0:T(1,128)} %param.15) | copy-start | bytes 1540
  16.9 1.9 %collective-permute-start.7 = (bf16[16,1792]{1,0:T(8,128)(2,1)S(1)}, bf16[16,1792]{1,0:T(8,128)(2,1)S(1)}, u32[]{:S(2)}, u32[]{:S(2)}) collective-permute-start(bf16[16,1792]{1,0:T(8,128)(2,1)S(1)} %get-tuple-element.41), channel_id=1, source_target_pairs={{0,4},{4,0},{8,12},{12,8},{1,5},{5,1},{9,13},{13,9},{2,6},{6,2},{1... | collective-permute-start | bytes 172040 | tf_op jit(solution)/shard_map/ppermute | solution.py:477
  17.0 4.3 %collective-permute-start.8 = (bf16[16,1792]{1,0:T(8,128)(2,1)S(1)}, bf16[16,1792]{1,0:T(8,128)(2,1)S(1)}, u32[]{:S(2)}, u32[]{:S(2)}) collective-permute-start(bf16[16,1792]{1,0:T(8,128)(2,1)S(1)} %get-tuple-element.42), channel_id=1, source_target_pairs={{0,8},{4,12},{8,0},{12,4},{1,9},{5,13},{9,1},{13,5},{2,10},{6,14},... | collective-permute-start | bytes 172040 | tf_op jit(solution)/shard_map/ppermute | solution.py:477
  18.5 3.9 %collective-permute-start.9 = (bf16[16,1792]{1,0:T(8,128)(2,1)S(1)}, bf16[16,1792]{1,0:T(8,128)(2,1)S(1)}, u32[]{:S(2)}, u32[]{:S(2)}) collective-permute-start(bf16[16,1792]{1,0:T(8,128)(2,1)S(1)} %get-tuple-element.43), channel_id=1, source_target_pairs={{0,12},{4,8},{8,4},{12,0},{1,13},{5,9},{9,5},{13,1},{2,14},{6,10},... | collective-permute-start | bytes 172040 | tf_op jit(solution)/shard_map/ppermute | solution.py:477
  24.6 7.1 %collective-permute-start.11 = (bf16[16,1792]{1,0:T(8,128)(2,1)S(1)}, bf16[16,1792]{1,0:T(8,128)(2,1)S(1)}, u32[]{:S(2)}, u32[]{:S(2)}) collective-permute-start(bf16[16,1792]{1,0:T(8,128)(2,1)S(1)} %get-tuple-element.45), channel_id=1, source_target_pairs={{0,20},{4,16},{8,28},{12,24},{16,4},{20,0},{24,12},{28,8},{1,21},{... | collective-permute-start | bytes 172040 | tf_op jit(solution)/shard_map/ppermute | solution.py:489
  24.8 6.9 %collective-permute-start.12 = (bf16[16,1792]{1,0:T(8,128)(2,1)S(1)}, bf16[16,1792]{1,0:T(8,128)(2,1)S(1)}, u32[]{:S(2)}, u32[]{:S(2)}) collective-permute-start(bf16[16,1792]{1,0:T(8,128)(2,1)S(1)} %get-tuple-element.46), channel_id=1, source_target_pairs={{0,24},{4,28},{8,16},{12,20},{16,8},{20,12},{24,0},{28,4},{1,25},{... | collective-permute-start | bytes 172040 | tf_op jit(solution)/shard_map/ppermute | solution.py:489
  26.8 4.9 %collective-permute-start.13 = (bf16[16,1792]{1,0:T(8,128)(2,1)S(1)}, bf16[16,1792]{1,0:T(8,128)(2,1)S(1)}, u32[]{:S(2)}, u32[]{:S(2)}) collective-permute-start(bf16[16,1792]{1,0:T(8,128)(2,1)S(1)} %get-tuple-element.47), channel_id=1, source_target_pairs={{0,28},{4,24},{8,20},{12,16},{16,12},{20,8},{24,4},{28,0},{1,29},{... | collective-permute-start | bytes 172040 | tf_op jit(solution)/shard_map/ppermute | solution.py:489
  28.3 4.7 %collective-permute-start.10 = (bf16[16,1792]{1,0:T(8,128)(2,1)S(1)}, bf16[16,1792]{1,0:T(8,128)(2,1)S(1)}, u32[]{:S(2)}, u32[]{:S(2)}) collective-permute-start(bf16[16,1792]{1,0:T(8,128)(2,1)S(1)} %get-tuple-element.44.refs_0_), channel_id=1, source_target_pairs={{0,16},{4,20},{8,24},{12,28},{16,0},{20,4},{24,8},{28,12},{1,17},{... | collective-permute-start | bytes 172040 | tf_op jit(solution)/shard_map/ppermute | solution.py:489
  29.1 10.7 %collective-permute-start.17 = (bf16[64,1792]{1,0:T(8,128)(2,1)S(1)}, bf16[64,1792]{1,0:T(8,128)(2,1)S(1)}, u32[]{:S(2)}, u32[]{:S(2)}) collective-permute-start(bf16[64,1792]{1,0:T(8,128)(2,1)S(1)} %shard_map.120), channel_id=1, source_target_pairs={{0,1},{1,0},{2,3},{3,2},{4,5},{5,4},{6,7},{7,6},{8,9},{9,8},{10,11... | collective-permute-start | bytes 688136 | tf_op jit(solution)/shard_map/ppermute | solution.py:477
  33.0 13.5 %collective-permute-start.15 = (bf16[64,1792]{1,0:T(8,128)(2,1)S(1)}, bf16[64,1792]{1,0:T(8,128)(2,1)S(1)}, u32[]{:S(2)}, u32[]{:S(2)}) collective-permute-start(bf16[64,1792]{1,0:T(8,128)(2,1)S(1)} %shard_map.118.refs_5_.refs_4_), channel_id=1, source_target_pairs={{0,2},{1,3},{2,0},{3,1},{4,6},{5,7},{6,4},{7,5},{8,10},{9,11},{10,... | collective-permute-start | bytes 688136 | tf_op jit(solution)/shard_map/ppermute | solution.py:477
  35.6 11.5 %collective-permute-start.14 = (bf16[64,1792]{1,0:T(8,128)(2,1)S(1)}, bf16[64,1792]{1,0:T(8,128)(2,1)S(1)}, u32[]{:S(2)}, u32[]{:S(2)}) collective-permute-start(bf16[64,1792]{1,0:T(8,128)(2,1)S(1)} %shard_map.118.refs_5_.refs_4_), channel_id=1, source_target_pairs={{0,1},{1,0},{2,3},{3,2},{4,5},{5,4},{6,7},{7,6},{8,9},{9,8},{10,11... | collective-permute-start | bytes 688136 | tf_op jit(solution)/shard_map/ppermute | solution.py:477
  42.3 4.9 %collective-permute-start.18 = (bf16[32,1792]{1,0:T(8,128)(2,1)S(1)}, bf16[32,1792]{1,0:T(8,128)(2,1)S(1)}, u32[]{:S(2)}, u32[]{:S(2)}) collective-permute-start(bf16[32,1792]{1,0:T(8,128)(2,1)S(1)} %get-tuple-element.50), channel_id=1, source_target_pairs={{0,4},{4,0},{8,12},{12,8},{1,5},{5,1},{9,13},{13,9},{2,6},{6,2},{1... | collective-permute-start | bytes 344072 | tf_op jit(solution)/shard_map/ppermute | solution.py:477
  42.3 12.1 %collective-permute-start.16 = (bf16[64,1792]{1,0:T(8,128)(2,1)S(1)}, bf16[64,1792]{1,0:T(8,128)(2,1)S(1)}, u32[]{:S(2)}, u32[]{:S(2)}) collective-permute-start(bf16[64,1792]{1,0:T(8,128)(2,1)S(1)} %get-tuple-element.48.refs_1_), channel_id=1, source_target_pairs={{0,16},{16,0},{1,17},{17,1},{2,18},{18,2},{3,19},{19,3},{4,20},{20... | collective-permute-start | bytes 688136 | tf_op jit(solution)/shard_map/ppermute | solution.py:596
  46.5 11.3 %collective-permute-start.21 = (bf16[64,1792]{1,0:T(8,128)(2,1)S(1)}, bf16[64,1792]{1,0:T(8,128)(2,1)S(1)}, u32[]{:S(2)}, u32[]{:S(2)}) collective-permute-start(bf16[64,1792]{1,0:T(8,128)(2,1)S(1)} %collective-permute-done.15.refs_7_), channel_id=1, source_target_pairs={{0,1},{1,0},{2,3},{3,2},{4,5},{5,4},{6,7},{7,6},{8,9},{9,8},{10,11... | collective-permute-start | bytes 688136 | tf_op jit(solution)/shard_map/ppermute | solution.py:477
  47.2 7.2 %collective-permute-start.19 = (bf16[32,1792]{1,0:T(8,128)(2,1)S(1)}, bf16[32,1792]{1,0:T(8,128)(2,1)S(1)}, u32[]{:S(2)}, u32[]{:S(2)}) collective-permute-start(bf16[32,1792]{1,0:T(8,128)(2,1)S(1)} %shard_map.122), channel_id=1, source_target_pairs={{0,8},{4,12},{8,0},{12,4},{1,9},{5,13},{9,1},{13,5},{2,10},{6,14},... | collective-permute-start | bytes 344072 | tf_op jit(solution)/shard_map/ppermute | solution.py:477
  48.6 5.2 %collective-permute-start.5 = (bf16[16,1792]{1,0:T(8,128)(2,1)S(1)}, bf16[16,1792]{1,0:T(8,128)(2,1)S(1)}, u32[]{:S(2)}, u32[]{:S(2)}) collective-permute-start(bf16[16,1792]{1,0:T(8,128)(2,1)S(1)} %get-tuple-element.37), channel_id=1, source_target_pairs={{0,2},{1,3},{2,0},{3,1},{4,6},{5,7},{6,4},{7,5},{8,10},{9,11},{10,... | collective-permute-start | bytes 172040 | tf_op jit(solution)/shard_map/ppermute | solution.py:477
  51.0 6.9 %collective-permute-start.20 = (bf16[16,1792]{1,0:T(8,128)(2,1)S(1)}, bf16[16,1792]{1,0:T(8,128)(2,1)S(1)}, u32[]{:S(2)}, u32[]{:S(2)}) collective-permute-start(bf16[16,1792]{1,0:T(8,128)(2,1)S(1)} %get-tuple-element.53), channel_id=1, source_target_pairs={{0,3},{1,2},{2,1},{3,0},{4,7},{5,6},{6,5},{7,4},{8,11},{9,10},{10,... | collective-permute-start | bytes 172040 | tf_op jit(solution)/shard_map/ppermute | solution.py:477

commit v5 on v4

--- a/solution.py
+++ b/solution.py
@@ -602,7 +602,7 @@
         first = at_distance(again, "edp", 1)
         third = at_distance(second, "edp", 1)
         units = [at_distance(hidden[step], "edp", step) for step in (2, 3)]
-        arrived, late, tail = [again], (last,), (first,)
+        arrived, late, tail = [again], (last,), (first, passed)
         now = [
             (hidden[0], 0, 0, joined),
             (near, rows, 0, near),

time: 59.3 us -> 59.3 us (level)
  waiting for transfers between devices: 14.7 us -> 14.1 us
  starting transfers between devices: 30.3 us -> 30.9 us
    ppermute x16, waiting for transfers between devices: 13.5 us -> 12.9 us  [at_distance(): lax.ppermute(value, axis, [(source, source ^ step) for source in range(co...]
where the time goes in v5:
time: 59.3 us; the launch traced here: 59.1 us
  starting transfers between devices  30.9 us (52%)
  waiting for transfers between devices  14.1 us (24%)
  Pallas kernels  13.2 us (22%)
  between operations  0.82 us (1%)
    ppermute x16, starting transfers between devices, at_distance(): lax.ppermute(value, axis, [(source, source ^ step) for source in range(co...  23.7 us
    pallas_call x12, Pallas kernels, on_chip(): pl.pallas_call(run, out_shape=outs, in_specs=[there] * first + [anywhere]...  13.2 us
    ppermute x16, waiting for transfers between devices, at_distance(): lax.ppermute(value, axis, [(source, source ^ step) for source in range(co...  12.9 us
    ppermute x4, starting transfers between devices, behind(): lax.ppermute(value, ('pipe', 'expert'), [(section * count + source, (sect...  4.46 us
    ppermute x1, starting transfers between devices, local(): lax.ppermute(table, 'pipe', [(source, (source + 1) % sections) for source...  1.7 us
    ppermute x4, waiting for transfers between devices, behind(): lax.ppermute(value, ('pipe', 'expert'), [(section * count + source, (sect...  1.2 us
  transfers between devices with their start and end apart: 22, of which 9 were waited for; matrix products, arithmetic and copies ran while one was open for 0% of the time, Pallas kernels for 16%

profile of v5, /device:TPU:0, one launch (start us, length us, event | category | flops | bytes accessed | tf_op | source)
XLA Modules:
  0.0 59.1 jit_solution(3037604235264785903)
XLA Ops:
  0.6 2.1 %shard_map.113 = (f32[2,64]{1,0:T(2,128)S(1)}, bf16[1,2,1,64,1408]{4,3,2,1,0:T(8,128)(2,1)S(1)}, bf16[704,1792]{1,0:T(8,128)(2,1)S(1)}, bf16[16,1792]{1,0:T(8,12...) custom-call(bf16[64,1792]{1,0:T(8,128)(2,1)} %bitcast.12, ...), custom_call_target="tpu_custom_call" | custom-call | bytes 688128 | tf_op jit(solution)/shard_map/pallas_call | solution.py:27
  2.7 0.5 collective-permute-start.1
  3.2 2.6 %collective-permute-start.2 = (bf16[16,1792]{1,0:T(8,128)(2,1)S(1)}, bf16[16,1792]{1,0:T(8,128)(2,1)S(1)}, u32[]{:S(2)}, u32[]{:S(2)}) collective-permute-start(bf16[16,1792]{1,0:T(8,128)(2,1)S(1)} %get-tuple-element.33), channel_id=1, source_target_pairs={{0,8},{4,12},{8,0},{12,4},{1,9},{5,13},{9,1},{13,5},{2,10},{6,14},... | collective-permute-start | bytes 172040 | tf_op jit(solution)/shard_map/ppermute | solution.py:477
  5.8 0.1 collective-permute-start.3
  5.9 1.7 %collective-permute-start = (f32[2,64]{1,0:T(2,128)S(1)}, f32[2,64]{1,0:T(2,128)S(1)}, u32[]{:S(2)}, u32[]{:S(2)}) collective-permute-start(f32[2,64]{1,0:T(2,128)S(1)} %get-tuple-element.29.refs_1_), channel_id=1, source_target_pairs={{0,16},{16,0},{1,17},{17,1},{2,18},{18,2},{3,19},{19,3},{4,20},{20... | collective-permute-start | bytes 1544 | tf_op jit(solution)/shard_map/ppermute | solution.py:558
  7.6 2.4 %shard_map.114.refs_0_.refs_1_.refs_2_ = bf16[1792,1408]{1,0:T(8,128)(2,1)S(1)} custom-call(bf16[1792,1408]{1,0:T(8,128)(2,1)} %bitcast.20, f32[2,64]{1,0:T(2,128)S(1)} %get-tuple-element.29.refs_1_), custom_call_target="tpu_custom_call" | custom-call | bytes 5046272 | tf_op jit(solution)/shard_map/pallas_call | solution.py:27
  10.0 0.0 collective-permute-done.refs_1_.refs_8_
  10.0 0.0 collective-permute-done.1.refs_4_
  10.0 0.0 collective-permute-done.2.refs_5_
  10.1 0.0 collective-permute-done.3.refs_6_
  10.1 1.6 %collective-permute-start.4 = (bf16[80,1792]{1,0:T(8,128)(2,1)S(1)}, bf16[80,1792]{1,0:T(8,128)(2,1)S(1)}, u32[]{:S(2)}, u32[]{:S(2)}) collective-permute-start(bf16[80,1792]{1,0:T(8,128)(2,1)S(1)} %get-tuple-element.36), channel_id=1, source_target_pairs={{0,1},{1,0},{2,3},{3,2},{4,5},{5,4},{6,7},{7,6},{8,9},{9,8},{10,11... | collective-permute-start | bytes 860168 | tf_op jit(solution)/shard_map/ppermute | solution.py:477
  11.8 2.6 %collective-permute-start.6 = (bf16[64,1792]{1,0:T(8,128)(2,1)S(1)}, bf16[64,1792]{1,0:T(8,128)(2,1)S(1)}, u32[]{:S(2)}, u32[]{:S(2)}) collective-permute-start(bf16[64,1792]{1,0:T(8,128)(2,1)S(1)} %get-tuple-element.35.refs_3_.refs_1_), channel_id=1, source_target_pairs={{0,2},{1,3},{2,0},{3,1},{4,6},{5,7},{6,4},{7,5},{8,10},{9,11},{10,... | collective-permute-start | bytes 688136 | tf_op jit(solution)/shard_map/ppermute | solution.py:477
  14.3 0.0 copy-start
  14.3 0.0 copy-start.1
  14.3 0.0 copy-start.2
  14.3 0.0 copy-start.3
  14.4 0.0 copy-start.4
  14.4 0.0 copy-start.5
  14.4 2.5 %shard_map.116 = (bf16[16,1792]{1,0:T(8,128)(2,1)S(1)}, bf16[16,1792]{1,0:T(8,128)(2,1)S(1)}, bf16[16,1792]{1,0:T(8,128)(2,1)S(1)}, bf16[16,1792]{1,0:T(8,128)(2,1)S(1)}) custom-call(bf16[1,2,1,64,1408]{4,3,2,1,0:T(8,128)(2,1)S(1)} %get-tuple-element.38.refs_0_.refs_1_, bf16[1792,1408]{1,0:T(8,128)(2,1)S(1)} %shard_map.114.refs_0_.refs_1_.refs_2_, ...), custom_call_target="tpu_custom_call" | custom-call | flops 484442112 | bytes 7569408 | tf_op jit(solution)/shard_map/pallas_call | solution.py:27
  16.9 0.1 collective-permute-start.7
  17.0 1.6 %collective-permute-start.8 = (bf16[16,1792]{1,0:T(8,128)(2,1)S(1)}, bf16[16,1792]{1,0:T(8,128)(2,1)S(1)}, u32[]{:S(2)}, u32[]{:S(2)}) collective-permute-start(bf16[16,1792]{1,0:T(8,128)(2,1)S(1)} %get-tuple-element.42), channel_id=1, source_target_pairs={{0,8},{4,12},{8,0},{12,4},{1,9},{5,13},{9,1},{13,5},{2,10},{6,14},... | collective-permute-start | bytes 172040 | tf_op jit(solution)/shard_map/ppermute | solution.py:477
  18.5 0.3 collective-permute-start.9
  18.8 0.0 collective-permute-done.7.refs_10_
  18.8 2.5 %collective-permute-done.8.refs_11_ = bf16[16,1792]{1,0:T(8,128)(2,1)S(1)} collective-permute-done((bf16[16,1792]{1,0:T(8,128)(2,1)S(1)}, bf16[16,1792]{1,0:T(8,128)(2,1)S(1)}, u32[]{:S(2)}, u32[]{:S(2)}) %collective-permute-start.8) | collective-permute-done | bytes 57376 | tf_op jit(solution)/shard_map/ppermute | solution.py:477
  21.3 1.1 %collective-permute-done.9.refs_12_ = bf16[16,1792]{1,0:T(8,128)(2,1)S(1)} collective-permute-done((bf16[16,1792]{1,0:T(8,128)(2,1)S(1)}, bf16[16,1792]{1,0:T(8,128)(2,1)S(1)}, u32[]{:S(2)}, u32[]{:S(2)}) %collective-permute-start.9) | collective-permute-done | bytes 57376 | tf_op jit(solution)/shard_map/ppermute | solution.py:477
  22.4 0.6 %collective-permute-done.6.refs_1_.refs_4_ = bf16[64,1792]{1,0:T(8,128)(2,1)S(1)} collective-permute-done((bf16[64,1792]{1,0:T(8,128)(2,1)S(1)}, bf16[64,1792]{1,0:T(8,128)(2,1)S(1)}, u32[]{:S(2)}, u32[]{:S(2)}) %collective-permute-start.6) | collective-permute-done | bytes 229408 | tf_op jit(solution)/shard_map/ppermute | solution.py:477
  23.0 0.9 %collective-permute-done.4.refs_0_.refs_2_ = bf16[80,1792]{1,0:T(8,128)(2,1)S(1)} collective-permute-done((bf16[80,1792]{1,0:T(8,128)(2,1)S(1)}, bf16[80,1792]{1,0:T(8,128)(2,1)S(1)}, u32[]{:S(2)}, u32[]{:S(2)}) %collective-permute-start.4) | collective-permute-done | bytes 286752 | tf_op jit(solution)/shard_map/ppermute | solution.py:477
  23.9 0.0 copy-done
  23.9 0.0 copy-done.1
  23.9 0.0 copy-done.2
  23.9 0.0 copy-done.3
  23.9 0.0 copy-done.4
  23.9 0.0 copy-done.5
  23.9 0.7 %shard_map.117 = (bf16[64,1792]{1,0:T(8,128)(2,1)S(1)}, bf16[16,1792]{1,0:T(8,128)(2,1)S(1)}, bf16[16,1792]{1,0:T(8,128)(2,1)S(1)}, bf16[16,1792]{1,0:T(8,128)(2,1)S(1)}, bf16[16,1792]{1,0:T(8,128)(2,1)S(1)}) custom-call(bf16[80,1792]{1,0:T(8,128)(2,1)S(1)} %collective-permute-done.4.refs_0_.refs_2_, ...), custom_call_target="tpu_custom_call" | custom-call | bytes 1835008 | tf_op jit(solution)/shard_map/pallas_call | solution.py:27
  24.6 0.2 collective-permute-start.11
  24.8 2.0 %collective-permute-start.12 = (bf16[16,1792]{1,0:T(8,128)(2,1)S(1)}, bf16[16,1792]{1,0:T(8,128)(2,1)S(1)}, u32[]{:S(2)}, u32[]{:S(2)}) collective-permute-start(bf16[16,1792]{1,0:T(8,128)(2,1)S(1)} %get-tuple-element.46), channel_id=1, source_target_pairs={{0,24},{4,28},{8,16},{12,20},{16,8},{20,12},{24,0},{28,4},{1,25},{... | collective-permute-start | bytes 172040 | tf_op jit(solution)/shard_map/ppermute | solution.py:489
  26.8 1.4 %collective-permute-start.13 = (bf16[16,1792]{1,0:T(8,128)(2,1)S(1)}, bf16[16,1792]{1,0:T(8,128)(2,1)S(1)}, u32[]{:S(2)}, u32[]{:S(2)}) collective-permute-start(bf16[16,1792]{1,0:T(8,128)(2,1)S(1)} %get-tuple-element.47), channel_id=1, source_target_pairs={{0,28},{4,24},{8,20},{12,16},{16,12},{20,8},{24,4},{28,0},{1,29},{... | collective-permute-start | bytes 172040 | tf_op jit(solution)/shard_map/ppermute | solution.py:489
  28.3 0.8 %collective-permute-start.10 = (bf16[16,1792]{1,0:T(8,128)(2,1)S(1)}, bf16[16,1792]{1,0:T(8,128)(2,1)S(1)}, u32[]{:S(2)}, u32[]{:S(2)}) collective-permute-start(bf16[16,1792]{1,0:T(8,128)(2,1)S(1)} %get-tuple-element.44.refs_0_), channel_id=1, source_target_pairs={{0,16},{4,20},{8,24},{12,28},{16,0},{20,4},{24,8},{28,12},{1,17},{... | collective-permute-start | bytes 172040 | tf_op jit(solution)/shard_map/ppermute | solution.py:489
  29.1 2.7 %collective-permute-start.17 = (bf16[64,1792]{1,0:T(8,128)(2,1)S(1)}, bf16[64,1792]{1,0:T(8,128)(2,1)S(1)}, u32[]{:S(2)}, u32[]{:S(2)}) collective-permute-start(bf16[64,1792]{1,0:T(8,128)(2,1)S(1)} %shard_map.120), channel_id=1, source_target_pairs={{0,1},{1,0},{2,3},{3,2},{4,5},{5,4},{6,7},{7,6},{8,9},{9,8},{10,11... | collective-permute-start | bytes 688136 | tf_op jit(solution)/shard_map/ppermute | solution.py:477
  31.8 0.0 collective-permute-done.11.refs_1_
  31.8 0.0 collective-permute-done.12.refs_2_
  31.8 0.0 collective-permute-done.13.refs_3_
  31.8 1.2 %collective-permute-done.10.refs_0_ = bf16[16,1792]{1,0:T(8,128)(2,1)S(1)} collective-permute-done((bf16[16,1792]{1,0:T(8,128)(2,1)S(1)}, bf16[16,1792]{1,0:T(8,128)(2,1)S(1)}, u32[]{:S(2)}, u32[]{:S(2)}) %collective-permute-start.10) | collective-permute-done | bytes 57376 | tf_op jit(solution)/shard_map/ppermute | solution.py:489
  33.0 2.7 %collective-permute-start.15 = (bf16[64,1792]{1,0:T(8,128)(2,1)S(1)}, bf16[64,1792]{1,0:T(8,128)(2,1)S(1)}, u32[]{:S(2)}, u32[]{:S(2)}) collective-permute-start(bf16[64,1792]{1,0:T(8,128)(2,1)S(1)} %shard_map.118.refs_5_.refs_4_), channel_id=1, source_target_pairs={{0,2},{1,3},{2,0},{3,1},{4,6},{5,7},{6,4},{7,5},{8,10},{9,11},{10,... | collective-permute-start | bytes 688136 | tf_op jit(solution)/shard_map/ppermute | solution.py:477
  35.6 1.1 %collective-permute-start.16 = (bf16[64,1792]{1,0:T(8,128)(2,1)S(1)}, bf16[64,1792]{1,0:T(8,128)(2,1)S(1)}, u32[]{:S(2)}, u32[]{:S(2)}) collective-permute-start(bf16[64,1792]{1,0:T(8,128)(2,1)S(1)} %get-tuple-element.48.refs_1_), channel_id=1, source_target_pairs={{0,16},{16,0},{1,17},{17,1},{2,18},{18,2},{3,19},{19,3},{4,20},{20... | collective-permute-start | bytes 688136 | tf_op jit(solution)/shard_map/ppermute | solution.py:596
  36.7 1.6 %collective-permute-start.14 = (bf16[64,1792]{1,0:T(8,128)(2,1)S(1)}, bf16[64,1792]{1,0:T(8,128)(2,1)S(1)}, u32[]{:S(2)}, u32[]{:S(2)}) collective-permute-start(bf16[64,1792]{1,0:T(8,128)(2,1)S(1)} %shard_map.118.refs_5_.refs_4_), channel_id=1, source_target_pairs={{0,1},{1,0},{2,3},{3,2},{4,5},{5,4},{6,7},{7,6},{8,9},{9,8},{10,11... | collective-permute-start | bytes 688136 | tf_op jit(solution)/shard_map/ppermute | solution.py:477
  38.3 1.4 %collective-permute-done.17.refs_0_.refs_2_ = bf16[64,1792]{1,0:T(8,128)(2,1)S(1)} collective-permute-done((bf16[64,1792]{1,0:T(8,128)(2,1)S(1)}, bf16[64,1792]{1,0:T(8,128)(2,1)S(1)}, u32[]{:S(2)}, u32[]{:S(2)}) %collective-permute-start.17) | collective-permute-done | bytes 229408 | tf_op jit(solution)/shard_map/ppermute | solution.py:477
  39.8 2.5 %shard_map.121 = (bf16[32,1792]{1,0:T(8,128)(2,1)S(1)}, bf16[32,1792]{1,0:T(8,128)(2,1)S(1)}) custom-call(bf16[64,1792]{1,0:T(8,128)(2,1)S(1)} %collective-permute-done.17.refs_0_.refs_2_, bf16[1,2,1,64,1408]{4,3,2,1,0:T(8,128)(2,1)S(1)} %get-tuple-element.38.refs_0_.refs_1_, bf16[1792,1408]{1,0:T(8,128)(2,1)S(1)} %shard_map.114.refs_0_.refs_1_.refs_2_, ...), custom_call_target="tpu_custom_call" | custom-call | flops 484442112 | bytes 7569408 | tf_op jit(solution)/shard_map/pallas_call | solution.py:27
  42.3 0.1 collective-permute-start.18
  42.3 4.2 %collective-permute-done.15.refs_7_ = bf16[64,1792]{1,0:T(8,128)(2,1)S(1)} collective-permute-done((bf16[64,1792]{1,0:T(8,128)(2,1)S(1)}, bf16[64,1792]{1,0:T(8,128)(2,1)S(1)}, u32[]{:S(2)}, u32[]{:S(2)}) %collective-permute-start.15) | collective-permute-done | bytes 229408 | tf_op jit(solution)/shard_map/ppermute | solution.py:477
  46.5 0.7 %collective-permute-start.21 = (bf16[64,1792]{1,0:T(8,128)(2,1)S(1)}, bf16[64,1792]{1,0:T(8,128)(2,1)S(1)}, u32[]{:S(2)}, u32[]{:S(2)}) collective-permute-start(bf16[64,1792]{1,0:T(8,128)(2,1)S(1)} %collective-permute-done.15.refs_7_), channel_id=1, source_target_pairs={{0,1},{1,0},{2,3},{3,2},{4,5},{5,4},{6,7},{7,6},{8,9},{9,8},{10,11... | collective-permute-start | bytes 688136 | tf_op jit(solution)/shard_map/ppermute | solution.py:477
  47.2 0.0 collective-permute-done.16.refs_1_.refs_2_
  47.2 0.0 collective-permute-done.14.refs_6_.refs_0_
  47.2 0.0 collective-permute-done.18.refs_3_.refs_9_
  47.2 1.9 %collective-permute-start.19 = (bf16[32,1792]{1,0:T(8,128)(2,1)S(1)}, bf16[32,1792]{1,0:T(8,128)(2,1)S(1)}, u32[]{:S(2)}, u32[]{:S(2)}) collective-permute-start(bf16[32,1792]{1,0:T(8,128)(2,1)S(1)} %shard_map.122), channel_id=1, source_target_pairs={{0,8},{4,12},{8,0},{12,4},{1,9},{5,13},{9,1},{13,5},{2,10},{6,14},... | collective-permute-start | bytes 344072 | tf_op jit(solution)/shard_map/ppermute | solution.py:477
  49.1 1.9 %collective-permute-start.5 = (bf16[16,1792]{1,0:T(8,128)(2,1)S(1)}, bf16[16,1792]{1,0:T(8,128)(2,1)S(1)}, u32[]{:S(2)}, u32[]{:S(2)}) collective-permute-start(bf16[16,1792]{1,0:T(8,128)(2,1)S(1)} %get-tuple-element.37), channel_id=1, source_target_pairs={{0,2},{1,3},{2,0},{3,1},{4,6},{5,7},{6,4},{7,5},{8,10},{9,11},{10,... | collective-permute-start | bytes 172040 | tf_op jit(solution)/shard_map/ppermute | solution.py:477
  51.0 3.0 %collective-permute-start.20 = (bf16[16,1792]{1,0:T(8,128)(2,1)S(1)}, bf16[16,1792]{1,0:T(8,128)(2,1)S(1)}, u32[]{:S(2)}, u32[]{:S(2)}) collective-permute-start(bf16[16,1792]{1,0:T(8,128)(2,1)S(1)} %get-tuple-element.53), channel_id=1, source_target_pairs={{0,3},{1,2},{2,1},{3,0},{4,7},{5,6},{6,5},{7,4},{8,11},{9,10},{10,... | collective-permute-start | bytes 172040 | tf_op jit(solution)/shard_map/ppermute | solution.py:477
  53.9 0.3 collective-permute-done.5.refs_3_
  54.3 0.5 shard_map.119.refs_0_.refs_4_
  54.8 0.0 collective-permute-done.19.refs_10_
  54.8 1.2 %shard_map.123 = (bf16[1,2,64,1792]{3,2,1,0:T(8,128)(2,1)}, f32[8,128]{1,0:T(8,128)S(1)}) custom-call(f32[1,1,176,1792]{3,2,1,0:T(8,128)S(1)} %shard_map.119.refs_0_.refs_4_, bf16[64,1792]{1,0:T(8,128)(2,1)S(1)} %get-tuple-element.48.refs_1_, bf16[64,1792]{1,0:T(8,128)(2,1)S(1)} %collective-permute-done.16.refs_1_.refs_2_, bf16[64,1792]{1,0:T(8,128)(2,1)S(1)} %copy-done.2, ...), custom_call_target="tpu_custom_call" | custom-call | bytes 1835008 | tf_op jit(solution)/shard_map/pallas_call | solution.py:27
  56.0 1.8 %collective-permute-done.20.refs_1_ = bf16[16,1792]{1,0:T(8,128)(2,1)S(1)} collective-permute-done((bf16[16,1792]{1,0:T(8,128)(2,1)S(1)}, bf16[16,1792]{1,0:T(8,128)(2,1)S(1)}, u32[]{:S(2)}, u32[]{:S(2)}) %collective-permute-start.20) | collective-permute-done | bytes 57376 | tf_op jit(solution)/shard_map/ppermute | solution.py:477
  57.9 0.0 collective-permute-done.21.refs_3_
  57.9 1.3 %shard_map.124 = f32[1,1,176,1792]{3,2,1,0:T(8,128)} custom-call(f32[8,128]{1,0:T(8,128)S(1)} %get-tuple-element.52.refs_0_, bf16[16,1792]{1,0:T(8,128)(2,1)S(1)} %collective-permute-done.20.refs_1_, bf16[64,1792]{1,0:T(8,128)(2,1)S(1)} %collective-permute-done.17.refs_0_.refs_2_, bf16[64,1792]{1,0:T(8,128)(2,1)S(1)} %collective-permute-done.21.refs_3_, ...), custom_call_target="tpu_custom_call" | custom-call | flops 80740352 | bytes 2523136 | tf_op jit(solution)/shard_map/pallas_call | solution.py:27
  (4 shorter events, 0.1 us)
Async XLA Ops:
  2.7 7.3 %collective-permute-start.1 = (bf16[16,1792]{1,0:T(8,128)(2,1)S(1)}, bf16[16,1792]{1,0:T(8,128)(2,1)S(1)}, u32[]{:S(2)}, u32[]{:S(2)}) collective-permute-start(bf16[16,1792]{1,0:T(8,128)(2,1)S(1)} %get-tuple-element.32), channel_id=1, source_target_pairs={{0,4},{4,0},{8,12},{12,8},{1,5},{5,1},{9,13},{13,9},{2,6},{6,2},{1... | collective-permute-start | bytes 172040 | tf_op jit(solution)/shard_map/ppermute | solution.py:477
  3.2 6.8 %collective-permute-start.2 = (bf16[16,1792]{1,0:T(8,128)(2,1)S(1)}, bf16[16,1792]{1,0:T(8,128)(2,1)S(1)}, u32[]{:S(2)}, u32[]{:S(2)}) collective-permute-start(bf16[16,1792]{1,0:T(8,128)(2,1)S(1)} %get-tuple-element.33), channel_id=1, source_target_pairs={{0,8},{4,12},{8,0},{12,4},{1,9},{5,13},{9,1},{13,5},{2,10},{6,14},... | collective-permute-start | bytes 172040 | tf_op jit(solution)/shard_map/ppermute | solution.py:477
  5.8 4.2 %collective-permute-start.3 = (bf16[16,1792]{1,0:T(8,128)(2,1)S(1)}, bf16[16,1792]{1,0:T(8,128)(2,1)S(1)}, u32[]{:S(2)}, u32[]{:S(2)}) collective-permute-start(bf16[16,1792]{1,0:T(8,128)(2,1)S(1)} %get-tuple-element.34), channel_id=1, source_target_pairs={{0,12},{4,8},{8,4},{12,0},{1,13},{5,9},{9,5},{13,1},{2,14},{6,10},... | collective-permute-start | bytes 172040 | tf_op jit(solution)/shard_map/ppermute | solution.py:477
  5.9 4.1 %collective-permute-start = (f32[2,64]{1,0:T(2,128)S(1)}, f32[2,64]{1,0:T(2,128)S(1)}, u32[]{:S(2)}, u32[]{:S(2)}) collective-permute-start(f32[2,64]{1,0:T(2,128)S(1)} %get-tuple-element.29.refs_1_), channel_id=1, source_target_pairs={{0,16},{16,0},{1,17},{17,1},{2,18},{18,2},{3,19},{19,3},{4,20},{20... | collective-permute-start | bytes 1544 | tf_op jit(solution)/shard_map/ppermute | solution.py:558
  10.1 13.8 %collective-permute-start.4 = (bf16[80,1792]{1,0:T(8,128)(2,1)S(1)}, bf16[80,1792]{1,0:T(8,128)(2,1)S(1)}, u32[]{:S(2)}, u32[]{:S(2)}) collective-permute-start(bf16[80,1792]{1,0:T(8,128)(2,1)S(1)} %get-tuple-element.36), channel_id=1, source_target_pairs={{0,1},{1,0},{2,3},{3,2},{4,5},{5,4},{6,7},{7,6},{8,9},{9,8},{10,11... | collective-permute-start | bytes 860168 | tf_op jit(solution)/shard_map/ppermute | solution.py:477
  11.8 11.3 %collective-permute-start.6 = (bf16[64,1792]{1,0:T(8,128)(2,1)S(1)}, bf16[64,1792]{1,0:T(8,128)(2,1)S(1)}, u32[]{:S(2)}, u32[]{:S(2)}) collective-permute-start(bf16[64,1792]{1,0:T(8,128)(2,1)S(1)} %get-tuple-element.35.refs_3_.refs_1_), channel_id=1, source_target_pairs={{0,2},{1,3},{2,0},{3,1},{4,6},{5,7},{6,4},{7,5},{8,10},{9,11},{10,... | collective-permute-start | bytes 688136 | tf_op jit(solution)/shard_map/ppermute | solution.py:477
  14.3 9.6 %copy-start = (bf16[1,2,64,1792]{3,2,1,0:T(8,128)(2,1)S(1)}, bf16[1,2,64,1792]{3,2,1,0:T(8,128)(2,1)}, u32[]{:S(2)}) copy-start(bf16[1,2,64,1792]{3,2,1,0:T(8,128)(2,1)} %refs_4_.5) | copy-start | bytes 1376260
  14.3 9.6 %copy-start.1 = (bf16[1,64,1792]{2,1,0:T(8,128)(2,1)S(1)}, bf16[1,64,1792]{2,1,0:T(8,128)(2,1)}, u32[]{:S(2)}) copy-start(bf16[1,64,1792]{2,1,0:T(8,128)(2,1)} %param.10) | copy-start | bytes 688132
  14.3 9.6 %copy-start.2 = (bf16[64,1792]{1,0:T(8,128)(2,1)S(1)}, bf16[64,1792]{1,0:T(8,128)(2,1)}, u32[]{:S(2)}) copy-start(bf16[64,1792]{1,0:T(8,128)(2,1)} %refs_3_.3) | copy-start | bytes 688132
  14.3 9.6 %copy-start.3 = (f32[1,1792]{1,0:T(1,128)S(1)}, f32[1,1792]{1,0:T(1,128)}, u32[]{:S(2)}) copy-start(f32[1,1792]{1,0:T(1,128)} %refs_5_.3) | copy-start | bytes 21508
  14.4 9.6 %copy-start.4 = (s32[1,2,64,1]{2,3,1,0:T(1,128)S(1)}, s32[1,2,64,1]{2,3,1,0:T(1,128)}, u32[]{:S(2)}) copy-start(s32[1,2,64,1]{2,3,1,0:T(1,128)} %param.14) | copy-start | bytes 1540
  14.4 9.6 %copy-start.5 = (s32[1,2,64,1]{2,3,1,0:T(1,128)S(1)}, s32[1,2,64,1]{2,3,1,0:T(1,128)}, u32[]{:S(2)}) copy-start(s32[1,2,64,1]{2,3,1,0:T(1,128)} %param.15) | copy-start | bytes 1540
  16.9 1.9 %collective-permute-start.7 = (bf16[16,1792]{1,0:T(8,128)(2,1)S(1)}, bf16[16,1792]{1,0:T(8,128)(2,1)S(1)}, u32[]{:S(2)}, u32[]{:S(2)}) collective-permute-start(bf16[16,1792]{1,0:T(8,128)(2,1)S(1)} %get-tuple-element.41), channel_id=1, source_target_pairs={{0,4},{4,0},{8,12},{12,8},{1,5},{5,1},{9,13},{13,9},{2,6},{6,2},{1... | collective-permute-start | bytes 172040 | tf_op jit(solution)/shard_map/ppermute | solution.py:477
  17.0 4.3 %collective-permute-start.8 = (bf16[16,1792]{1,0:T(8,128)(2,1)S(1)}, bf16[16,1792]{1,0:T(8,128)(2,1)S(1)}, u32[]{:S(2)}, u32[]{:S(2)}) collective-permute-start(bf16[16,1792]{1,0:T(8,128)(2,1)S(1)} %get-tuple-element.42), channel_id=1, source_target_pairs={{0,8},{4,12},{8,0},{12,4},{1,9},{5,13},{9,1},{13,5},{2,10},{6,14},... | collective-permute-start | bytes 172040 | tf_op jit(solution)/shard_map/ppermute | solution.py:477
  18.5 3.9 %collective-permute-start.9 = (bf16[16,1792]{1,0:T(8,128)(2,1)S(1)}, bf16[16,1792]{1,0:T(8,128)(2,1)S(1)}, u32[]{:S(2)}, u32[]{:S(2)}) collective-permute-start(bf16[16,1792]{1,0:T(8,128)(2,1)S(1)} %get-tuple-element.43), channel_id=1, source_target_pairs={{0,12},{4,8},{8,4},{12,0},{1,13},{5,9},{9,5},{13,1},{2,14},{6,10},... | collective-permute-start | bytes 172040 | tf_op jit(solution)/shard_map/ppermute | solution.py:477
  24.6 7.1 %collective-permute-start.11 = (bf16[16,1792]{1,0:T(8,128)(2,1)S(1)}, bf16[16,1792]{1,0:T(8,128)(2,1)S(1)}, u32[]{:S(2)}, u32[]{:S(2)}) collective-permute-start(bf16[16,1792]{1,0:T(8,128)(2,1)S(1)} %get-tuple-element.45), channel_id=1, source_target_pairs={{0,20},{4,16},{8,28},{12,24},{16,4},{20,0},{24,12},{28,8},{1,21},{... | collective-permute-start | bytes 172040 | tf_op jit(solution)/shard_map/ppermute | solution.py:489
  24.8 6.9 %collective-permute-start.12 = (bf16[16,1792]{1,0:T(8,128)(2,1)S(1)}, bf16[16,1792]{1,0:T(8,128)(2,1)S(1)}, u32[]{:S(2)}, u32[]{:S(2)}) collective-permute-start(bf16[16,1792]{1,0:T(8,128)(2,1)S(1)} %get-tuple-element.46), channel_id=1, source_target_pairs={{0,24},{4,28},{8,16},{12,20},{16,8},{20,12},{24,0},{28,4},{1,25},{... | collective-permute-start | bytes 172040 | tf_op jit(solution)/shard_map/ppermute | solution.py:489
  26.8 4.9 %collective-permute-start.13 = (bf16[16,1792]{1,0:T(8,128)(2,1)S(1)}, bf16[16,1792]{1,0:T(8,128)(2,1)S(1)}, u32[]{:S(2)}, u32[]{:S(2)}) collective-permute-start(bf16[16,1792]{1,0:T(8,128)(2,1)S(1)} %get-tuple-element.47), channel_id=1, source_target_pairs={{0,28},{4,24},{8,20},{12,16},{16,12},{20,8},{24,4},{28,0},{1,29},{... | collective-permute-start | bytes 172040 | tf_op jit(solution)/shard_map/ppermute | solution.py:489
  28.3 4.7 %collective-permute-start.10 = (bf16[16,1792]{1,0:T(8,128)(2,1)S(1)}, bf16[16,1792]{1,0:T(8,128)(2,1)S(1)}, u32[]{:S(2)}, u32[]{:S(2)}) collective-permute-start(bf16[16,1792]{1,0:T(8,128)(2,1)S(1)} %get-tuple-element.44.refs_0_), channel_id=1, source_target_pairs={{0,16},{4,20},{8,24},{12,28},{16,0},{20,4},{24,8},{28,12},{1,17},{... | collective-permute-start | bytes 172040 | tf_op jit(solution)/shard_map/ppermute | solution.py:489
  29.1 10.7 %collective-permute-start.17 = (bf16[64,1792]{1,0:T(8,128)(2,1)S(1)}, bf16[64,1792]{1,0:T(8,128)(2,1)S(1)}, u32[]{:S(2)}, u32[]{:S(2)}) collective-permute-start(bf16[64,1792]{1,0:T(8,128)(2,1)S(1)} %shard_map.120), channel_id=1, source_target_pairs={{0,1},{1,0},{2,3},{3,2},{4,5},{5,4},{6,7},{7,6},{8,9},{9,8},{10,11... | collective-permute-start | bytes 688136 | tf_op jit(solution)/shard_map/ppermute | solution.py:477
  33.0 13.5 %collective-permute-start.15 = (bf16[64,1792]{1,0:T(8,128)(2,1)S(1)}, bf16[64,1792]{1,0:T(8,128)(2,1)S(1)}, u32[]{:S(2)}, u32[]{:S(2)}) collective-permute-start(bf16[64,1792]{1,0:T(8,128)(2,1)S(1)} %shard_map.118.refs_5_.refs_4_), channel_id=1, source_target_pairs={{0,2},{1,3},{2,0},{3,1},{4,6},{5,7},{6,4},{7,5},{8,10},{9,11},{10,... | collective-permute-start | bytes 688136 | tf_op jit(solution)/shard_map/ppermute | solution.py:477
  35.6 11.5 %collective-permute-start.16 = (bf16[64,1792]{1,0:T(8,128)(2,1)S(1)}, bf16[64,1792]{1,0:T(8,128)(2,1)S(1)}, u32[]{:S(2)}, u32[]{:S(2)}) collective-permute-start(bf16[64,1792]{1,0:T(8,128)(2,1)S(1)} %get-tuple-element.48.refs_1_), channel_id=1, source_target_pairs={{0,16},{16,0},{1,17},{17,1},{2,18},{18,2},{3,19},{19,3},{4,20},{20... | collective-permute-start | bytes 688136 | tf_op jit(solution)/shard_map/ppermute | solution.py:596
  36.7 10.4 %collective-permute-start.14 = (bf16[64,1792]{1,0:T(8,128)(2,1)S(1)}, bf16[64,1792]{1,0:T(8,128)(2,1)S(1)}, u32[]{:S(2)}, u32[]{:S(2)}) collective-permute-start(bf16[64,1792]{1,0:T(8,128)(2,1)S(1)} %shard_map.118.refs_5_.refs_4_), channel_id=1, source_target_pairs={{0,1},{1,0},{2,3},{3,2},{4,5},{5,4},{6,7},{7,6},{8,9},{9,8},{10,11... | collective-permute-start | bytes 688136 | tf_op jit(solution)/shard_map/ppermute | solution.py:477
  42.3 4.9 %collective-permute-start.18 = (bf16[32,1792]{1,0:T(8,128)(2,1)S(1)}, bf16[32,1792]{1,0:T(8,128)(2,1)S(1)}, u32[]{:S(2)}, u32[]{:S(2)}) collective-permute-start(bf16[32,1792]{1,0:T(8,128)(2,1)S(1)} %get-tuple-element.50), channel_id=1, source_target_pairs={{0,4},{4,0},{8,12},{12,8},{1,5},{5,1},{9,13},{13,9},{2,6},{6,2},{1... | collective-permute-start | bytes 344072 | tf_op jit(solution)/shard_map/ppermute | solution.py:477
  46.5 11.3 %collective-permute-start.21 = (bf16[64,1792]{1,0:T(8,128)(2,1)S(1)}, bf16[64,1792]{1,0:T(8,128)(2,1)S(1)}, u32[]{:S(2)}, u32[]{:S(2)}) collective-permute-start(bf16[64,1792]{1,0:T(8,128)(2,1)S(1)} %collective-permute-done.15.refs_7_), channel_id=1, source_target_pairs={{0,1},{1,0},{2,3},{3,2},{4,5},{5,4},{6,7},{7,6},{8,9},{9,8},{10,11... | collective-permute-start | bytes 688136 | tf_op jit(solution)/shard_map/ppermute | solution.py:477
  47.2 7.6 %collective-permute-start.19 = (bf16[32,1792]{1,0:T(8,128)(2,1)S(1)}, bf16[32,1792]{1,0:T(8,128)(2,1)S(1)}, u32[]{:S(2)}, u32[]{:S(2)}) collective-permute-start(bf16[32,1792]{1,0:T(8,128)(2,1)S(1)} %shard_map.122), channel_id=1, source_target_pairs={{0,8},{4,12},{8,0},{12,4},{1,9},{5,13},{9,1},{13,5},{2,10},{6,14},... | collective-permute-start | bytes 344072 | tf_op jit(solution)/shard_map/ppermute | solution.py:477
  49.1 5.2 %collective-permute-start.5 = (bf16[16,1792]{1,0:T(8,128)(2,1)S(1)}, bf16[16,1792]{1,0:T(8,128)(2,1)S(1)}, u32[]{:S(2)}, u32[]{:S(2)}) collective-permute-start(bf16[16,1792]{1,0:T(8,128)(2,1)S(1)} %get-tuple-element.37), channel_id=1, source_target_pairs={{0,2},{1,3},{2,0},{3,1},{4,6},{5,7},{6,4},{7,5},{8,10},{9,11},{10,... | collective-permute-start | bytes 172040 | tf_op jit(solution)/shard_map/ppermute | solution.py:477
  51.0 6.9 %collective-permute-start.20 = (bf16[16,1792]{1,0:T(8,128)(2,1)S(1)}, bf16[16,1792]{1,0:T(8,128)(2,1)S(1)}, u32[]{:S(2)}, u32[]{:S(2)}) collective-permute-start(bf16[16,1792]{1,0:T(8,128)(2,1)S(1)} %get-tuple-element.53), channel_id=1, source_target_pairs={{0,3},{1,2},{2,1},{3,0},{4,7},{5,6},{6,5},{7,4},{8,11},{9,10},{10,... | collective-permute-start | bytes 172040 | tf_op jit(solution)/shard_map/ppermute | solution.py:477
